TPU v7x, 512 devices: a whole 4x4x16 slice. The times are simulated.
512 devices in a mesh: space: 32 (over z, core), mode: 16 (over y, x).
Axes of the slice: x: 4, y: 4, z: 16, core: 2. Of those that a mesh axis runs over, the one named last changes fastest.
Arguments:
- basis: float32 [3, 256, 16, 8, 2048], P(None, 'space', None, None, 'mode'), may hold values from -132 to 132
- mean_flow: float32 [3, 256, 16, 8], P(None, 'space'), may hold values from -3 to 3
- flow_gradient: float32 [3, 3, 256, 16, 8], P(None, None, 'space'), may hold values from -2 to 2
- viscosity: float32 [256, 16, 8], P('space'), may hold values from 0.02 to 0.2
Outputs:
- reduced: float32 [2048, 2048], P('mode', 'space')
- advected: float32 [3, 256, 16, 8, 2048], P(None, 'space', None, None, 'mode')
- r_factor: float32 [2048, 128], P('mode')
All inputs are finite; a program needn't handle non-finite values.
Results may differ from a plain program's by a relative error of at most 0.00074.
Values may be sent and summed in bfloat16 or wider, within the bound.
No kernel may reach another device: no remote copies, remote signals or barrier semaphores. Data moves between devices by JAX's collectives and lax.ppermute only.
A program may use at most 64 MiB of HBM per device.

v0:
```python
import jax
import jax.numpy as jnp
from jax import lax
from jax.sharding import PartitionSpec as P


def extended(cells, sides, width):
    for axis, dim in sides:
        count = lax.axis_size(axis)
        ends = count - 1
        head = lax.slice_in_dim(cells, 0, width, axis=dim)
        tail = lax.slice_in_dim(cells, cells.shape[dim] - width, cells.shape[dim], axis=dim)
        cells = jnp.concatenate(
            [
                lax.ppermute(tail, axis, [(i, (i + 1) % count) for i in range(ends)]),
                cells,
                lax.ppermute(head, axis, [((i + 1) % count, i) for i in range(ends)]),
            ],
            axis=dim,
        )
    return cells


def transport(padded, mean_flow, flow_gradient, viscosity):
    center = padded[:, 1:-1]
    widen_y = jnp.pad(center, ((0, 0), (0, 0), (1, 1), (0, 0), (0, 0)))
    widen_z = jnp.pad(center, ((0, 0), (0, 0), (0, 0), (1, 1), (0, 0)))
    east_side = padded[:, 2:]
    west_side = padded[:, :-2]
    north_side = widen_y[:, :, 2:]
    south_side = widen_y[:, :, :-2]
    upper_side = widen_z[:, :, :, 2:]
    lower_side = widen_z[:, :, :, :-2]
    laplacian = (
        east_side + west_side + north_side + south_side + upper_side + lower_side - 6.0 * center
    )
    advection = 0.5 * (
        mean_flow[0][None, :, :, :, None] * (east_side - west_side)
        + mean_flow[1][None, :, :, :, None] * (north_side - south_side)
        + mean_flow[2][None, :, :, :, None] * (upper_side - lower_side)
    )
    coupling = flow_gradient[:, 0][..., None] * center[0][None]
    coupling = coupling + flow_gradient[:, 1][..., None] * center[1][None]
    coupling = coupling + flow_gradient[:, 2][..., None] * center[2][None]
    return viscosity[None, :, :, :, None] * laplacian - advection - coupling


def apply_inverse(field, lower_factor):
    width = field.shape[4]
    flat_rows = field.reshape(-1, width)
    solved = jax.scipy.linalg.solve_triangular(lower_factor, flat_rows.T, lower=True)
    return solved.T.reshape(field.shape)


def body(basis, mean_flow, flow_gradient, viscosity):
    cells_x = basis.shape[1]
    cells_y = basis.shape[2]
    cells_z = basis.shape[3]
    panel_width = basis.shape[4]
    weight = 1.0 / (3 * cells_x * cells_y * cells_z * lax.axis_size("space"))
    flat_basis = basis.reshape(-1, panel_width)
    gram_local = (
        jnp.dot(
            flat_basis.T,
            flat_basis,
            precision=lax.Precision.HIGHEST,
            preferred_element_type=jnp.float32,
        )
        * weight
    )
    gram = lax.psum(gram_local, "space")
    lower_factor = jnp.linalg.cholesky(gram)
    ortho = apply_inverse(basis, lower_factor)
    padded_ortho = extended(ortho, (("space", 1),), 1)
    advected = transport(padded_ortho, mean_flow, flow_gradient, viscosity)
    rounded_images = advected.astype(jnp.bfloat16)
    rounded_rows = ortho.astype(jnp.bfloat16).reshape(-1, panel_width)
    panel_piece = lax.all_gather(rounded_images, "mode", axis=4, tiled=True)
    piece_rows = panel_piece.reshape(-1, panel_piece.shape[4])
    strip = (
        jnp.einsum("ra,rk->ak", rounded_rows, piece_rows, preferred_element_type=jnp.float32)
        * weight
    )
    reduced = lax.psum_scatter(strip, "space", scatter_dimension=1, tiled=True)
    return (reduced, advected, lower_factor.T)


def solution(mesh):
    placed = (
        P(None, "space", None, None, "mode"),
        P(None, "space", None, None),
        P(None, None, "space", None, None),
        P("space", None, None),
    )
    return jax.shard_map(
        body,
        mesh=mesh,
        in_specs=placed,
        out_specs=(P("mode", "space"), P(None, "space", None, None, "mode"), P("mode", None)),
        check_vma=False,
    )
```

profile of v0, /device:TPU:6, one launch (start us, length us, event | category | flops | bytes accessed | tf_op | source)
XLA Modules:
  0.0 491.2 jit_solution(15039007794072252386)
XLA Ops:
  7.2 1.3 copy-done
  8.6 3.3 fusion.8
  12.6 186.7 %all-reduce.4.cloned.1.call-done = f32[128,128]{0,1:T(8,128)} async-done(((f32[128,128]{0,1:T(8,128)}), f32[128,128]{0,1:T(8,128)}) %all-reduce.4.cloned.1.call-update) | async-done | bytes 65552 | tf_op jit(solution)/shard_map/psum | solution.py:71
  199.3 0.9 copy.27
  200.2 0.9 fusion.11
  201.1 11.7 %cholesky.16 = f32[128,128]{1,0:T(8,128)S(1)} custom-call(f32[128,128]{1,0:T(8,128)S(1)} %fusion.11), custom_call_target="Cholesky" | custom-call | tf_op jit(solution)/shard_map/jit(cholesky)/cholesky | solution.py:72
  214.2 10.4 %custom-call.7 = f32[1,128,128]{1,2,0:T(8,128)} custom-call(f32[1,128,128]{2,1,0:T(8,128)S(1)} %get-tuple-element.23), custom_call_target="InvertDiagBlocksLowerTriangular" | custom-call | tf_op jit(solution)/shard_map/jit(_solve_triangular)/triangular_solve | solution.py:51
  224.6 2.3 convolution_bitcast_fusion
  227.0 1.6 copy.28
  228.6 1.7 copy.30
  231.1 1.3 collective-permute-start
  232.4 3.7 collective-permute-start.1
  236.1 1.2 fusion.15
  237.3 1.3 copy.36
  238.6 0.9 copy.37
  239.5 1.0 copy.40
  240.5 2.1 copy.41
  242.6 2.1 copy.38
  244.6 1.1 copy.39
  245.8 4.9 %fusion.13 = (bf16[3,8,16,8,128]{4,2,3,1,0:T(8,128)(2,1)}, f32[3,8,16,8,128]{4,2,3,1,0:T(8,128)}) fusion(f32[8,16,8,128]{3,1,2,0:T(8,128)} %copy.41, f32[3,8,16,8]{2,3,1,0:T(8,128)S(1)} %get-tuple-element.17, f32[8,16,8,128]{3,1,2,0:T(8,128)S(1)} %copy.39, f32[3,8,16,8]{2,3,1,0:T(8,128)S(1)} %get-tuple-element.18, f32[8,16,8,128]{3,1,2,0:T(8,128)} %copy.37, ...), kind=kLoop, calls=%fused_computation.31 | loop fusion | flops 10616832 | bytes 5951488 | tf_op jit(solution)/shard_map/convert_element_type | solution.py:76
  250.8 110.3 %all-gather.2.cloned.1.call-done = bf16[3,8,16,8,2048]{4,2,3,1,0:T(8,128)(2,1)} async-done(((bf16[3,8,16,8,128]{4,2,3,1,0:T(8,128)(2,1)}), bf16[3,8,16,8,2048]{4,2,3,1,0:T(8,128)(2,1)}) %all-gather.2.cloned.1.call-update) | async-done | bytes 12582928 | tf_op jit(solution)/shard_map/all_gather | solution.py:78
  361.1 15.4 %fusion.5 = f32[128,2048]{0,1:T(8,128)} fusion(bf16[3,8,16,8,2048]{4,2,3,1,0:T(8,128)(2,1)} %all-gather.2.cloned.1.call-done, f32[3,8,16,8,128]{4,3,2,1,0:T(8,128)} %bitcast.45), kind=kOutput, calls=%fused_computation.6 | convolution fusion | flops 1611268096 | bytes 15204352 | tf_op jit(solution)/shard_map/ra,rk->ak/dot_general | solution.py:81
  377.3 1.7 copy.43
  379.0 105.6 %reduce-scatter.2.cloned.1.call-done = f32[128,64]{0,1:T(8,128)} async-done(((f32[128,2048]{0,1:T(8,128)}), f32[128,64]{0,1:T(8,128)}) %reduce-scatter.2.cloned.1.call-update) | async-done | bytes 32784 | tf_op jit(solution)/shard_map/reduce_scatter | solution.py:84
  (28 shorter events, 3.7 us)
Async XLA Ops:
  7.2 1.4 copy-start
  7.2 4.7 copy-start.5
  7.2 4.8 copy-start.6
  7.2 192.1 %all-reduce.4.cloned.1.call-start = ((), (), s32[]{:S(2)}) async-start(), calls=%async_computation.1 | async-start | bytes 131072 | tf_op jit(solution)/shard_map/psum | solution.py:71
  11.9 349.2 %all-gather.2.cloned.1.call-start = ((), (), s32[]{:S(2)}) async-start(), calls=%async_computation.2 | async-start | bytes 13369344 | tf_op jit(solution)/shard_map/all_gather | solution.py:78
  230.3 7.0 %copy-start.1 = (f32[3,8,16,8,128]{4,2,3,1,0:T(8,128)}, f32[3,8,16,8,128]{4,2,3,1,0:T(8,128)S(1)}, u32[]{:S(2)}) copy-start(f32[3,8,16,8,128]{4,2,3,1,0:T(8,128)S(1)} %copy.30) | copy-start | bytes 4718596
  231.1 14.7 %collective-permute-start = (f32[3,1,16,8,128]{4,2,3,1,0:T(8,128)}, f32[3,1,16,8,128]{4,2,3,1,0:T(8,128)}, u32[]{:S(2)}, u32[]{:S(2)}) collective-permute-start(f32[3,1,16,8,128]{4,2,3,1,0:T(8,128)} %get-tuple-element.11), channel_id=1, source_target_pairs={{16,0},{32,16},{48,32},{64,48},{80,64},{96,80},{112,96},{128,112},... | collective-permute-start | bytes 589832 | tf_op jit(solution)/shard_map/ppermute | solution.py:17
  232.4 13.4 %collective-permute-start.1 = (f32[3,1,16,8,128]{4,2,3,1,0:T(8,128)}, f32[3,1,16,8,128]{4,2,3,1,0:T(8,128)}, u32[]{:S(2)}, u32[]{:S(2)}) collective-permute-start(f32[3,1,16,8,128]{4,2,3,1,0:T(8,128)} %get-tuple-element.12), channel_id=1, source_target_pairs={{0,16},{16,32},{32,48},{48,64},{64,80},{80,96},{96,112},{112,128},... | collective-permute-start | bytes 589832 | tf_op jit(solution)/shard_map/ppermute | solution.py:15
  237.3 2.2 copy-start.4
  240.5 5.3 %copy-start.2 = (f32[3,8,16,8,128]{4,2,3,1,0:T(8,128)S(1)}, f32[3,8,16,8,128]{4,2,3,1,0:T(8,128)}, u32[]{:S(2)}) copy-start(f32[3,8,16,8,128]{4,2,3,1,0:T(8,128)} %copy-done.1) | copy-start | bytes 4718596
  250.8 233.9 %reduce-scatter.2.cloned.1.call-start = ((), (), s32[]{:S(2)}) async-start(), calls=%async_computation.3 | async-start | bytes 1081344 | tf_op jit(solution)/shard_map/reduce_scatter | solution.py:84
  361.1 16.2 %copy-start.3 = (f32[3,8,16,8,128]{4,2,3,1,0:T(8,128)S(1)}, f32[3,8,16,8,128]{4,2,3,1,0:T(8,128)}, u32[]{:S(2)}) copy-start(f32[3,8,16,8,128]{4,2,3,1,0:T(8,128)} %get-tuple-element.10) | copy-start | bytes 4718596
Sparse Core Ops, SparseCore 0:
  12.0 187.2 all-reduce.3
  250.9 110.1 all-gather.1
  376.7 107.9 reduce-scatter.1
where the time goes:
time: 492 us; the launch traced here: 491 us
  waiting for transfers between devices  403 us (82%)
  other arithmetic  29.3 us (6%)
  matrix products  21 us (4%)
  local copies, waits for them, and re-layouts  19.2 us (4%)
  between operations  13.9 us (3%)
  starting transfers between devices  5.11 us (1%)
    psum x1, waiting for transfers between devices, body(): gram = lax.psum(gram_local, 'space')  187 us
    all_gather x1, waiting for transfers between devices, body(): panel_piece = lax.all_gather(rounded_images, 'mode', axis=4, tiled=True)  110 us
    reduce_scatter x1, waiting for transfers between devices, body(): reduced = lax.psum_scatter(strip, 'space', scatter_dimension=1, tiled=True)  106 us
    dot_general x1, matrix products, body(): jnp.einsum('ra,rk->ak', rounded_rows, piece_rows, preferred_element_type=...  15.4 us
    another operation x3, other arithmetic, body(): lower_factor = jnp.linalg.cholesky(gram)  12.4 us
    another operation x1, other arithmetic, apply_inverse(): jax.scipy.linalg.solve_triangular(lower_factor, flat_rows.T, lower=True)  10.4 us
  transfers between devices with their start and end apart: 5, of which 3 were waited for; matrix products, arithmetic and copies ran while one was open for 3% of the time, Pallas kernels for 0%

commit v1 on v0

v1 whole, which is shorter than its diff:
```python
import functools

import jax
import jax.numpy as jnp
from jax import lax
from jax.experimental import pallas as pl
from jax.experimental.pallas import tpu as pltpu
from jax.sharding import Mesh
from jax.sharding import PartitionSpec as P

F32 = jnp.float32
BF16 = jnp.bfloat16
AXES = ("zh", "zl", "core", "y", "x")
SPACE = ("zh", "zl", "core")
MODE = ("y", "x")
VMEM_BYTES = 48 * 1024 * 1024


def kernel_call(body, outs, scratch=(), flops=0, moved=0, name=None):
    whole = pl.BlockSpec(memory_space=pltpu.VMEM)
    multiple = isinstance(outs, (tuple, list))
    return pl.pallas_call(
        body,
        out_shape=outs,
        out_specs=[whole] * len(outs) if multiple else whole,
        scratch_shapes=list(scratch),
        compiler_params=pltpu.CompilerParams(vmem_limit_bytes=VMEM_BYTES),
        cost_estimate=pl.CostEstimate(flops=flops, bytes_accessed=moved, transcendentals=0),
        name=name,
    )


def split3(a):
    high = a.astype(BF16)
    rest = a - high.astype(F32)
    mid = rest.astype(BF16)
    low = (rest - mid.astype(F32)).astype(BF16)
    return high, mid, low


def dot_rows(a, b):
    return lax.dot_general(a, b, (((0,), (0,)), ((), ())), preferred_element_type=F32)


def gram_kernel(x_ref, out_ref):
    rows = x_ref.shape[0]
    step = rows // 3
    total = jnp.zeros((256, 256), F32)
    side = jnp.zeros((128, 128), F32)
    for start in range(0, rows, step):
        high, mid, low = split3(x_ref[start : start + step, :])
        both = jnp.concatenate([high, mid], axis=1)
        total = total + dot_rows(both, both)
        side = side + dot_rows(high, low)
    gram = total[:128, :128] + total[:128, 128:] + total[128:, :128] + total[128:, 128:]
    gram = gram + side + side.T
    top, bottom = gram[:64], gram[64:]
    row = lax.broadcasted_iota(jnp.int32, (64, 128), 0)
    lane = lax.broadcasted_iota(jnp.int32, (64, 128), 1)
    packed = jnp.where((lane >= 64) & (row >= lane - 64), pltpu.roll(top, 64, 1), bottom)
    diagonal = jnp.sum(jnp.where(row == lane - 64, bottom, 0.0), axis=0, keepdims=True)
    out_ref[:64, :] = packed
    out_ref[64:, :] = jnp.broadcast_to(diagonal, (8, 128))


def stencil_kernel(x_ref, west_ref, east_ref, flow_ref, gradient_ref, viscosity_ref, out_ref):
    cells_x, cells_y = x_ref.shape[1], x_ref.shape[2]
    level = lax.broadcasted_iota(jnp.int32, (8, 128), 0)
    nu = viscosity_ref[...].T
    half = [0.5 * flow_ref[d].T for d in range(3)]
    to_east, to_west = nu - half[0], nu + half[0]
    to_north, to_south = nu - half[1], nu + half[1]
    to_upper = jnp.where(level < 7, nu - half[2], 0.0)
    to_lower = jnp.where(level > 0, nu + half[2], 0.0)
    own = [[gradient_ref[3 * i + j].T for j in range(3)] for i in range(3)]
    for i in range(3):
        own[i][i] = own[i][i] + 6.0 * nu
    for x in range(cells_x):
        for y in range(cells_y):
            place = x * cells_y + y

            def cell(values, place=place):
                return jnp.broadcast_to(values[:, place : place + 1], (8, 128))

            east_c, west_c = cell(to_east), cell(to_west)
            north_c = cell(to_north) if y + 1 < cells_y else None
            south_c = cell(to_south) if y > 0 else None
            upper_c, lower_c = cell(to_upper), cell(to_lower)
            center = [x_ref[i, x, y] for i in range(3)]
            for i in range(3):
                east = x_ref[i, x + 1, y] if x + 1 < cells_x else east_ref[i, 0, y]
                west = x_ref[i, x - 1, y] if x > 0 else west_ref[i, 0, y]
                image = east_c * east + west_c * west
                if north_c is not None:
                    image = image + north_c * x_ref[i, x, y + 1]
                if south_c is not None:
                    image = image + south_c * x_ref[i, x, y - 1]
                image = image + upper_c * pltpu.roll(center[i], 7, 0)
                image = image + lower_c * pltpu.roll(center[i], 1, 0)
                for j in range(3):
                    image = image - cell(own[i][j]) * center[j]
                out_ref[i, x, y] = image


def factor_kernel(weight, parts_ref, r_ref, inverse_ref):
    packed = parts_ref[0] + parts_ref[1] + (parts_ref[2] + parts_ref[3])
    packed = packed * weight
    top = packed[:64]
    diagonal = packed[64:65]
    turned = pltpu.roll(top, 64, 1)
    across = jnp.concatenate([top, turned], axis=0).T
    row = lax.broadcasted_iota(jnp.int32, (64, 128), 0)
    lane = lax.broadcasted_iota(jnp.int32, (64, 128), 1)
    upper_half = jnp.where((lane < 64) & (row >= lane), turned, across[64:])
    lower_half = jnp.where(
        (lane < 64) | (row < lane - 64), top, jnp.where(row > lane - 64, across[:64], diagonal)
    )
    a = [upper_half[8 * b : 8 * b + 8] for b in range(8)]
    a += [lower_half[8 * b : 8 * b + 8] for b in range(8)]
    sub = lax.broadcasted_iota(jnp.int32, (8, 128), 0)
    col = lax.broadcasted_iota(jnp.int32, (8, 128), 1)
    w = [jnp.where(sub + 8 * b == col, 1.0, 0.0).astype(F32) for b in range(16)]

    def spread_row(values, t):
        return jnp.broadcast_to(values[t : t + 1, :], (8, 128))

    def combine(columns, values):
        terms = [c * spread_row(values, t) for t, c in enumerate(columns)]
        while len(terms) > 1:
            terms = [p + q for p, q in zip(terms[::2], terms[1::2])]
        return terms[0]

    inverse_rows = []
    for k in range(16):
        r, v = a[k], w[k]
        e = {}
        for j in range(8):
            column = jnp.broadcast_to(r[:, 8 * k + j : 8 * k + j + 1], (8, 128))
            for i in range(j + 1):
                e[i, j] = spread_row(column, i)
        inv = {}
        u = {}
        for t in range(8):
            scale = lax.rsqrt(e[t, t])
            inv[t, t] = scale
            for j in range(t + 1, 8):
                u[t, j] = e[t, j] * scale
            for i in range(t + 1, 8):
                for j in range(i, 8):
                    e[i, j] = e[i, j] - u[t, i] * u[t, j]
        for t in range(8):
            for i in range(t + 1, 8):
                total = u[t, i] * inv[t, t]
                for m in range(t + 1, i):
                    total = total + u[m, i] * inv[m, t]
                inv[i, t] = -inv[i, i] * total
        columns, turned_columns = [], []
        for j in range(8):
            column = jnp.zeros((8, 128), F32)
            for i in range(j, 8):
                column = jnp.where(sub == i, inv[i, j], column)
            columns.append(column)
            column = jnp.zeros((8, 128), F32)
            for i in range(j + 1):
                column = jnp.where(sub == i, inv[j, i], column)
            turned_columns.append(column)
        upper = combine(columns, r)
        lower_inverse = combine(columns, v)
        r_ref[8 * k : 8 * k + 8, :] = jnp.where(col >= sub + 8 * k, upper, 0.0)
        inverse_rows.append(lower_inverse)
        if k < 15:
            z = combine(turned_columns, upper)
            zv = combine(turned_columns, lower_inverse)
            z_rows = [spread_row(z, t) for t in range(8)]
            zv_rows = [spread_row(zv, t) for t in range(8)]
            for b in range(k + 1, 16):
                cs = [
                    jnp.broadcast_to(a[b][:, 8 * k + j : 8 * k + j + 1], (8, 128)) for j in range(8)
                ]
                s = [c * z_rows[j] for j, c in enumerate(cs)]
                sv = [c * zv_rows[j] for j, c in enumerate(cs)]
                a[b] = a[b] - (((s[0] + s[1]) + (s[2] + s[3])) + ((s[4] + s[5]) + (s[6] + s[7])))
                w[b] = w[b] - (
                    ((sv[0] + sv[1]) + (sv[2] + sv[3])) + ((sv[4] + sv[5]) + (sv[6] + sv[7]))
                )
    r_inverse = jnp.concatenate(inverse_rows, axis=0).T
    high, mid, low = split3(r_inverse)
    inverse_ref[:, :128] = high
    inverse_ref[:, 128:256] = mid
    inverse_ref[:, 256:] = low


def apply_kernel(x_ref, image_ref, inverse_ref, rounded_ref, advected_ref, rounded_image_ref):
    rows = x_ref.shape[0]
    step = 512
    high, mid, low = (inverse_ref[:, 128 * t : 128 * t + 128] for t in range(3))
    pair = jnp.concatenate([high, mid], axis=1)
    main = jnp.concatenate([pair, pair], axis=0)
    side = jnp.concatenate([low, high], axis=0)

    def times(values):
        h, m, l = split3(values)
        first = jnp.dot(jnp.concatenate([h, m], axis=1), main, preferred_element_type=F32)
        second = jnp.dot(jnp.concatenate([h, l], axis=1), side, preferred_element_type=F32)
        return first[:, :128] + (first[:, 128:] + second)

    def chunk(n, carry):
        at = pl.ds(pl.multiple_of(n * step, step), step)
        rounded_ref[at, :] = times(x_ref[at, :]).astype(BF16)
        advected = times(image_ref[at, :])
        advected_ref[at, :] = advected
        rounded_image_ref[at, :] = advected.astype(BF16)
        return carry

    lax.fori_loop(0, rows // step, chunk, 0)


def product_kernel(place_ref, *refs):
    mode_refs, image_refs = refs[:5], refs[5:10]
    keep_ref, send_ref, total_ref = refs[10:]
    rows = mode_refs[0].shape[0]
    half = rows // 2
    for part in range(2):
        at = slice(part * half, part * half + half)
        wide = [
            jnp.concatenate([r[0][at, :], r[1][at, :], r[2][at, :], r[3 + part][...]], axis=1)
            for r in (mode_refs, image_refs)
        ]
        product = dot_rows(wide[1], wide[0])
        if part == 0:
            total_ref[...] = product
        else:
            total_ref[...] += product
    core, y, x = place_ref[0], place_ref[1], place_ref[2]
    for b, back_y in enumerate((0, 1, 3, 2)):
        panel_y = lax.rem(y + 4 - back_y, 4)
        for a, back_x in enumerate((0, 1, 3, 2)):
            piece = panel_y * 4 + lax.rem(x + 4 - back_x, 4)
            lanes = slice(128 * a, 128 * a + 128)
            mine = pl.ds(pl.multiple_of(128 * b + 64 * core, 64), 64)
            other = pl.ds(pl.multiple_of(128 * b + 64 * (1 - core), 64), 64)
            keep_ref[piece] = total_ref[mine, lanes]
            send_ref[piece] = total_ref[other, lanes]


def ring(shift):
    return [(i, (i + shift) % 4) for i in range(4)]


SWAP = [(0, 1), (1, 0)]


def spread(block, axis):
    half = block.shape[0] // 2
    up = lax.ppermute(block, axis, ring(1))
    down = lax.ppermute(block, axis, ring(3))
    far_up = lax.ppermute(up[:half], axis, ring(1))
    far_down = lax.ppermute(down[half:], axis, ring(3))
    return block, up, down, far_up, far_down


def copies(block, count):
    return jnp.broadcast_to(block[None], (count,) + block.shape)


def last_move():
    pairs = []
    for zh in range(4):
        for zl in range(4):
            for core in range(2):
                for y in range(4):
                    for x in range(4):
                        source = (((zh * 4 + zl) * 2 + core) * 4 + y) * 4 + x
                        target = (((zh * 4 + x) * 2 + core) * 4 + y) * 4 + zl
                        pairs.append((source, target))
    return pairs


def body(basis, mean_flow, flow_gradient, viscosity):
    _, cells_x, cells_y, cells_z, width = basis.shape
    rows = 3 * cells_x * cells_y * cells_z
    blocks = 32
    weight = 1.0 / (rows * blocks)
    flat = basis.reshape(rows, width)
    west = lax.ppermute(basis[:, -1:], SPACE, [(i, i + 1) for i in range(blocks - 1)])
    east = lax.ppermute(basis[:, :1], SPACE, [(i + 1, i) for i in range(blocks - 1)])

    gram = kernel_call(
        gram_kernel, jax.ShapeDtypeStruct((72, 128), F32), flops=600_000_000, moved=1_600_000
    )(flat)
    image = kernel_call(
        stencil_kernel, jax.ShapeDtypeStruct(basis.shape, F32), flops=30_000_000, moved=3_500_000
    )(
        basis,
        west,
        east,
        mean_flow.reshape(3, cells_x * cells_y, cells_z),
        flow_gradient.reshape(9, cells_x * cells_y, cells_z),
        viscosity.reshape(cells_x * cells_y, cells_z),
    ).reshape(rows, width)

    gram = gram + lax.ppermute(gram, "core", SWAP)
    gram = jnp.sum(lax.all_to_all(copies(gram, 4), "zl", 0, 0, tiled=True), axis=0)
    parts = lax.all_to_all(copies(gram, 4), "zh", 0, 0, tiled=True)
    r_factor, inverse = kernel_call(
        functools.partial(factor_kernel, weight),
        (jax.ShapeDtypeStruct((128, 128), F32), jax.ShapeDtypeStruct((128, 384), BF16)),
        flops=10_000_000,
        moved=400_000,
    )(parts)

    rounded, advected, rounded_image = kernel_call(
        apply_kernel,
        (
            jax.ShapeDtypeStruct((rows, width), BF16),
            jax.ShapeDtypeStruct((rows, width), F32),
            jax.ShapeDtypeStruct((rows, width), BF16),
        ),
        flops=1_200_000_000,
        moved=6_000_000,
    )(flat, image, inverse)

    place = jnp.stack([lax.axis_index("core"), lax.axis_index("y"), lax.axis_index("x")])
    pieces = jax.ShapeDtypeStruct((16, 64, 128), F32)
    whole = pl.BlockSpec(memory_space=pltpu.VMEM)
    keep, send = pl.pallas_call(
        product_kernel,
        out_shape=(pieces, pieces),
        in_specs=[pl.BlockSpec(memory_space=pltpu.SMEM)] + [whole] * 10,
        out_specs=[whole, whole],
        scratch_shapes=[pltpu.VMEM((512, 512), F32)],
        compiler_params=pltpu.CompilerParams(vmem_limit_bytes=VMEM_BYTES),
        cost_estimate=pl.CostEstimate(
            flops=1_600_000_000, bytes_accessed=8_000_000, transcendentals=0
        ),
    )(place, *spread(rounded, "x"), *spread(rounded_image, "y"))

    partial = keep + lax.ppermute(send, "core", SWAP)
    summands = lax.all_to_all(partial, ("zh", "zl"), 0, 0, tiled=True)
    piece = jnp.sum(summands, axis=0) * weight
    reduced = lax.ppermute(piece, AXES, last_move()).T
    return reduced, advected.reshape(basis.shape), r_factor


def solution(mesh):
    fine = Mesh(mesh.devices.reshape(4, 4, 2, 4, 4), AXES)
    placed = (
        P(None, SPACE, None, None, MODE),
        P(None, SPACE, None, None),
        P(None, None, SPACE, None, None),
        P(SPACE, None, None),
    )
    return jax.shard_map(
        body,
        mesh=fine,
        in_specs=placed,
        out_specs=(P(MODE, SPACE), P(None, SPACE, None, None, MODE), P(MODE, None)),
        check_vma=False,
    )
```

time: 492 us -> 164 us (0.33)
  waiting for transfers between devices: 403 us -> 30.6 us
  blocking collectives: 0 us -> 53.1 us
  starting transfers between devices: 5.11 us -> 52.6 us
  other arithmetic: 29.3 us -> 0.21 us
  matrix products: 21 us -> 0 us
  Pallas kernels: 0 us -> 16.4 us
  between operations: 13.9 us -> 0.92 us
  local copies, waits for them, and re-layouts: 19.2 us -> 9.83 us
    psum x1 -> x0, waiting for transfers between devices: 187 us -> none  [body(): gram = lax.psum(gram_local, 'space')]
    all_gather x1 -> x0, waiting for transfers between devices: 110 us -> none  [body(): panel_piece = lax.all_gather(rounded_images, 'mode', axis=4, tiled=True)]
    reduce_scatter x1 -> x0, waiting for transfers between devices: 106 us -> none  [body(): reduced = lax.psum_scatter(strip, 'space', scatter_dimension=1, tiled=True)]
    all_to_all x0 -> x2, blocking collectives: none -> 53.1 us  [the longest x1 40.6 us: body(): summands = lax.all_to_all(partial, ('zh', 'zl'), 0, 0, tiled=True)]
    ppermute x2 -> x13, starting transfers between devices: 4.99 us -> 40.3 us  [the longest x2 7.65 us: spread(): down = lax.ppermute(block, axis, ring(3))]
    ppermute x2 -> x13, waiting for transfers between devices: 0.01 us -> 24.9 us  [the longest x2 6.68 us: spread(): far_up = lax.ppermute(up[:half], axis, ring(1))]
    another operation x4 -> x1, other arithmetic: 22.8 us -> 0.08 us  [body(): jnp.stack([lax.axis_index('core'), lax.axis_index('y'), lax.axis_index('x...]
    dot_general x2 -> x0, matrix products: 18.7 us -> none  [the longest x1 15.4 us: body(): jnp.einsum('ra,rk->ak', rounded_rows, piece_rows, preferred_element_type=...]
  transfers between devices with their start and end apart: 5 -> 14, of which waited for: 3 -> 8; matrix products, arithmetic and copies ran while one was open for 3% -> 3% of each run, Pallas kernels for 0% -> 2%
where the time goes in v1:
time: 164 us
  blocking collectives  53.1 us (32%)
  starting transfers between devices  52.6 us (32%)
  waiting for transfers between devices  30.6 us (19%)
  Pallas kernels  16.4 us (10%)
  local copies, waits for them, and re-layouts  9.83 us (6%)
    all_to_all x1, blocking collectives, body(): summands = lax.all_to_all(partial, ('zh', 'zl'), 0, 0, tiled=True)  40.6 us
    all_to_all x1, blocking collectives, body(): lax.all_to_all(copies(gram, 4), 'zl', 0, 0, tiled=True)  12.5 us
    all_to_all x1, starting transfers between devices, body(): parts = lax.all_to_all(copies(gram, 4), 'zh', 0, 0, tiled=True)  12.4 us
    ppermute x2, starting transfers between devices, spread(): down = lax.ppermute(block, axis, ring(3))  7.65 us
    ppermute x2, starting transfers between devices, spread(): far_up = lax.ppermute(up[:half], axis, ring(1))  7.03 us
    ppermute x2, starting transfers between devices, spread(): far_down = lax.ppermute(down[half:], axis, ring(3))  6.82 us
    ppermute x2, waiting for transfers between devices, spread(): far_up = lax.ppermute(up[:half], axis, ring(1))  6.68 us
    ppermute x2, waiting for transfers between devices, spread(): down = lax.ppermute(block, axis, ring(3))  6.57 us
  transfers between devices with their start and end apart: 14, of which 8 were waited for; matrix products, arithmetic and copies ran while one was open for 3% of the time, Pallas kernels for 2%

profile of v1, /device:TPU:6, one launch (start us, length us, event | category | flops | bytes accessed | tf_op | source)
XLA Modules:
  0.0 163.6 jit_solution(285974756474854428)
XLA Ops:
  3.0 2.1 %collective-permute-start.2 = (f32[72,128]{1,0:T(8,128)S(1)}, f32[72,128]{1,0:T(8,128)S(1)}, u32[]{:S(2)}, u32[]{:S(2)}) collective-permute-start(f32[72,128]{1,0:T(8,128)S(1)} %shard_map.68), channel_id=1, source_target_pairs={{0,16},{16,0},{1,17},{17,1},{2,18},{18,2},{3,19},{19,3},{4,20},{20... | collective-permute-start | bytes 110600 | tf_op jit(solution)/shard_map/ppermute | solution.py:302
  6.3 12.5 %all_to_all.15 = f32[4,72,128]{2,1,0:T(8,128)S(1)} all-to-all(f32[4,72,128]{2,1,0:T(8,128)S(1)} %broadcast_in_dim.4), channel_id=1, replica_groups=mesh['zh'=4,'zl'=4,'core'=2,'y'=4,'x'=4] {'zl'}, dimensions={0} | all-to-all | bytes 294912 | tf_op jit(solution)/shard_map/all_to_all | solution.py:303
  19.5 12.4 %all-to-all-start.1 = ((f32[4,72,128]{2,1,0:T(8,128)}), f32[4,72,128]{2,1,0:T(8,128)S(1)}, u32[]{:S(2)}, u32[]{:S(2)}) async-start(f32[4,72,128]{2,1,0:T(8,128)} %broadcast_in_dim.5), calls=%async_computation.1 | async-start | bytes 294912 | tf_op jit(solution)/shard_map/all_to_all | solution.py:304
  33.8 3.0 %collective-permute-start = (f32[3,1,16,8,128]{4,3,2,1,0:T(8,128)S(1)}, f32[3,1,16,8,128]{4,3,2,1,0:T(8,128)S(1)}, u32[]{:S(2)}, u32[]{:S(2)}) collective-permute-start(f32[3,1,16,8,128]{4,3,2,1,0:T(8,128)S(1)} %get-tuple-element.18), channel_id=1, source_target_pairs={{0,16},{16,32},{32,48},{48,64},{64,80},{80,96},{96,112},{112,128},... | collective-permute-start | bytes 589832 | tf_op jit(solution)/shard_map/ppermute | solution.py:285
  37.9 2.5 %shard_map.67 = f32[3,8,16,8,128]{4,3,2,1,0:T(8,128)S(1)} custom-call(f32[3,8,16,8,128]{4,3,2,1,0:T(8,128)S(1)} %copy-done.1, f32[3,1,16,8,128]{4,3,2,1,0:T(8,128)S(1)} %collective-permute-done.west_ref, f32[3,1,16,8,128]{4,3,2,1,0:T(8,128)S(1)} %collective-permute-done.1.east_ref, f32[3,128,8]{2,1,0:T(8,128)S(1)} %bitcast.14, f32[9,128,8]{2,1,0:T(8,128)S(1)} %bitcast.12, ...), custom_call_target="tpu_custom_call" | custom-call | flops 30000000 | bytes 3500000 | tf_op jit(solution)/shard_map/pallas_call | solution.py:291
  41.6 5.7 %all-to-all-done.1.parts_ref = f32[4,72,128]{2,1,0:T(8,128)S(1)} async-done(((f32[4,72,128]{2,1,0:T(8,128)}), f32[4,72,128]{2,1,0:T(8,128)S(1)}, u32[]{:S(2)}, u32[]{:S(2)}) %all-to-all-start.1) | async-done | bytes 147488 | tf_op jit(solution)/shard_map/all_to_all | solution.py:304
  47.3 5.5 %shard_map.69 = (f32[128,128]{1,0:T(8,128)}, bf16[128,384]{1,0:T(8,128)(2,1)S(1)}) custom-call(f32[4,72,128]{2,1,0:T(8,128)S(1)} %all-to-all-done.1.parts_ref), custom_call_target="tpu_custom_call" | custom-call | flops 10000000 | bytes 400000 | tf_op jit(solution)/shard_map/pallas_call | solution.py:305
  54.2 3.8 %shard_map.70 = (bf16[3072,128]{1,0:T(8,128)(2,1)S(1)}, f32[3072,128]{1,0:T(8,128)}, bf16[3072,128]{1,0:T(8,128)(2,1)S(1)}) custom-call(f32[3072,128]{1,0:T(8,128)S(1)} %bitcast.11, f32[3072,128]{1,0:T(8,128)S(1)} %bitcast.13, bf16[128,384]{1,0:T(8,128)(2,1)S(1)} %get-tuple-element.10.inverse_ref), custom_call_target="tpu_custom_call" | custom-call | flops 1200000000 | bytes 6000000 | tf_op jit(solution)/shard_map/pallas_call | solution.py:312
  58.1 2.7 %collective-permute-start.4 = (bf16[3072,128]{1,0:T(8,128)(2,1)S(1)}, bf16[3072,128]{1,0:T(8,128)(2,1)S(1)}, u32[]{:S(2)}, u32[]{:S(2)}) collective-permute-start(bf16[3072,128]{1,0:T(8,128)(2,1)S(1)} %get-tuple-element.11.refs_0_), channel_id=1, source_target_pairs={{0,3},{1,0},{2,1},{3,2},{4,7},{5,4},{6,5},{7,6},{8,11},{9,8},{10,9... | collective-permute-start | bytes 2359304 | tf_op jit(solution)/shard_map/ppermute | solution.py:256
  60.8 4.3 %collective-permute-start.3 = (bf16[3072,128]{1,0:T(8,128)(2,1)S(1)}, bf16[3072,128]{1,0:T(8,128)(2,1)S(1)}, u32[]{:S(2)}, u32[]{:S(2)}) collective-permute-start(bf16[3072,128]{1,0:T(8,128)(2,1)S(1)} %get-tuple-element.11.refs_0_), channel_id=1, source_target_pairs={{0,1},{1,2},{2,3},{3,0},{4,5},{5,6},{6,7},{7,4},{8,9},{9,10},{10,1... | collective-permute-start | bytes 2359304 | tf_op jit(solution)/shard_map/ppermute | solution.py:255
  65.1 4.9 %collective-permute-start.8 = (bf16[3072,128]{1,0:T(8,128)(2,1)S(1)}, bf16[3072,128]{1,0:T(8,128)(2,1)S(1)}, u32[]{:S(2)}, u32[]{:S(2)}) collective-permute-start(bf16[3072,128]{1,0:T(8,128)(2,1)S(1)} %get-tuple-element.12.refs_5_), channel_id=1, source_target_pairs={{0,12},{4,0},{8,4},{12,8},{1,13},{5,1},{9,5},{13,9},{2,14},{6,2},{... | collective-permute-start | bytes 2359304 | tf_op jit(solution)/shard_map/ppermute | solution.py:256
  70.1 1.9 %collective-permute-start.7 = (bf16[3072,128]{1,0:T(8,128)(2,1)S(1)}, bf16[3072,128]{1,0:T(8,128)(2,1)S(1)}, u32[]{:S(2)}, u32[]{:S(2)}) collective-permute-start(bf16[3072,128]{1,0:T(8,128)(2,1)S(1)} %get-tuple-element.12.refs_5_), channel_id=1, source_target_pairs={{0,4},{4,8},{8,12},{12,0},{1,5},{5,9},{9,13},{13,1},{2,6},{6,10},{... | collective-permute-start | bytes 2359304 | tf_op jit(solution)/shard_map/ppermute | solution.py:255
  72.0 6.6 %collective-permute-done.4.refs_2_ = bf16[3072,128]{1,0:T(8,128)(2,1)S(1)} collective-permute-done((bf16[3072,128]{1,0:T(8,128)(2,1)S(1)}, bf16[3072,128]{1,0:T(8,128)(2,1)S(1)}, u32[]{:S(2)}, u32[]{:S(2)}) %collective-permute-start.4) | collective-permute-done | bytes 786464 | tf_op jit(solution)/shard_map/ppermute | solution.py:256
  79.3 1.9 %collective-permute-start.6 = (bf16[1536,128]{1,0:T(8,128)(2,1)}, bf16[1536,128]{1,0:T(8,128)(2,1)S(1)}, u32[]{:S(2)}, u32[]{:S(2)}) collective-permute-start(bf16[1536,128]{1,0:T(8,128)(2,1)} %slice.25), channel_id=1, source_target_pairs={{0,3},{1,0},{2,1},{3,2},{4,7},{5,4},{6,5},{7,6},{8,11},{9,8},{10,9... | collective-permute-start | bytes 1179656 | tf_op jit(solution)/shard_map/ppermute | solution.py:258
  82.0 5.1 %collective-permute-start.5 = (bf16[1536,128]{1,0:T(8,128)(2,1)}, bf16[1536,128]{1,0:T(8,128)(2,1)}, u32[]{:S(2)}, u32[]{:S(2)}) collective-permute-start(bf16[1536,128]{1,0:T(8,128)(2,1)} %slice.24), channel_id=1, source_target_pairs={{0,1},{1,2},{2,3},{3,0},{4,5},{5,6},{6,7},{7,4},{8,9},{9,10},{10,1... | collective-permute-start | bytes 1179656 | tf_op jit(solution)/shard_map/ppermute | solution.py:257
  88.0 4.9 %collective-permute-start.10 = (bf16[1536,128]{1,0:T(8,128)(2,1)}, bf16[1536,128]{1,0:T(8,128)(2,1)}, u32[]{:S(2)}, u32[]{:S(2)}) collective-permute-start(bf16[1536,128]{1,0:T(8,128)(2,1)} %slice.27), channel_id=1, source_target_pairs={{0,12},{4,0},{8,4},{12,8},{1,13},{5,1},{9,5},{13,9},{2,14},{6,2},{... | collective-permute-start | bytes 1179656 | tf_op jit(solution)/shard_map/ppermute | solution.py:258
  94.0 1.9 %collective-permute-start.9 = (bf16[1536,128]{1,0:T(8,128)(2,1)}, bf16[1536,128]{1,0:T(8,128)(2,1)}, u32[]{:S(2)}, u32[]{:S(2)}) collective-permute-start(bf16[1536,128]{1,0:T(8,128)(2,1)} %slice.26), channel_id=1, source_target_pairs={{0,4},{4,8},{8,12},{12,0},{1,5},{5,9},{9,13},{13,1},{2,6},{6,10},{... | collective-permute-start | bytes 1179656 | tf_op jit(solution)/shard_map/ppermute | solution.py:257
  96.0 2.5 %collective-permute-done.10.refs_9_ = bf16[1536,128]{1,0:T(8,128)(2,1)} collective-permute-done((bf16[1536,128]{1,0:T(8,128)(2,1)}, bf16[1536,128]{1,0:T(8,128)(2,1)}, u32[]{:S(2)}, u32[]{:S(2)}) %collective-permute-start.10) | collective-permute-done | bytes 393248 | tf_op jit(solution)/shard_map/ppermute | solution.py:258
  98.5 6.7 %collective-permute-done.9.refs_8_ = bf16[1536,128]{1,0:T(8,128)(2,1)} collective-permute-done((bf16[1536,128]{1,0:T(8,128)(2,1)}, bf16[1536,128]{1,0:T(8,128)(2,1)}, u32[]{:S(2)}, u32[]{:S(2)}) %collective-permute-start.9) | collective-permute-done | bytes 393248 | tf_op jit(solution)/shard_map/ppermute | solution.py:257
  105.2 3.6 %shard_map.71 = (f32[16,64,128]{2,1,0:T(8,128)S(1)}, f32[16,64,128]{2,1,0:T(8,128)S(1)}) custom-call(s32[3]{0:T(128)S(1)} %pad_add_fusion.place_ref, bf16[3072,128]{1,0:T(8,128)(2,1)S(1)} %get-tuple-element.11.refs_0_, bf16[3072,128]{1,0:T(8,128)(2,1)S(1)} %collective-permute-done.3.refs_1_, bf16[3072,128]{1,0:T(8,128)(2,1)S(1)} %collective-permute-done.4.refs_2_, ...), custom_call_target="tpu_custom_call" | custom-call | flops 1600000000 | bytes 8000000 | tf_op jit(solution)/shard_map/pallas_call | solution.py:326
  108.8 1.9 %collective-permute-start.11 = (f32[16,64,128]{2,1,0:T(8,128)S(1)}, f32[16,64,128]{2,1,0:T(8,128)S(1)}, u32[]{:S(2)}, u32[]{:S(2)}) collective-permute-start(f32[16,64,128]{2,1,0:T(8,128)S(1)} %get-tuple-element.14), channel_id=1, source_target_pairs={{0,16},{16,0},{1,17},{17,1},{2,18},{18,2},{3,19},{19,3},{4,20},{20... | collective-permute-start | bytes 1572872 | tf_op jit(solution)/shard_map/ppermute | solution.py:338
  112.7 40.6 %all_to_all.16 = f32[16,64,128]{2,1,0:T(8,128)S(1)} all-to-all(f32[16,64,128]{2,1,0:T(8,128)S(1)} %add.7), channel_id=1, replica_groups=mesh['zh'=4,'zl'=4,'core'=2,'y'=4,'x'=4] {'zh','zl'}, dimensions={0} | all-to-all | bytes 1048576 | tf_op jit(solution)/shard_map/all_to_all | solution.py:339
  153.3 4.2 %collective-permute-start.12 = (f32[64,128]{1,0:T(8,128)S(1)}, f32[64,128]{1,0:T(8,128)S(1)}, u32[]{:S(2)}, u32[]{:S(2)}) collective-permute-start(f32[64,128]{1,0:T(8,128)S(1)} %broadcast_multiply_fusion), channel_id=1, source_target_pairs={{0,0},{1,32},{2,64},{3,96},{4,4},{5,36},{6,68},{7,100},{8,8},{9,40... | collective-permute-start | bytes 98312 | tf_op jit(solution)/shard_map/ppermute | solution.py:341
  157.5 5.5 %collective-permute-done.12 = f32[64,128]{1,0:T(8,128)S(1)} collective-permute-done((f32[64,128]{1,0:T(8,128)S(1)}, f32[64,128]{1,0:T(8,128)S(1)}, u32[]{:S(2)}, u32[]{:S(2)}) %collective-permute-start.12) | collective-permute-done | bytes 32800 | tf_op jit(solution)/shard_map/ppermute | solution.py:341
  (46 shorter events, 15.9 us)
Async XLA Ops:
  0.6 1.4 copy-start
  2.0 29.8 %copy-start.1 = (f32[3,8,16,8,128]{4,3,2,1,0:T(8,128)S(1)}, f32[3,8,16,8,128]{4,3,2,1,0:T(8,128)}, u32[]{:S(2)}) copy-start(f32[3,8,16,8,128]{4,3,2,1,0:T(8,128)} %x_ref.1) | copy-start | bytes 4718596
  3.0 33.9 %copy-start.8 = (f32[8,16,8]{1,2,0:T(8,128)S(1)}, f32[8,16,8]{1,2,0:T(8,128)}, u32[]{:S(2)}) copy-start(f32[8,16,8]{1,2,0:T(8,128)} %param.7) | copy-start | bytes 12292
  3.0 34.0 %copy-start.7 = (f32[3,8,16,8]{2,3,1,0:T(8,128)S(1)}, f32[3,8,16,8]{2,3,1,0:T(8,128)}, u32[]{:S(2)}) copy-start(f32[3,8,16,8]{2,3,1,0:T(8,128)} %param.5) | copy-start | bytes 36868
  3.0 34.1 %copy-start.6 = (f32[3,3,8,16,8]{3,4,2,1,0:T(8,128)S(1)}, f32[3,3,8,16,8]{3,4,2,1,0:T(8,128)}, u32[]{:S(2)}) copy-start(f32[3,3,8,16,8]{3,4,2,1,0:T(8,128)} %param.6) | copy-start | bytes 110596
  3.0 3.2 %collective-permute-start.2 = (f32[72,128]{1,0:T(8,128)S(1)}, f32[72,128]{1,0:T(8,128)S(1)}, u32[]{:S(2)}, u32[]{:S(2)}) collective-permute-start(f32[72,128]{1,0:T(8,128)S(1)} %shard_map.68), channel_id=1, source_target_pairs={{0,16},{16,0},{1,17},{17,1},{2,18},{18,2},{3,19},{19,3},{4,20},{20... | collective-permute-start | bytes 110600 | tf_op jit(solution)/shard_map/ppermute | solution.py:302
  19.5 27.9 %all-to-all-start.1 = ((f32[4,72,128]{2,1,0:T(8,128)}), f32[4,72,128]{2,1,0:T(8,128)S(1)}, u32[]{:S(2)}, u32[]{:S(2)}) async-start(f32[4,72,128]{2,1,0:T(8,128)} %broadcast_in_dim.5), calls=%async_computation.1 | async-start | bytes 294912 | tf_op jit(solution)/shard_map/all_to_all | solution.py:304
  32.5 4.8 %collective-permute-start.1 = (f32[3,1,16,8,128]{4,3,2,1,0:T(8,128)}, f32[3,1,16,8,128]{4,3,2,1,0:T(8,128)S(1)}, u32[]{:S(2)}, u32[]{:S(2)}) collective-permute-start(f32[3,1,16,8,128]{4,3,2,1,0:T(8,128)} %get-tuple-element.17), channel_id=1, source_target_pairs={{16,0},{32,16},{48,32},{64,48},{80,64},{96,80},{112,96},{128,112},... | collective-permute-start | bytes 589832 | tf_op jit(solution)/shard_map/ppermute | solution.py:286
  33.8 4.1 %collective-permute-start = (f32[3,1,16,8,128]{4,3,2,1,0:T(8,128)S(1)}, f32[3,1,16,8,128]{4,3,2,1,0:T(8,128)S(1)}, u32[]{:S(2)}, u32[]{:S(2)}) collective-permute-start(f32[3,1,16,8,128]{4,3,2,1,0:T(8,128)S(1)} %get-tuple-element.18), channel_id=1, source_target_pairs={{0,16},{16,32},{32,48},{48,64},{64,80},{80,96},{96,112},{112,128},... | collective-permute-start | bytes 589832 | tf_op jit(solution)/shard_map/ppermute | solution.py:285
  40.5 1.1 copy-start.2
  52.8 1.4 copy-start.3
  58.1 20.5 %collective-permute-start.4 = (bf16[3072,128]{1,0:T(8,128)(2,1)S(1)}, bf16[3072,128]{1,0:T(8,128)(2,1)S(1)}, u32[]{:S(2)}, u32[]{:S(2)}) collective-permute-start(bf16[3072,128]{1,0:T(8,128)(2,1)S(1)} %get-tuple-element.11.refs_0_), channel_id=1, source_target_pairs={{0,3},{1,0},{2,1},{3,2},{4,7},{5,4},{6,5},{7,6},{8,11},{9,8},{10,9... | collective-permute-start | bytes 2359304 | tf_op jit(solution)/shard_map/ppermute | solution.py:256
  60.8 20.4 %collective-permute-start.3 = (bf16[3072,128]{1,0:T(8,128)(2,1)S(1)}, bf16[3072,128]{1,0:T(8,128)(2,1)S(1)}, u32[]{:S(2)}, u32[]{:S(2)}) collective-permute-start(bf16[3072,128]{1,0:T(8,128)(2,1)S(1)} %get-tuple-element.11.refs_0_), channel_id=1, source_target_pairs={{0,1},{1,2},{2,3},{3,0},{4,5},{5,6},{6,7},{7,4},{8,9},{9,10},{10,1... | collective-permute-start | bytes 2359304 | tf_op jit(solution)/shard_map/ppermute | solution.py:255
  65.1 22.0 %collective-permute-start.8 = (bf16[3072,128]{1,0:T(8,128)(2,1)S(1)}, bf16[3072,128]{1,0:T(8,128)(2,1)S(1)}, u32[]{:S(2)}, u32[]{:S(2)}) collective-permute-start(bf16[3072,128]{1,0:T(8,128)(2,1)S(1)} %get-tuple-element.12.refs_5_), channel_id=1, source_target_pairs={{0,12},{4,0},{8,4},{12,8},{1,13},{5,1},{9,5},{13,9},{2,14},{6,2},{... | collective-permute-start | bytes 2359304 | tf_op jit(solution)/shard_map/ppermute | solution.py:256
  70.1 22.9 %collective-permute-start.7 = (bf16[3072,128]{1,0:T(8,128)(2,1)S(1)}, bf16[3072,128]{1,0:T(8,128)(2,1)S(1)}, u32[]{:S(2)}, u32[]{:S(2)}) collective-permute-start(bf16[3072,128]{1,0:T(8,128)(2,1)S(1)} %get-tuple-element.12.refs_5_), channel_id=1, source_target_pairs={{0,4},{4,8},{8,12},{12,0},{1,5},{5,9},{9,13},{13,1},{2,6},{6,10},{... | collective-permute-start | bytes 2359304 | tf_op jit(solution)/shard_map/ppermute | solution.py:255
  79.3 16.7 %collective-permute-start.6 = (bf16[1536,128]{1,0:T(8,128)(2,1)}, bf16[1536,128]{1,0:T(8,128)(2,1)S(1)}, u32[]{:S(2)}, u32[]{:S(2)}) collective-permute-start(bf16[1536,128]{1,0:T(8,128)(2,1)} %slice.25), channel_id=1, source_target_pairs={{0,3},{1,0},{2,1},{3,2},{4,7},{5,4},{6,5},{7,6},{8,11},{9,8},{10,9... | collective-permute-start | bytes 1179656 | tf_op jit(solution)/shard_map/ppermute | solution.py:258
  82.0 14.0 %collective-permute-start.5 = (bf16[1536,128]{1,0:T(8,128)(2,1)}, bf16[1536,128]{1,0:T(8,128)(2,1)}, u32[]{:S(2)}, u32[]{:S(2)}) collective-permute-start(bf16[1536,128]{1,0:T(8,128)(2,1)} %slice.24), channel_id=1, source_target_pairs={{0,1},{1,2},{2,3},{3,0},{4,5},{5,6},{6,7},{7,4},{8,9},{9,10},{10,1... | collective-permute-start | bytes 1179656 | tf_op jit(solution)/shard_map/ppermute | solution.py:257
  87.2 5.8 %copy-start.4 = (bf16[3072,128]{1,0:T(8,128)(2,1)}, bf16[3072,128]{1,0:T(8,128)(2,1)S(1)}, u32[]{:S(2)}) copy-start(bf16[3072,128]{1,0:T(8,128)(2,1)S(1)} %collective-permute-done.8.refs_7_) | copy-start | bytes 2359300
  88.0 10.5 %collective-permute-start.10 = (bf16[1536,128]{1,0:T(8,128)(2,1)}, bf16[1536,128]{1,0:T(8,128)(2,1)}, u32[]{:S(2)}, u32[]{:S(2)}) collective-permute-start(bf16[1536,128]{1,0:T(8,128)(2,1)} %slice.27), channel_id=1, source_target_pairs={{0,12},{4,0},{8,4},{12,8},{1,13},{5,1},{9,5},{13,9},{2,14},{6,2},{... | collective-permute-start | bytes 1179656 | tf_op jit(solution)/shard_map/ppermute | solution.py:258
  93.0 1.1 copy-start.5
  94.0 11.2 %collective-permute-start.9 = (bf16[1536,128]{1,0:T(8,128)(2,1)}, bf16[1536,128]{1,0:T(8,128)(2,1)}, u32[]{:S(2)}, u32[]{:S(2)}) collective-permute-start(bf16[1536,128]{1,0:T(8,128)(2,1)} %slice.26), channel_id=1, source_target_pairs={{0,4},{4,8},{8,12},{12,0},{1,5},{5,9},{9,13},{13,1},{2,6},{6,10},{... | collective-permute-start | bytes 1179656 | tf_op jit(solution)/shard_map/ppermute | solution.py:257
  108.8 3.8 %collective-permute-start.11 = (f32[16,64,128]{2,1,0:T(8,128)S(1)}, f32[16,64,128]{2,1,0:T(8,128)S(1)}, u32[]{:S(2)}, u32[]{:S(2)}) collective-permute-start(f32[16,64,128]{2,1,0:T(8,128)S(1)} %get-tuple-element.14), channel_id=1, source_target_pairs={{0,16},{16,0},{1,17},{17,1},{2,18},{18,2},{3,19},{19,3},{4,20},{20... | collective-permute-start | bytes 1572872 | tf_op jit(solution)/shard_map/ppermute | solution.py:338
  153.3 9.7 %collective-permute-start.12 = (f32[64,128]{1,0:T(8,128)S(1)}, f32[64,128]{1,0:T(8,128)S(1)}, u32[]{:S(2)}, u32[]{:S(2)}) collective-permute-start(f32[64,128]{1,0:T(8,128)S(1)} %broadcast_multiply_fusion), channel_id=1, source_target_pairs={{0,0},{1,32},{2,64},{3,96},{4,4},{5,36},{6,68},{7,100},{8,8},{9,40... | collective-permute-start | bytes 98312 | tf_op jit(solution)/shard_map/ppermute | solution.py:341

commit v2 on v1

v2 whole, which is shorter than its diff:
```python
import functools

import jax
import jax.numpy as jnp
from jax import lax
from jax.experimental import pallas as pl
from jax.experimental.pallas import tpu as pltpu
from jax.sharding import Mesh
from jax.sharding import PartitionSpec as P

F32 = jnp.float32
BF16 = jnp.bfloat16
AXES = ("zh", "zl", "core", "y", "x")
SPACE = ("zh", "zl", "core")
MODE = ("y", "x")
VMEM_BYTES = 16 * 1024 * 1024


def kernel_call(body, outs, scratch=(), flops=0, moved=0, name=None):
    whole = pl.BlockSpec(memory_space=pltpu.VMEM)
    multiple = isinstance(outs, (tuple, list))
    return pl.pallas_call(
        body,
        out_shape=outs,
        out_specs=[whole] * len(outs) if multiple else whole,
        scratch_shapes=list(scratch),
        compiler_params=pltpu.CompilerParams(vmem_limit_bytes=VMEM_BYTES),
        cost_estimate=pl.CostEstimate(flops=flops, bytes_accessed=moved, transcendentals=0),
        name=name,
    )


def split3(a):
    high = a.astype(BF16)
    rest = a - high.astype(F32)
    mid = rest.astype(BF16)
    low = (rest - mid.astype(F32)).astype(BF16)
    return high, mid, low


def dot_rows(a, b):
    return lax.dot_general(a, b, (((0,), (0,)), ((), ())), preferred_element_type=F32)


def coefficient_kernel(flow_ref, gradient_ref, viscosity_ref, out_ref):
    def wide(values):
        return jnp.concatenate([values[x] for x in range(values.shape[0])], axis=1)

    nu = wide(viscosity_ref[...])
    level = lax.broadcasted_iota(jnp.int32, nu.shape, 0)
    for d in range(3):
        half = 0.5 * wide(flow_ref[d])
        ahead, back = nu - half, nu + half
        if d == 2:
            ahead = jnp.where(level < nu.shape[0] - 1, ahead, 0.0)
            back = jnp.where(level > 0, back, 0.0)
        out_ref[2 * d] = ahead
        out_ref[2 * d + 1] = back
    for i in range(3):
        for j in range(3):
            own = wide(gradient_ref[i, j])
            out_ref[6 + 3 * i + j] = own + 6.0 * nu if i == j else own


def gram_kernel(x_ref, out_ref):
    rows = x_ref.shape[0]
    step = rows // 3
    total = jnp.zeros((256, 256), F32)
    side = jnp.zeros((128, 128), F32)
    for start in range(0, rows, step):
        high, mid, low = split3(x_ref[start : start + step, :])
        both = jnp.concatenate([high, mid], axis=1)
        total = total + dot_rows(both, both)
        side = side + dot_rows(high, low)
    gram = total[:128, :128] + total[:128, 128:] + total[128:, :128] + total[128:, 128:]
    gram = gram + side + side.T
    top, bottom = gram[:64], gram[64:]
    row = lax.broadcasted_iota(jnp.int32, (64, 128), 0)
    lane = lax.broadcasted_iota(jnp.int32, (64, 128), 1)
    packed = jnp.where((lane >= 64) & (row >= lane - 64), pltpu.roll(top, 64, 1), bottom)
    diagonal = jnp.sum(jnp.where(row == lane - 64, bottom, 0.0), axis=0, keepdims=True)
    out_ref[:64, :] = packed
    out_ref[64:, :] = jnp.broadcast_to(diagonal, (8, 128))


def times_inverse(inverse):
    high, mid, low = (inverse[:, 128 * t : 128 * t + 128] for t in range(3))
    pair = jnp.concatenate([high, mid], axis=1)
    main = jnp.concatenate([pair, pair], axis=0)
    side = jnp.concatenate([low, high], axis=0)

    def times(values):
        h, m, l = split3(values)
        first = jnp.dot(jnp.concatenate([h, m], axis=1), main, preferred_element_type=F32)
        second = jnp.dot(jnp.concatenate([h, l], axis=1), side, preferred_element_type=F32)
        return first[:, :128] + (first[:, 128:] + second)

    return times


def modes_kernel(x_ref, inverse_ref, rounded_ref):
    times = times_inverse(inverse_ref[...])
    step = 1024
    for first in range(0, x_ref.shape[0], step):
        at = slice(first, first + step)
        rounded_ref[at, :] = times(x_ref[at, :]).astype(BF16)


def image_kernel(
    x_ref, west_ref, east_ref, coefficient_ref, inverse_ref,
    advected_ref, rounded_ref, raw_ref, sems,
):
    cells_x, cells_y, cells_z = x_ref.shape[1:4]
    layer = cells_y * cells_z
    times = times_inverse(inverse_ref[...])
    sent = []
    values = [coefficient_ref[n] for n in range(15)]
    for x in range(cells_x):
        for y in range(cells_y):
            place = slice(x * cells_y + y, x * cells_y + y + 1)
            cell = [jnp.broadcast_to(v[:, place], (8, 128)) for v in values]
            east_c, west_c, north_c, south_c, upper_c, lower_c = cell[:6]
            center = [x_ref[i, x, y] for i in range(3)]
            for i in range(3):
                east = x_ref[i, x + 1, y] if x + 1 < cells_x else east_ref[i, 0, y]
                west = x_ref[i, x - 1, y] if x > 0 else west_ref[i, 0, y]
                image = east_c * east + west_c * west
                if y + 1 < cells_y:
                    image = image + north_c * x_ref[i, x, y + 1]
                if y > 0:
                    image = image + south_c * x_ref[i, x, y - 1]
                image = image + upper_c * pltpu.roll(center[i], 7, 0)
                image = image + lower_c * pltpu.roll(center[i], 1, 0)
                for j in range(3):
                    image = image - cell[6 + 3 * i + j] * center[j]
                first = ((i * cells_x + x) * cells_y + y) * cells_z
                raw_ref[first : first + cells_z, :] = image

        if x % 2 == 1:
            for i in range(3):
                first = (i * cells_x + x - 1) * layer
                at = pl.ds(first, 2 * layer)
                advected = times(raw_ref[at, :])
                raw_ref[at, :] = advected
                rounded_ref[at, :] = advected.astype(BF16)
                sent.append(
                    pltpu.make_async_copy(
                        raw_ref.at[at, :], advected_ref.at[at, :], sems.at[len(sent)]
                    )
                )
                sent[-1].start()
    for copy in sent:
        copy.wait()


def pair_kernel(a_ref, b_ref, out_ref):
    total = a_ref[...] + b_ref[...]
    for n in range(4):
        out_ref[n] = total


def four_kernel(parts_ref, out_ref):
    total = (parts_ref[0] + parts_ref[1]) + (parts_ref[2] + parts_ref[3])
    for n in range(4):
        out_ref[n] = total


def factor_kernel(weight, parts_ref, west_ref, east_ref, coefficient_ref, r_ref, inverse_ref):
    del west_ref, east_ref, coefficient_ref
    packed = parts_ref[0] + parts_ref[1] + (parts_ref[2] + parts_ref[3])
    packed = packed * weight
    top = packed[:64]
    diagonal = packed[64:65]
    turned = pltpu.roll(top, 64, 1)
    across = jnp.concatenate([top, turned], axis=0).T
    row = lax.broadcasted_iota(jnp.int32, (64, 128), 0)
    lane = lax.broadcasted_iota(jnp.int32, (64, 128), 1)
    upper_half = jnp.where((lane < 64) & (row >= lane), turned, across[64:])
    lower_half = jnp.where(
        (lane < 64) | (row < lane - 64), top, jnp.where(row > lane - 64, across[:64], diagonal)
    )
    a = [upper_half[8 * b : 8 * b + 8] for b in range(8)]
    a += [lower_half[8 * b : 8 * b + 8] for b in range(8)]
    sub = lax.broadcasted_iota(jnp.int32, (8, 128), 0)
    col = lax.broadcasted_iota(jnp.int32, (8, 128), 1)
    w = [jnp.where(sub + 8 * b == col, 1.0, 0.0).astype(F32) for b in range(16)]

    def spread_row(values, t):
        return jnp.broadcast_to(values[t : t + 1, :], (8, 128))

    def combine(columns, values):
        terms = [c * spread_row(values, t) for t, c in enumerate(columns)]
        while len(terms) > 1:
            terms = [p + q for p, q in zip(terms[::2], terms[1::2])]
        return terms[0]

    inverse_rows = []
    for k in range(16):
        r, v = a[k], w[k]
        e = {}
        for j in range(8):
            column = jnp.broadcast_to(r[:, 8 * k + j : 8 * k + j + 1], (8, 128))
            for i in range(j + 1):
                e[i, j] = spread_row(column, i)
        inv = {}
        u = {}
        for t in range(8):
            scale = lax.rsqrt(e[t, t])
            inv[t, t] = scale
            for j in range(t + 1, 8):
                u[t, j] = e[t, j] * scale
            for i in range(t + 1, 8):
                for j in range(i, 8):
                    e[i, j] = e[i, j] - u[t, i] * u[t, j]
        for t in range(8):
            for i in range(t + 1, 8):
                total = u[t, i] * inv[t, t]
                for m in range(t + 1, i):
                    total = total + u[m, i] * inv[m, t]
                inv[i, t] = -inv[i, i] * total
        columns, turned_columns = [], []
        for j in range(8):
            column = jnp.zeros((8, 128), F32)
            for i in range(j, 8):
                column = jnp.where(sub == i, inv[i, j], column)
            columns.append(column)
            column = jnp.zeros((8, 128), F32)
            for i in range(j + 1):
                column = jnp.where(sub == i, inv[j, i], column)
            turned_columns.append(column)
        upper = combine(columns, r)
        lower_inverse = combine(columns, v)
        r_ref[8 * k : 8 * k + 8, :] = jnp.where(col >= sub + 8 * k, upper, 0.0)
        inverse_rows.append(lower_inverse)
        if k < 15:
            z = combine(turned_columns, upper)
            zv = combine(turned_columns, lower_inverse)
            z_rows = [spread_row(z, t) for t in range(8)]
            zv_rows = [spread_row(zv, t) for t in range(8)]
            for b in range(k + 1, 16):
                cs = [
                    jnp.broadcast_to(a[b][:, 8 * k + j : 8 * k + j + 1], (8, 128)) for j in range(8)
                ]
                s = [c * z_rows[j] for j, c in enumerate(cs)]
                sv = [c * zv_rows[j] for j, c in enumerate(cs)]
                a[b] = a[b] - (((s[0] + s[1]) + (s[2] + s[3])) + ((s[4] + s[5]) + (s[6] + s[7])))
                w[b] = w[b] - (
                    ((sv[0] + sv[1]) + (sv[2] + sv[3])) + ((sv[4] + sv[5]) + (sv[6] + sv[7]))
                )
    r_inverse = jnp.concatenate(inverse_rows, axis=0).T
    high, mid, low = split3(r_inverse)
    inverse_ref[:, :128] = high
    inverse_ref[:, 128:256] = mid
    inverse_ref[:, 256:] = low


def product_kernel(mode_turns, place_ref, *refs):
    mode_refs = refs[: len(mode_turns)]
    image_refs = refs[len(mode_turns) : -3]
    keep_ref, send_ref, total_ref = refs[-3:]
    half = mode_refs[0].shape[0] // 2
    for part in range(2):
        at = slice(part * half, part * half + half)
        wide = [
            jnp.concatenate([r[at, :] for r in group], axis=1) for group in (mode_refs, image_refs)
        ]
        product = dot_rows(wide[1], wide[0])
        if part == 0:
            total_ref[...] = product
        else:
            total_ref[...] += product
    core, x = place_ref[0], place_ref[1]
    ahead = 2 * core - 1
    for a, mode_turn in enumerate(mode_turns):
        panel_x = lax.rem(x + 4 + ahead * mode_turn, 4)
        lanes = slice(128 * a, 128 * a + 128)
        for b in range(len(image_refs)):
            slot = b if b == 0 else b + core * (3 - 2 * b)
            mine = pl.ds(pl.multiple_of(128 * b + 64 * core, 64), 64)
            other = pl.ds(pl.multiple_of(128 * b + 64 * (1 - core), 64), 64)
            keep_ref[panel_x, slot] = total_ref[mine, lanes]
            send_ref[panel_x, slot] = total_ref[other, lanes]


def product(place, modes, images, mode_turns):
    shape = jax.ShapeDtypeStruct((4, len(images), 64, 128), F32)
    whole = pl.BlockSpec(memory_space=pltpu.VMEM)
    return pl.pallas_call(
        functools.partial(product_kernel, mode_turns),
        out_shape=(shape, shape),
        in_specs=[pl.BlockSpec(memory_space=pltpu.SMEM)] + [whole] * (len(modes) + len(images)),
        out_specs=[whole, whole],
        scratch_shapes=[pltpu.VMEM((128 * len(images), 128 * len(modes)), F32)],
        compiler_params=pltpu.CompilerParams(vmem_limit_bytes=VMEM_BYTES),
        cost_estimate=pl.CostEstimate(
            flops=100_000_000 * len(modes) * len(images), bytes_accessed=6_000_000, transcendentals=0
        ),
    )(place, *modes, *images)


def join_kernel(keep_ref, received_ref, keep_last_ref, received_last_ref, out_ref):
    for n in range(4):
        out_ref[n, :3] = keep_ref[n] + received_ref[n]
        out_ref[n, 3] = keep_last_ref[n, 0] + received_last_ref[n, 0]


def near_kernel(place_ref, parts_ref, out_ref):
    y = place_ref[2]
    for slot, turn in enumerate((0, -1, 1, 2)):
        out_ref[lax.rem(y + 4 + turn, 4)] = (parts_ref[0, slot] + parts_ref[1, slot]) + (
            parts_ref[2, slot] + parts_ref[3, slot]
        )


def far_kernel(weight, parts_ref, out_ref):
    out_ref[...] = ((parts_ref[0] + parts_ref[1]) + (parts_ref[2] + parts_ref[3])) * weight


AHEAD = [(i, (i + 1) % 4) for i in range(4)] + [(4 + i, 4 + (i + 3) % 4) for i in range(4)]
BACK = [(target, source) for source, target in AHEAD]


def pass_on(block, axis, pairs):
    return lax.ppermute(block, ("core", axis), pairs)


SWAP = [(0, 1), (1, 0)]


def copies(block, count):
    return jnp.broadcast_to(block[None], (count,) + block.shape)


def turn_over(block):
    pairs = [(4 * zl + x, 4 * x + zl) for zl in range(4) for x in range(4)]
    return lax.ppermute(block, ("zl", "x"), pairs)


def body(basis, mean_flow, flow_gradient, viscosity):
    _, cells_x, cells_y, cells_z, width = basis.shape
    rows = 3 * cells_x * cells_y * cells_z
    blocks = 32
    weight = 1.0 / (rows * blocks)
    flat = basis.reshape(rows, width)
    west = lax.ppermute(basis[:, -1:], SPACE, [(i, i + 1) for i in range(blocks - 1)])
    east = lax.ppermute(basis[:, :1], SPACE, [(i + 1, i) for i in range(blocks - 1)])

    packed = jax.ShapeDtypeStruct((72, 128), F32)
    packed4 = jax.ShapeDtypeStruct((4, 72, 128), F32)
    gram = kernel_call(gram_kernel, packed, flops=600_000_000, moved=1_600_000)(flat)
    coefficients = kernel_call(
        coefficient_kernel,
        jax.ShapeDtypeStruct((15, cells_z, cells_x * cells_y), F32),
        flops=200_000,
        moved=500_000,
    )(mean_flow.swapaxes(2, 3), flow_gradient.swapaxes(3, 4), viscosity.swapaxes(1, 2))
    received = lax.ppermute(gram, "core", SWAP)
    mine = kernel_call(pair_kernel, packed4, moved=200_000)(gram, received)
    near = lax.all_to_all(mine, "zl", 0, 0, tiled=True)
    near = kernel_call(four_kernel, packed4, moved=300_000)(near)
    parts = lax.all_to_all(near, "zh", 0, 0, tiled=True)
    whole = pl.BlockSpec(memory_space=pltpu.VMEM)
    anywhere = pl.BlockSpec(memory_space=pl.ANY)
    r_factor, inverse = pl.pallas_call(
        functools.partial(factor_kernel, weight),
        out_shape=(
            jax.ShapeDtypeStruct((128, 128), F32),
            jax.ShapeDtypeStruct((128, 384), BF16),
        ),
        in_specs=[whole, anywhere, anywhere, anywhere],
        out_specs=[whole, whole],
        compiler_params=pltpu.CompilerParams(vmem_limit_bytes=VMEM_BYTES),
        cost_estimate=pl.CostEstimate(flops=10_000_000, bytes_accessed=400_000, transcendentals=0),
    )(parts, west, east, coefficients)
    rounded = pl.pallas_call(
        modes_kernel,
        out_shape=jax.ShapeDtypeStruct((rows, width), BF16),
        in_specs=[whole, whole],
        out_specs=whole,
        compiler_params=pltpu.CompilerParams(vmem_limit_bytes=VMEM_BYTES),
        cost_estimate=pl.CostEstimate(
            flops=600_000_000, bytes_accessed=2_400_000, transcendentals=0
        ),
    )(flat, inverse)
    modes = [rounded, pass_on(rounded, "x", AHEAD), pass_on(rounded, "x", BACK)]
    advected, rounded_image = pl.pallas_call(
        image_kernel,
        out_shape=(
            jax.ShapeDtypeStruct((rows, width), F32),
            jax.ShapeDtypeStruct((rows, width), BF16),
        ),
        in_specs=[whole] * 5,
        out_specs=[anywhere, whole],
        scratch_shapes=[
            pltpu.VMEM((rows, width), F32),
            pltpu.SemaphoreType.DMA((3 * (cells_x // 2),)),
        ],
        compiler_params=pltpu.CompilerParams(vmem_limit_bytes=VMEM_BYTES),
        cost_estimate=pl.CostEstimate(
            flops=600_000_000, bytes_accessed=5_000_000, transcendentals=0
        ),
    )(
        basis,
        west,
        east,
        coefficients,
        inverse,
    )
    images = [rounded_image, pass_on(rounded_image, "y", AHEAD), pass_on(rounded_image, "y", BACK)]
    modes.append(pass_on(modes[1], "x", AHEAD))
    last_image = pass_on(images[1], "y", AHEAD)

    place = jnp.stack([lax.axis_index(axis) for axis in ("core", "x", "y")])
    turns = (0, 1, -1, 2)
    keep, send = product(place, modes, images, turns)
    received = lax.ppermute(send, "core", SWAP)
    keep_last, send_last = product(place, modes, [last_image], turns)
    received_last = lax.ppermute(send_last, "core", SWAP)
    partial = kernel_call(
        join_kernel, jax.ShapeDtypeStruct((4, 4, 64, 128), F32), moved=1_500_000
    )(keep, received, keep_last, received_last)
    near = lax.all_to_all(partial, "zl", 0, 0, tiled=True)
    near = pl.pallas_call(
        near_kernel,
        out_shape=jax.ShapeDtypeStruct((4, 64, 128), F32),
        in_specs=[pl.BlockSpec(memory_space=pltpu.SMEM), whole],
        out_specs=whole,
        compiler_params=pltpu.CompilerParams(vmem_limit_bytes=VMEM_BYTES),
    )(place, near)
    far = lax.all_to_all(near, "zh", 0, 0, tiled=True)
    piece = kernel_call(
        functools.partial(far_kernel, weight), jax.ShapeDtypeStruct((64, 128), F32), moved=200_000
    )(far)
    reduced = turn_over(piece).T
    return reduced, advected.reshape(basis.shape), r_factor


def solution(mesh):
    fine = Mesh(mesh.devices.reshape(4, 4, 2, 4, 4), AXES)
    placed = (
        P(None, SPACE, None, None, MODE),
        P(None, SPACE, None, None),
        P(None, None, SPACE, None, None),
        P(SPACE, None, None),
    )
    return jax.shard_map(
        body,
        mesh=fine,
        in_specs=placed,
        out_specs=(P(MODE, SPACE), P(None, SPACE, None, None, MODE), P(MODE, None)),
        check_vma=False,
    )
```

time: 164 us -> 152 us (0.927); the launches traced: 164 us -> 149 us
  local copies, waits for them, and re-layouts: 9.83 us -> 2.06 us
  blocking collectives: 53.1 us -> 47.5 us
  starting transfers between devices: 52.6 us -> 49.1 us
  Pallas kernels: 16.4 us -> 18.1 us
    all_to_all x2 -> x3, blocking collectives: 53.1 us -> 47.5 us  [the longest x1 17.5 us: body(): far = lax.all_to_all(near, 'zh', 0, 0, tiled=True)]
    all_to_all x1, waiting for transfers between devices: 5.71 us -> 10.1 us  [body(): parts = lax.all_to_all(near, 'zh', 0, 0, tiled=True)]
    ppermute x11 -> x10, waiting for transfers between devices: 24.3 us -> 20.2 us  [the longest x6 14.1 us: pass_on(): return lax.ppermute(block, ('core', axis), pairs)]
    ppermute x11 -> x10, starting transfers between devices: 35.9 us -> 32.4 us  [the longest x6 20.5 us: pass_on(): return lax.ppermute(block, ('core', axis), pairs)]
    slice x4 -> x0, local copies, waits for them, and re-layouts: 3.24 us -> none  [the longest x2 1.64 us: spread(): far_up = lax.ppermute(up[:half], axis, ring(1))]
    unnamed x22 -> x15, local copies, waits for them, and re-layouts: 5.2 us -> 2.04 us
    pallas_call x5 -> x12, Pallas kernels: 16.4 us -> 18.1 us  [the longest x1 5.51 us: body(): pl.pallas_call(functools.partial(factor_kernel, weight), out_shape=(jax.S...]
  transfers between devices with their start and end apart: 14 -> 13, of which waited for: 8 -> 9; matrix products, arithmetic and copies ran while one was open for 3% -> 0% of each run, Pallas kernels for 2% -> 6%
where the time goes in v2:
time: 152 us; the launch traced here: 149 us
  starting transfers between devices  49.1 us (32%)
  blocking collectives  47.5 us (31%)
  waiting for transfers between devices  31.1 us (20%)
  Pallas kernels  18.1 us (12%)
  local copies, waits for them, and re-layouts  2.06 us (1%)
    ppermute x6, starting transfers between devices, pass_on(): return lax.ppermute(block, ('core', axis), pairs)  20.5 us
    all_to_all x1, blocking collectives, body(): far = lax.all_to_all(near, 'zh', 0, 0, tiled=True)  17.5 us
    all_to_all x1, blocking collectives, body(): near = lax.all_to_all(partial, 'zl', 0, 0, tiled=True)  17.5 us
    ppermute x6, waiting for transfers between devices, pass_on(): return lax.ppermute(block, ('core', axis), pairs)  14.1 us
    all_to_all x1, blocking collectives, body(): near = lax.all_to_all(mine, 'zl', 0, 0, tiled=True)  12.5 us
    all_to_all x1, starting transfers between devices, body(): parts = lax.all_to_all(near, 'zh', 0, 0, tiled=True)  12.4 us
    all_to_all x1, waiting for transfers between devices, body(): parts = lax.all_to_all(near, 'zh', 0, 0, tiled=True)  10.1 us
    ppermute x1, starting transfers between devices, turn_over(): return lax.ppermute(block, ('zl', 'x'), pairs)  6.12 us
  transfers between devices with their start and end apart: 13, of which 9 were waited for; matrix products, arithmetic and copies ran while one was open for 0% of the time, Pallas kernels for 6%

profile of v2, /device:TPU:6, one launch (start us, length us, event | category | flops | bytes accessed | tf_op | source)
XLA Modules:
  0.0 148.8 jit_solution(17647866182629140034)
XLA Ops:
  3.0 1.9 %collective-permute-start = (f32[72,128]{1,0:T(8,128)S(1)}, f32[72,128]{1,0:T(8,128)S(1)}, u32[]{:S(2)}, u32[]{:S(2)}) collective-permute-start(f32[72,128]{1,0:T(8,128)S(1)} %shard_map.67.a_ref), channel_id=1, source_target_pairs={{0,16},{16,0},{1,17},{17,1},{2,18},{18,2},{3,19},{19,3},{4,20},{20... | collective-permute-start | bytes 110600 | tf_op jit(solution)/shard_map/ppermute | solution.py:357
  6.1 12.5 %all_to_all.20.parts_ref = f32[4,72,128]{2,1,0:T(8,128)S(1)} all-to-all(f32[4,72,128]{2,1,0:T(8,128)S(1)} %shard_map.68), channel_id=1, replica_groups=mesh['zh'=4,'zl'=4,'core'=2,'y'=4,'x'=4] {'zl'}, dimensions={0} | all-to-all | bytes 294912 | tf_op jit(solution)/shard_map/all_to_all | solution.py:359
  19.3 12.4 %all-to-all-start.1 = ((f32[4,72,128]{2,1,0:T(8,128)}), f32[4,72,128]{2,1,0:T(8,128)S(1)}, u32[]{:S(2)}, u32[]{:S(2)}) async-start(f32[4,72,128]{2,1,0:T(8,128)} %shard_map.69), calls=%async_computation.1 | async-start | bytes 294912 | tf_op jit(solution)/shard_map/all_to_all | solution.py:361
  33.0 3.0 %collective-permute-start.1 = (f32[3,1,16,8,128]{4,3,2,1,0:T(8,128)S(1)}, f32[3,1,16,8,128]{4,3,2,1,0:T(8,128)S(1)}, u32[]{:S(2)}, u32[]{:S(2)}) collective-permute-start(f32[3,1,16,8,128]{4,3,2,1,0:T(8,128)S(1)} %get-tuple-element.20), channel_id=1, source_target_pairs={{0,16},{16,32},{32,48},{48,64},{64,80},{80,96},{96,112},{112,128},... | collective-permute-start | bytes 589832 | tf_op jit(solution)/shard_map/ppermute | solution.py:345
  37.1 10.1 %all-to-all-done.1.parts_ref = f32[4,72,128]{2,1,0:T(8,128)S(1)} async-done(((f32[4,72,128]{2,1,0:T(8,128)}), f32[4,72,128]{2,1,0:T(8,128)S(1)}, u32[]{:S(2)}, u32[]{:S(2)}) %all-to-all-start.1) | async-done | bytes 147488 | tf_op jit(solution)/shard_map/all_to_all | solution.py:361
  47.1 5.5 %shard_map.71 = (f32[128,128]{1,0:T(8,128)}, bf16[128,384]{1,0:T(8,128)(2,1)S(1)}) custom-call(f32[4,72,128]{2,1,0:T(8,128)S(1)} %all-to-all-done.1.parts_ref, f32[3,1,16,8,128]{4,3,2,1,0:T(8,128)S(1)} %collective-permute-done.1.west_ref, f32[3,1,16,8,128]{4,3,2,1,0:T(8,128)S(1)} %collective-permute-done.2.east_ref, f32[15,8,128]{2,1,0:T(8,128)S(1)} %shard_map.70.coefficient_ref), custom_call_target="tpu_custom_call" | custom-call | flops 10000000 | bytes 400000 | tf_op jit(solution)/shard_map/pallas_call | solution.py:364
  53.7 2.4 %collective-permute-start.3 = (bf16[3072,128]{1,0:T(8,128)(2,1)S(1)}, bf16[3072,128]{1,0:T(8,128)(2,1)S(1)}, u32[]{:S(2)}, u32[]{:S(2)}) collective-permute-start(bf16[3072,128]{1,0:T(8,128)(2,1)S(1)} %shard_map.72.refs_0_), channel_id=1, source_target_pairs={{0,1},{1,2},{2,3},{3,0},{16,19},{17,16},{18,17},{19,18},{4,5},{5,6... | collective-permute-start | bytes 2359304 | tf_op jit(solution)/shard_map/ppermute | solution.py:324
  56.1 4.4 %shard_map.73 = (f32[3072,128]{1,0:T(8,128)}, bf16[3072,128]{1,0:T(8,128)(2,1)}) custom-call(f32[3,8,16,8,128]{4,3,2,1,0:T(8,128)S(1)} %copy-done.1, f32[3,1,16,8,128]{4,3,2,1,0:T(8,128)S(1)} %copy-done.4, f32[3,1,16,8,128]{4,3,2,1,0:T(8,128)S(1)} %collective-permute-done.2.east_ref, f32[15,8,128]{2,1,0:T(8,128)S(1)} %shard_map.70.coefficient_ref, ...), custom_call_target="tpu_custom_call" | custom-call | flops 600000000 | bytes 5000000 | tf_op jit(solution)/shard_map/pallas_call | solution.py:386
  60.5 3.5 %collective-permute-start.6 = (bf16[3072,128]{1,0:T(8,128)(2,1)}, bf16[3072,128]{1,0:T(8,128)(2,1)}, u32[]{:S(2)}, u32[]{:S(2)}) collective-permute-start(bf16[3072,128]{1,0:T(8,128)(2,1)} %get-tuple-element.12.refs_4_), channel_id=1, source_target_pairs={{0,4},{4,8},{8,12},{12,0},{16,28},{20,16},{24,20},{28,24},{1,5},{5... | collective-permute-start | bytes 2359304 | tf_op jit(solution)/shard_map/ppermute | solution.py:324
  64.0 3.5 %collective-permute-start.4 = (bf16[3072,128]{1,0:T(8,128)(2,1)S(1)}, bf16[3072,128]{1,0:T(8,128)(2,1)S(1)}, u32[]{:S(2)}, u32[]{:S(2)}) collective-permute-start(bf16[3072,128]{1,0:T(8,128)(2,1)S(1)} %shard_map.72.refs_0_), channel_id=1, source_target_pairs={{1,0},{2,1},{3,2},{0,3},{19,16},{16,17},{17,18},{18,19},{5,4},{6,5... | collective-permute-start | bytes 2359304 | tf_op jit(solution)/shard_map/ppermute | solution.py:324
  67.4 3.6 %collective-permute-start.7 = (bf16[3072,128]{1,0:T(8,128)(2,1)}, bf16[3072,128]{1,0:T(8,128)(2,1)}, u32[]{:S(2)}, u32[]{:S(2)}) collective-permute-start(bf16[3072,128]{1,0:T(8,128)(2,1)} %get-tuple-element.12.refs_4_), channel_id=1, source_target_pairs={{4,0},{8,4},{12,8},{0,12},{28,16},{16,20},{20,24},{24,28},{5,1},{9... | collective-permute-start | bytes 2359304 | tf_op jit(solution)/shard_map/ppermute | solution.py:324
  71.0 3.6 %collective-permute-start.5 = (bf16[3072,128]{1,0:T(8,128)(2,1)S(1)}, bf16[3072,128]{1,0:T(8,128)(2,1)S(1)}, u32[]{:S(2)}, u32[]{:S(2)}) collective-permute-start(bf16[3072,128]{1,0:T(8,128)(2,1)S(1)} %collective-permute-done.3.refs_1_), channel_id=1, source_target_pairs={{0,1},{1,2},{2,3},{3,0},{16,19},{17,16},{18,17},{19,18},{4,5},{5,6... | collective-permute-start | bytes 2359304 | tf_op jit(solution)/shard_map/ppermute | solution.py:324
  74.6 6.8 %collective-permute-done.6.refs_5_ = bf16[3072,128]{1,0:T(8,128)(2,1)} collective-permute-done((bf16[3072,128]{1,0:T(8,128)(2,1)}, bf16[3072,128]{1,0:T(8,128)(2,1)}, u32[]{:S(2)}, u32[]{:S(2)}) %collective-permute-start.6) | collective-permute-done | bytes 786464 | tf_op jit(solution)/shard_map/ppermute | solution.py:324
  81.4 4.0 %collective-permute-start.9 = (bf16[3072,128]{1,0:T(8,128)(2,1)}, bf16[3072,128]{1,0:T(8,128)(2,1)}, u32[]{:S(2)}, u32[]{:S(2)}) collective-permute-start(bf16[3072,128]{1,0:T(8,128)(2,1)} %collective-permute-done.6.refs_5_), channel_id=1, source_target_pairs={{0,4},{4,8},{8,12},{12,0},{16,28},{20,16},{24,20},{28,24},{1,5},{5... | collective-permute-start | bytes 2359304 | tf_op jit(solution)/shard_map/ppermute | solution.py:324
  86.2 2.8 %collective-permute-done.7.refs_6_ = bf16[3072,128]{1,0:T(8,128)(2,1)} collective-permute-done((bf16[3072,128]{1,0:T(8,128)(2,1)}, bf16[3072,128]{1,0:T(8,128)(2,1)}, u32[]{:S(2)}, u32[]{:S(2)}) %collective-permute-start.7) | collective-permute-done | bytes 786464 | tf_op jit(solution)/shard_map/ppermute | solution.py:324
  89.0 3.1 %shard_map.74 = (f32[4,3,64,128]{3,2,1,0:T(8,128)S(1)}, f32[4,3,64,128]{3,2,1,0:T(8,128)S(1)}) custom-call(s32[3]{0:T(128)S(1)} %pad_add_fusion.place_ref, bf16[3072,128]{1,0:T(8,128)(2,1)S(1)} %shard_map.72.refs_0_, bf16[3072,128]{1,0:T(8,128)(2,1)S(1)} %collective-permute-done.3.refs_1_, bf16[3072,128]{1,0:T(8,128)(2,1)S(1)} %collective-permute-done.4.refs_2_, ...), custom_call_target="tpu_custom_call" | custom-call | flops 1200000000 | bytes 6000000 | tf_op jit(solution)/shard_map/pallas_call | solution.py:288
  92.1 1.9 %collective-permute-start.8 = (f32[4,3,64,128]{3,2,1,0:T(8,128)S(1)}, f32[4,3,64,128]{3,2,1,0:T(8,128)S(1)}, u32[]{:S(2)}, u32[]{:S(2)}) collective-permute-start(f32[4,3,64,128]{3,2,1,0:T(8,128)S(1)} %get-tuple-element.14), channel_id=1, source_target_pairs={{0,16},{16,0},{1,17},{17,1},{2,18},{18,2},{3,19},{19,3},{4,20},{20... | collective-permute-start | bytes 1179656 | tf_op jit(solution)/shard_map/ppermute | solution.py:416
  94.0 3.8 %collective-permute-done.9.refs_4_ = bf16[3072,128]{1,0:T(8,128)(2,1)} collective-permute-done((bf16[3072,128]{1,0:T(8,128)(2,1)}, bf16[3072,128]{1,0:T(8,128)(2,1)}, u32[]{:S(2)}, u32[]{:S(2)}) %collective-permute-start.9) | collective-permute-done | bytes 786464 | tf_op jit(solution)/shard_map/ppermute | solution.py:324
  97.8 1.8 %shard_map.75 = (f32[4,1,64,128]{3,2,1,0:T(8,128)S(1)}, f32[4,1,64,128]{3,2,1,0:T(8,128)S(1)}) custom-call(s32[3]{0:T(128)S(1)} %pad_add_fusion.place_ref, bf16[3072,128]{1,0:T(8,128)(2,1)S(1)} %shard_map.72.refs_0_, bf16[3072,128]{1,0:T(8,128)(2,1)S(1)} %collective-permute-done.3.refs_1_, bf16[3072,128]{1,0:T(8,128)(2,1)S(1)} %collective-permute-done.4.refs_2_, ...), custom_call_target="tpu_custom_call" | custom-call | flops 400000000 | bytes 6000000 | tf_op jit(solution)/shard_map/pallas_call | solution.py:288
  99.6 1.9 %collective-permute-start.10 = (f32[4,1,64,128]{3,2,1,0:T(8,128)S(1)}, f32[4,1,64,128]{3,2,1,0:T(8,128)S(1)}, u32[]{:S(2)}, u32[]{:S(2)}) collective-permute-start(f32[4,1,64,128]{3,2,1,0:T(8,128)S(1)} %get-tuple-element.16), channel_id=1, source_target_pairs={{0,16},{16,0},{1,17},{17,1},{2,18},{18,2},{3,19},{19,3},{4,20},{20... | collective-permute-start | bytes 393224 | tf_op jit(solution)/shard_map/ppermute | solution.py:418
  102.9 17.5 %all_to_all.21.parts_ref = f32[4,4,64,128]{3,2,1,0:T(8,128)S(1)} all-to-all(f32[4,4,64,128]{3,2,1,0:T(8,128)S(1)} %shard_map.76), channel_id=1, replica_groups=mesh['zh'=4,'zl'=4,'core'=2,'y'=4,'x'=4] {'zl'}, dimensions={0} | all-to-all | bytes 1048576 | tf_op jit(solution)/shard_map/all_to_all | solution.py:422
  121.0 17.5 %all_to_all.22.parts_ref = f32[4,64,128]{2,1,0:T(8,128)S(1)} all-to-all(f32[4,64,128]{2,1,0:T(8,128)S(1)} %shard_map.77), channel_id=1, replica_groups=mesh['zh'=4,'zl'=4,'core'=2,'y'=4,'x'=4] {'zh'}, dimensions={0} | all-to-all | bytes 262144 | tf_op jit(solution)/shard_map/all_to_all | solution.py:430
  138.5 6.1 %collective-permute-start.11 = (f32[64,128]{1,0:T(8,128)S(1)}, f32[64,128]{1,0:T(8,128)S(1)}, u32[]{:S(2)}, u32[]{:S(2)}) collective-permute-start(f32[64,128]{1,0:T(8,128)S(1)} %shard_map.78), channel_id=1, source_target_pairs={{0,0},{1,32},{2,64},{3,96},{32,1},{33,33},{34,65},{35,97},{64,2},{... | collective-permute-start | bytes 98312 | tf_op jit(solution)/shard_map/ppermute | solution.py:336
  144.6 3.6 %collective-permute-done.11 = f32[64,128]{1,0:T(8,128)S(1)} collective-permute-done((f32[64,128]{1,0:T(8,128)S(1)}, f32[64,128]{1,0:T(8,128)S(1)}, u32[]{:S(2)}, u32[]{:S(2)}) %collective-permute-start.11) | collective-permute-done | bytes 32800 | tf_op jit(solution)/shard_map/ppermute | solution.py:336
  (34 shorter events, 10.8 us)
Async XLA Ops:
  0.6 1.4 copy-start
  2.0 29.6 %copy-start.1 = (f32[3,8,16,8,128]{4,3,2,1,0:T(8,128)S(1)}, f32[3,8,16,8,128]{4,3,2,1,0:T(8,128)}, u32[]{:S(2)}) copy-start(f32[3,8,16,8,128]{4,3,2,1,0:T(8,128)} %x_ref.1) | copy-start | bytes 4718596
  2.0 34.0 %copy-start.2 = (f32[3,3,8,16,8]{3,4,2,1,0:T(8,128)S(1)}, f32[3,3,8,16,8]{3,4,2,1,0:T(8,128)}, u32[]{:S(2)}) copy-start(f32[3,3,8,16,8]{3,4,2,1,0:T(8,128)} %param.6) | copy-start | bytes 110596
  2.0 34.0 %copy-start.5 = (f32[3,8,16,8]{2,3,1,0:T(8,128)S(1)}, f32[3,8,16,8]{2,3,1,0:T(8,128)}, u32[]{:S(2)}) copy-start(f32[3,8,16,8]{2,3,1,0:T(8,128)} %param.5) | copy-start | bytes 36868
  2.0 34.0 %copy-start.6 = (f32[8,16,8]{1,2,0:T(8,128)S(1)}, f32[8,16,8]{1,2,0:T(8,128)}, u32[]{:S(2)}) copy-start(f32[8,16,8]{1,2,0:T(8,128)} %param.7) | copy-start | bytes 12292
  3.0 3.1 %collective-permute-start = (f32[72,128]{1,0:T(8,128)S(1)}, f32[72,128]{1,0:T(8,128)S(1)}, u32[]{:S(2)}, u32[]{:S(2)}) collective-permute-start(f32[72,128]{1,0:T(8,128)S(1)} %shard_map.67.a_ref), channel_id=1, source_target_pairs={{0,16},{16,0},{1,17},{17,1},{2,18},{18,2},{3,19},{19,3},{4,20},{20... | collective-permute-start | bytes 110600 | tf_op jit(solution)/shard_map/ppermute | solution.py:357
  19.3 27.9 %all-to-all-start.1 = ((f32[4,72,128]{2,1,0:T(8,128)}), f32[4,72,128]{2,1,0:T(8,128)S(1)}, u32[]{:S(2)}, u32[]{:S(2)}) async-start(f32[4,72,128]{2,1,0:T(8,128)} %shard_map.69), calls=%async_computation.1 | async-start | bytes 294912 | tf_op jit(solution)/shard_map/all_to_all | solution.py:361
  31.7 4.5 %collective-permute-start.2 = (f32[3,1,16,8,128]{4,3,2,1,0:T(8,128)S(1)}, f32[3,1,16,8,128]{4,3,2,1,0:T(8,128)S(1)}, u32[]{:S(2)}, u32[]{:S(2)}) collective-permute-start(f32[3,1,16,8,128]{4,3,2,1,0:T(8,128)S(1)} %get-tuple-element.19), channel_id=1, source_target_pairs={{16,0},{32,16},{48,32},{64,48},{80,64},{96,80},{112,96},{128,112},... | collective-permute-start | bytes 589832 | tf_op jit(solution)/shard_map/ppermute | solution.py:346
  33.0 4.1 %collective-permute-start.1 = (f32[3,1,16,8,128]{4,3,2,1,0:T(8,128)S(1)}, f32[3,1,16,8,128]{4,3,2,1,0:T(8,128)S(1)}, u32[]{:S(2)}, u32[]{:S(2)}) collective-permute-start(f32[3,1,16,8,128]{4,3,2,1,0:T(8,128)S(1)} %get-tuple-element.20), channel_id=1, source_target_pairs={{0,16},{16,32},{32,48},{48,64},{64,80},{80,96},{96,112},{112,128},... | collective-permute-start | bytes 589832 | tf_op jit(solution)/shard_map/ppermute | solution.py:345
  37.1 15.6 %copy-start.3 = (f32[3,1,16,8,128]{4,3,2,1,0:T(8,128)}, f32[3,1,16,8,128]{4,3,2,1,0:T(8,128)S(1)}, u32[]{:S(2)}) copy-start(f32[3,1,16,8,128]{4,3,2,1,0:T(8,128)S(1)} %collective-permute-done.1.west_ref) | copy-start | bytes 589828
  52.7 3.4 %copy-start.4 = (f32[3,1,16,8,128]{4,3,2,1,0:T(8,128)S(1)}, f32[3,1,16,8,128]{4,3,2,1,0:T(8,128)}, u32[]{:S(2)}) copy-start(f32[3,1,16,8,128]{4,3,2,1,0:T(8,128)} %copy-done.3) | copy-start | bytes 589828
  53.7 17.4 %collective-permute-start.3 = (bf16[3072,128]{1,0:T(8,128)(2,1)S(1)}, bf16[3072,128]{1,0:T(8,128)(2,1)S(1)}, u32[]{:S(2)}, u32[]{:S(2)}) collective-permute-start(bf16[3072,128]{1,0:T(8,128)(2,1)S(1)} %shard_map.72.refs_0_), channel_id=1, source_target_pairs={{0,1},{1,2},{2,3},{3,0},{16,19},{17,16},{18,17},{19,18},{4,5},{5,6... | collective-permute-start | bytes 2359304 | tf_op jit(solution)/shard_map/ppermute | solution.py:324
  60.5 21.0 %collective-permute-start.6 = (bf16[3072,128]{1,0:T(8,128)(2,1)}, bf16[3072,128]{1,0:T(8,128)(2,1)}, u32[]{:S(2)}, u32[]{:S(2)}) collective-permute-start(bf16[3072,128]{1,0:T(8,128)(2,1)} %get-tuple-element.12.refs_4_), channel_id=1, source_target_pairs={{0,4},{4,8},{8,12},{12,0},{16,28},{20,16},{24,20},{28,24},{1,5},{5... | collective-permute-start | bytes 2359304 | tf_op jit(solution)/shard_map/ppermute | solution.py:324
  64.0 22.2 %collective-permute-start.4 = (bf16[3072,128]{1,0:T(8,128)(2,1)S(1)}, bf16[3072,128]{1,0:T(8,128)(2,1)S(1)}, u32[]{:S(2)}, u32[]{:S(2)}) collective-permute-start(bf16[3072,128]{1,0:T(8,128)(2,1)S(1)} %shard_map.72.refs_0_), channel_id=1, source_target_pairs={{1,0},{2,1},{3,2},{0,3},{19,16},{16,17},{17,18},{18,19},{5,4},{6,5... | collective-permute-start | bytes 2359304 | tf_op jit(solution)/shard_map/ppermute | solution.py:324
  67.4 21.6 %collective-permute-start.7 = (bf16[3072,128]{1,0:T(8,128)(2,1)}, bf16[3072,128]{1,0:T(8,128)(2,1)}, u32[]{:S(2)}, u32[]{:S(2)}) collective-permute-start(bf16[3072,128]{1,0:T(8,128)(2,1)} %get-tuple-element.12.refs_4_), channel_id=1, source_target_pairs={{4,0},{8,4},{12,8},{0,12},{28,16},{16,20},{20,24},{24,28},{5,1},{9... | collective-permute-start | bytes 2359304 | tf_op jit(solution)/shard_map/ppermute | solution.py:324
  71.0 18.0 %collective-permute-start.5 = (bf16[3072,128]{1,0:T(8,128)(2,1)S(1)}, bf16[3072,128]{1,0:T(8,128)(2,1)S(1)}, u32[]{:S(2)}, u32[]{:S(2)}) collective-permute-start(bf16[3072,128]{1,0:T(8,128)(2,1)S(1)} %collective-permute-done.3.refs_1_), channel_id=1, source_target_pairs={{0,1},{1,2},{2,3},{3,0},{16,19},{17,16},{18,17},{19,18},{4,5},{5,6... | collective-permute-start | bytes 2359304 | tf_op jit(solution)/shard_map/ppermute | solution.py:324
  81.4 16.4 %collective-permute-start.9 = (bf16[3072,128]{1,0:T(8,128)(2,1)}, bf16[3072,128]{1,0:T(8,128)(2,1)}, u32[]{:S(2)}, u32[]{:S(2)}) collective-permute-start(bf16[3072,128]{1,0:T(8,128)(2,1)} %collective-permute-done.6.refs_5_), channel_id=1, source_target_pairs={{0,4},{4,8},{8,12},{12,0},{16,28},{20,16},{24,20},{28,24},{1,5},{5... | collective-permute-start | bytes 2359304 | tf_op jit(solution)/shard_map/ppermute | solution.py:324
  92.1 10.7 %collective-permute-start.8 = (f32[4,3,64,128]{3,2,1,0:T(8,128)S(1)}, f32[4,3,64,128]{3,2,1,0:T(8,128)S(1)}, u32[]{:S(2)}, u32[]{:S(2)}) collective-permute-start(f32[4,3,64,128]{3,2,1,0:T(8,128)S(1)} %get-tuple-element.14), channel_id=1, source_target_pairs={{0,16},{16,0},{1,17},{17,1},{2,18},{18,2},{3,19},{19,3},{4,20},{20... | collective-permute-start | bytes 1179656 | tf_op jit(solution)/shard_map/ppermute | solution.py:416
  99.6 3.2 %collective-permute-start.10 = (f32[4,1,64,128]{3,2,1,0:T(8,128)S(1)}, f32[4,1,64,128]{3,2,1,0:T(8,128)S(1)}, u32[]{:S(2)}, u32[]{:S(2)}) collective-permute-start(f32[4,1,64,128]{3,2,1,0:T(8,128)S(1)} %get-tuple-element.16), channel_id=1, source_target_pairs={{0,16},{16,0},{1,17},{17,1},{2,18},{18,2},{3,19},{19,3},{4,20},{20... | collective-permute-start | bytes 393224 | tf_op jit(solution)/shard_map/ppermute | solution.py:418
  138.5 9.7 %collective-permute-start.11 = (f32[64,128]{1,0:T(8,128)S(1)}, f32[64,128]{1,0:T(8,128)S(1)}, u32[]{:S(2)}, u32[]{:S(2)}) collective-permute-start(f32[64,128]{1,0:T(8,128)S(1)} %shard_map.78), channel_id=1, source_target_pairs={{0,0},{1,32},{2,64},{3,96},{32,1},{33,33},{34,65},{35,97},{64,2},{... | collective-permute-start | bytes 98312 | tf_op jit(solution)/shard_map/ppermute | solution.py:336

commit v3 on v2

--- a/solution.py
+++ b/solution.py
@@ -106,49 +106,66 @@
         rounded_ref[at, :] = times(x_ref[at, :]).astype(BF16)
 
 
+def image_layer(x, x_ref, beside, coefficient_ref, out_ref):
+    cells_x, cells_y, cells_z = x_ref.shape[1:4]
+    values = [coefficient_ref[n] for n in range(15)]
+    for y in range(cells_y):
+        place = slice(x * cells_y + y, x * cells_y + y + 1)
+        cell = [jnp.broadcast_to(v[:, place], (8, 128)) for v in values]
+        east_c, west_c, north_c, south_c, upper_c, lower_c = cell[:6]
+        center = [x_ref[i, x, y] for i in range(3)]
+        for i in range(3):
+            image = east_c * beside(i, x + 1, y) + west_c * beside(i, x - 1, y)
+            if y + 1 < cells_y:
+                image = image + north_c * x_ref[i, x, y + 1]
+            if y > 0:
+                image = image + south_c * x_ref[i, x, y - 1]
+            image = image + upper_c * pltpu.roll(center[i], 7, 0)
+            image = image + lower_c * pltpu.roll(center[i], 1, 0)
+            for j in range(3):
+                image = image - cell[6 + 3 * i + j] * center[j]
+            first = ((i * cells_x + x) * cells_y + y) * cells_z
+            out_ref[first : first + cells_z, :] = image
+
+
+def inner_kernel(x_ref, coefficient_ref, raw_ref):
+    for x in range(1, x_ref.shape[1] - 1):
+        image_layer(x, x_ref, lambda i, x, y: x_ref[i, x, y], coefficient_ref, raw_ref)
+
+
 def image_kernel(
-    x_ref, west_ref, east_ref, coefficient_ref, inverse_ref,
-    advected_ref, rounded_ref, raw_ref, sems,
+    x_ref, west_ref, east_ref, coefficient_ref, inner_ref, inverse_ref,
+    advected_ref, rounded_ref, work_ref, sems,
 ):
     cells_x, cells_y, cells_z = x_ref.shape[1:4]
     layer = cells_y * cells_z
+
+    def beside(i, x, y):
+        if x < 0:
+            return west_ref[i, 0, y]
+        return x_ref[i, x, y] if x < cells_x else east_ref[i, 0, y]
+
     times = times_inverse(inverse_ref[...])
     sent = []
-    values = [coefficient_ref[n] for n in range(15)]
-    for x in range(cells_x):
-        for y in range(cells_y):
-            place = slice(x * cells_y + y, x * cells_y + y + 1)
-            cell = [jnp.broadcast_to(v[:, place], (8, 128)) for v in values]
-            east_c, west_c, north_c, south_c, upper_c, lower_c = cell[:6]
-            center = [x_ref[i, x, y] for i in range(3)]
-            for i in range(3):
-                east = x_ref[i, x + 1, y] if x + 1 < cells_x else east_ref[i, 0, y]
-                west = x_ref[i, x - 1, y] if x > 0 else west_ref[i, 0, y]
-                image = east_c * east + west_c * west
-                if y + 1 < cells_y:
-                    image = image + north_c * x_ref[i, x, y + 1]
-                if y > 0:
-                    image = image + south_c * x_ref[i, x, y - 1]
-                image = image + upper_c * pltpu.roll(center[i], 7, 0)
-                image = image + lower_c * pltpu.roll(center[i], 1, 0)
-                for j in range(3):
-                    image = image - cell[6 + 3 * i + j] * center[j]
-                first = ((i * cells_x + x) * cells_y + y) * cells_z
-                raw_ref[first : first + cells_z, :] = image
-
-        if x % 2 == 1:
-            for i in range(3):
-                first = (i * cells_x + x - 1) * layer
-                at = pl.ds(first, 2 * layer)
-                advected = times(raw_ref[at, :])
-                raw_ref[at, :] = advected
-                rounded_ref[at, :] = advected.astype(BF16)
-                sent.append(
-                    pltpu.make_async_copy(
-                        raw_ref.at[at, :], advected_ref.at[at, :], sems.at[len(sent)]
-                    )
-                )
-                sent[-1].start()
+
+    def finish(source_ref, x, layers):
+        for i in range(3):
+            at = pl.ds((i * cells_x + x) * layer, layers * layer)
+            advected = times(source_ref[at, :])
+            work_ref[at, :] = advected
+            rounded_ref[at, :] = advected.astype(BF16)
+            sent.append(
+                pltpu.make_async_copy(work_ref.at[at, :], advected_ref.at[at, :], sems.at[len(sent)])
+            )
+            sent[-1].start()
+
+    half = cells_x // 2
+    finish(inner_ref, 1, half - 1)
+    image_layer(0, x_ref, beside, coefficient_ref, work_ref)
+    finish(inner_ref, half, half - 1)
+    image_layer(cells_x - 1, x_ref, beside, coefficient_ref, work_ref)
+    finish(work_ref, 0, 1)
+    finish(work_ref, cells_x - 1, 1)
     for copy in sent:
         copy.wait()
 
@@ -165,8 +182,8 @@
         out_ref[n] = total
 
 
-def factor_kernel(weight, parts_ref, west_ref, east_ref, coefficient_ref, r_ref, inverse_ref):
-    del west_ref, east_ref, coefficient_ref
+def factor_kernel(weight, parts_ref, west_ref, east_ref, inner_ref, r_ref, inverse_ref):
+    del west_ref, east_ref, inner_ref
     packed = parts_ref[0] + parts_ref[1] + (parts_ref[2] + parts_ref[3])
     packed = packed * weight
     top = packed[:64]
@@ -354,6 +371,9 @@
         flops=200_000,
         moved=500_000,
     )(mean_flow.swapaxes(2, 3), flow_gradient.swapaxes(3, 4), viscosity.swapaxes(1, 2))
+    inner = kernel_call(
+        inner_kernel, jax.ShapeDtypeStruct((rows, width), F32), flops=25_000_000, moved=3_000_000
+    )(basis, coefficients)
     received = lax.ppermute(gram, "core", SWAP)
     mine = kernel_call(pair_kernel, packed4, moved=200_000)(gram, received)
     near = lax.all_to_all(mine, "zl", 0, 0, tiled=True)
@@ -371,7 +391,7 @@
         out_specs=[whole, whole],
         compiler_params=pltpu.CompilerParams(vmem_limit_bytes=VMEM_BYTES),
         cost_estimate=pl.CostEstimate(flops=10_000_000, bytes_accessed=400_000, transcendentals=0),
-    )(parts, west, east, coefficients)
+    )(parts, west, east, inner)
     rounded = pl.pallas_call(
         modes_kernel,
         out_shape=jax.ShapeDtypeStruct((rows, width), BF16),
@@ -389,11 +409,11 @@
             jax.ShapeDtypeStruct((rows, width), F32),
             jax.ShapeDtypeStruct((rows, width), BF16),
         ),
-        in_specs=[whole] * 5,
+        in_specs=[whole] * 6,
         out_specs=[anywhere, whole],
         scratch_shapes=[
             pltpu.VMEM((rows, width), F32),
-            pltpu.SemaphoreType.DMA((3 * (cells_x // 2),)),
+            pltpu.SemaphoreType.DMA((12,)),
         ],
         compiler_params=pltpu.CompilerParams(vmem_limit_bytes=VMEM_BYTES),
         cost_estimate=pl.CostEstimate(
@@ -404,6 +424,7 @@
         west,
         east,
         coefficients,
+        inner,
         inverse,
     )
     images = [rounded_image, pass_on(rounded_image, "y", AHEAD), pass_on(rounded_image, "y", BACK)]

time: 152 us -> 152 us (level)
  Pallas kernels: 18.1 us -> 20.5 us
  starting transfers between devices: 49.1 us -> 47.5 us
    pallas_call x0 -> x1, Pallas kernels: none -> 1.73 us  [body(): kernel_call(inner_kernel, jax.ShapeDtypeStruct((rows, width), F32), flops...]
    ppermute x6, starting transfers between devices: 20.5 us -> 18.9 us  [pass_on(): return lax.ppermute(block, ('core', axis), pairs)]
    pallas_call x1, Pallas kernels: 4.4 us -> 2.8 us  [body(): pl.pallas_call(image_kernel, out_shape=(jax.ShapeDtypeStruct((rows, width...]
  transfers between devices with their start and end apart: 13 -> 13, of which waited for: 9 -> 9; matrix products, arithmetic and copies ran while one was open for 0% -> 0% of each run, Pallas kernels for 6% -> 7%
where the time goes in v3:
time: 152 us; the launch traced here: 149 us
  starting transfers between devices  47.5 us (31%)
  blocking collectives  47.4 us (31%)
  waiting for transfers between devices  30.4 us (20%)
  Pallas kernels  20.5 us (13%)
  local copies, waits for them, and re-layouts  2.06 us (1%)
    ppermute x6, starting transfers between devices, pass_on(): return lax.ppermute(block, ('core', axis), pairs)  18.9 us
    all_to_all x1, blocking collectives, body(): near = lax.all_to_all(partial, 'zl', 0, 0, tiled=True)  17.5 us
    all_to_all x1, blocking collectives, body(): far = lax.all_to_all(near, 'zh', 0, 0, tiled=True)  17.4 us
    ppermute x6, waiting for transfers between devices, pass_on(): return lax.ppermute(block, ('core', axis), pairs)  15 us
    all_to_all x1, blocking collectives, body(): near = lax.all_to_all(mine, 'zl', 0, 0, tiled=True)  12.5 us
    all_to_all x1, starting transfers between devices, body(): parts = lax.all_to_all(near, 'zh', 0, 0, tiled=True)  12.4 us
    all_to_all x1, waiting for transfers between devices, body(): parts = lax.all_to_all(near, 'zh', 0, 0, tiled=True)  9.24 us
    pallas_call x1, Pallas kernels, body(): pl.pallas_call(functools.partial(factor_kernel, weight), out_shape=(jax.S...  6.41 us
  transfers between devices with their start and end apart: 13, of which 9 were waited for; matrix products, arithmetic and copies ran while one was open for 0% of the time, Pallas kernels for 7%

profile of v3, /device:TPU:6, one launch (start us, length us, event | category | flops | bytes accessed | tf_op | source)
XLA Modules:
  0.0 148.8 jit_solution(2172449133899429966)
XLA Ops:
  3.0 1.9 %collective-permute-start = (f32[72,128]{1,0:T(8,128)S(1)}, f32[72,128]{1,0:T(8,128)S(1)}, u32[]{:S(2)}, u32[]{:S(2)}) collective-permute-start(f32[72,128]{1,0:T(8,128)S(1)} %shard_map.67.a_ref), channel_id=1, source_target_pairs={{0,16},{16,0},{1,17},{17,1},{2,18},{18,2},{3,19},{19,3},{4,20},{20... | collective-permute-start | bytes 110600 | tf_op jit(solution)/shard_map/ppermute | solution.py:377
  6.1 12.5 %all_to_all.20.parts_ref = f32[4,72,128]{2,1,0:T(8,128)S(1)} all-to-all(f32[4,72,128]{2,1,0:T(8,128)S(1)} %shard_map.68), channel_id=1, replica_groups=mesh['zh'=4,'zl'=4,'core'=2,'y'=4,'x'=4] {'zl'}, dimensions={0} | all-to-all | bytes 294912 | tf_op jit(solution)/shard_map/all_to_all | solution.py:379
  19.3 12.4 %all-to-all-start.1 = ((f32[4,72,128]{2,1,0:T(8,128)}), f32[4,72,128]{2,1,0:T(8,128)}, u32[]{:S(2)}, u32[]{:S(2)}) async-start(f32[4,72,128]{2,1,0:T(8,128)} %shard_map.69), calls=%async_computation.1 | async-start | bytes 294912 | tf_op jit(solution)/shard_map/all_to_all | solution.py:381
  33.0 3.0 %collective-permute-start.1 = (f32[3,1,16,8,128]{4,3,2,1,0:T(8,128)S(1)}, f32[3,1,16,8,128]{4,3,2,1,0:T(8,128)S(1)}, u32[]{:S(2)}, u32[]{:S(2)}) collective-permute-start(f32[3,1,16,8,128]{4,3,2,1,0:T(8,128)S(1)} %get-tuple-element.20), channel_id=1, source_target_pairs={{0,16},{16,32},{32,48},{48,64},{64,80},{80,96},{96,112},{112,128},... | collective-permute-start | bytes 589832 | tf_op jit(solution)/shard_map/ppermute | solution.py:362
  38.0 9.2 %all-to-all-done.1.parts_ref = f32[4,72,128]{2,1,0:T(8,128)} async-done(((f32[4,72,128]{2,1,0:T(8,128)}), f32[4,72,128]{2,1,0:T(8,128)}, u32[]{:S(2)}, u32[]{:S(2)}) %all-to-all-start.1) | async-done | bytes 147488 | tf_op jit(solution)/shard_map/all_to_all | solution.py:381
  47.3 6.4 %shard_map.72 = (f32[128,128]{1,0:T(8,128)}, bf16[128,384]{1,0:T(8,128)(2,1)S(1)}) custom-call(f32[4,72,128]{2,1,0:T(8,128)} %all-to-all-done.1.parts_ref, f32[3,1,16,8,128]{4,3,2,1,0:T(8,128)S(1)} %collective-permute-done.1.west_ref, f32[3,1,16,8,128]{4,3,2,1,0:T(8,128)S(1)} %collective-permute-done.2.east_ref, f32[3072,128]{1,0:T(8,128)S(1)} %shard_map.71.inner_ref), custom_call_target="tpu_custom_call" | custom-call | flops 10000000 | bytes 400000 | tf_op jit(solution)/shard_map/pallas_call | solution.py:384
  55.5 2.4 %collective-permute-start.3 = (bf16[3072,128]{1,0:T(8,128)(2,1)}, bf16[3072,128]{1,0:T(8,128)(2,1)}, u32[]{:S(2)}, u32[]{:S(2)}) collective-permute-start(bf16[3072,128]{1,0:T(8,128)(2,1)} %shard_map.73.refs_0_), channel_id=1, source_target_pairs={{0,1},{1,2},{2,3},{3,0},{16,19},{17,16},{18,17},{19,18},{4,5},{5,6... | collective-permute-start | bytes 2359304 | tf_op jit(solution)/shard_map/ppermute | solution.py:341
  57.9 2.8 %shard_map.74 = (f32[3072,128]{1,0:T(8,128)}, bf16[3072,128]{1,0:T(8,128)(2,1)}) custom-call(f32[3,8,16,8,128]{4,3,2,1,0:T(8,128)S(1)} %copy-done.1, f32[3,1,16,8,128]{4,3,2,1,0:T(8,128)S(1)} %collective-permute-done.1.west_ref, f32[3,1,16,8,128]{4,3,2,1,0:T(8,128)S(1)} %collective-permute-done.2.east_ref, f32[15,8,128]{2,1,0:T(8,128)S(1)} %copy-done.3, ...), custom_call_target="tpu_custom_call" | custom-call | flops 600000000 | bytes 5000000 | tf_op jit(solution)/shard_map/pallas_call | solution.py:406
  60.7 3.5 %collective-permute-start.6 = (bf16[3072,128]{1,0:T(8,128)(2,1)}, bf16[3072,128]{1,0:T(8,128)(2,1)S(1)}, u32[]{:S(2)}, u32[]{:S(2)}) collective-permute-start(bf16[3072,128]{1,0:T(8,128)(2,1)} %get-tuple-element.12.refs_4_), channel_id=1, source_target_pairs={{0,4},{4,8},{8,12},{12,0},{16,28},{20,16},{24,20},{28,24},{1,5},{5... | collective-permute-start | bytes 2359304 | tf_op jit(solution)/shard_map/ppermute | solution.py:341
  64.2 3.5 %collective-permute-start.4 = (bf16[3072,128]{1,0:T(8,128)(2,1)}, bf16[3072,128]{1,0:T(8,128)(2,1)S(1)}, u32[]{:S(2)}, u32[]{:S(2)}) collective-permute-start(bf16[3072,128]{1,0:T(8,128)(2,1)} %shard_map.73.refs_0_), channel_id=1, source_target_pairs={{1,0},{2,1},{3,2},{0,3},{19,16},{16,17},{17,18},{18,19},{5,4},{6,5... | collective-permute-start | bytes 2359304 | tf_op jit(solution)/shard_map/ppermute | solution.py:341
  67.7 3.6 %collective-permute-start.7 = (bf16[3072,128]{1,0:T(8,128)(2,1)}, bf16[3072,128]{1,0:T(8,128)(2,1)}, u32[]{:S(2)}, u32[]{:S(2)}) collective-permute-start(bf16[3072,128]{1,0:T(8,128)(2,1)} %get-tuple-element.12.refs_4_), channel_id=1, source_target_pairs={{4,0},{8,4},{12,8},{0,12},{28,16},{16,20},{20,24},{24,28},{5,1},{9... | collective-permute-start | bytes 2359304 | tf_op jit(solution)/shard_map/ppermute | solution.py:341
  71.3 2.8 %collective-permute-done.3.refs_1_ = bf16[3072,128]{1,0:T(8,128)(2,1)} collective-permute-done((bf16[3072,128]{1,0:T(8,128)(2,1)}, bf16[3072,128]{1,0:T(8,128)(2,1)}, u32[]{:S(2)}, u32[]{:S(2)}) %collective-permute-start.3) | collective-permute-done | bytes 786464 | tf_op jit(solution)/shard_map/ppermute | solution.py:341
  76.0 5.6 %collective-permute-done.6.refs_5_ = bf16[3072,128]{1,0:T(8,128)(2,1)S(1)} collective-permute-done((bf16[3072,128]{1,0:T(8,128)(2,1)}, bf16[3072,128]{1,0:T(8,128)(2,1)S(1)}, u32[]{:S(2)}, u32[]{:S(2)}) %collective-permute-start.6) | collective-permute-done | bytes 786464 | tf_op jit(solution)/shard_map/ppermute | solution.py:341
  81.6 4.1 %collective-permute-start.9 = (bf16[3072,128]{1,0:T(8,128)(2,1)S(1)}, bf16[3072,128]{1,0:T(8,128)(2,1)S(1)}, u32[]{:S(2)}, u32[]{:S(2)}) collective-permute-start(bf16[3072,128]{1,0:T(8,128)(2,1)S(1)} %collective-permute-done.6.refs_5_), channel_id=1, source_target_pairs={{0,4},{4,8},{8,12},{12,0},{16,28},{20,16},{24,20},{28,24},{1,5},{5... | collective-permute-start | bytes 2359304 | tf_op jit(solution)/shard_map/ppermute | solution.py:341
  86.7 2.9 %collective-permute-done.7.refs_6_ = bf16[3072,128]{1,0:T(8,128)(2,1)} collective-permute-done((bf16[3072,128]{1,0:T(8,128)(2,1)}, bf16[3072,128]{1,0:T(8,128)(2,1)}, u32[]{:S(2)}, u32[]{:S(2)}) %collective-permute-start.7) | collective-permute-done | bytes 786464 | tf_op jit(solution)/shard_map/ppermute | solution.py:341
  89.5 3.3 %shard_map.75 = (f32[4,3,64,128]{3,2,1,0:T(8,128)S(1)}, f32[4,3,64,128]{3,2,1,0:T(8,128)S(1)}) custom-call(s32[3]{0:T(128)S(1)} %pad_add_fusion.place_ref, bf16[3072,128]{1,0:T(8,128)(2,1)} %shard_map.73.refs_0_, bf16[3072,128]{1,0:T(8,128)(2,1)} %collective-permute-done.3.refs_1_, bf16[3072,128]{1,0:T(8,128)(2,1)S(1)} %collective-permute-done.4.refs_2_, ...), custom_call_target="tpu_custom_call" | custom-call | flops 1200000000 | bytes 6000000 | tf_op jit(solution)/shard_map/pallas_call | solution.py:305
  92.9 1.9 %collective-permute-start.8 = (f32[4,3,64,128]{3,2,1,0:T(8,128)S(1)}, f32[4,3,64,128]{3,2,1,0:T(8,128)S(1)}, u32[]{:S(2)}, u32[]{:S(2)}) collective-permute-start(f32[4,3,64,128]{3,2,1,0:T(8,128)S(1)} %get-tuple-element.14), channel_id=1, source_target_pairs={{0,16},{16,0},{1,17},{17,1},{2,18},{18,2},{3,19},{19,3},{4,20},{20... | collective-permute-start | bytes 1179656 | tf_op jit(solution)/shard_map/ppermute | solution.py:437
  94.8 2.9 %collective-permute-done.9.refs_4_ = bf16[3072,128]{1,0:T(8,128)(2,1)S(1)} collective-permute-done((bf16[3072,128]{1,0:T(8,128)(2,1)S(1)}, bf16[3072,128]{1,0:T(8,128)(2,1)S(1)}, u32[]{:S(2)}, u32[]{:S(2)}) %collective-permute-start.9) | collective-permute-done | bytes 786464 | tf_op jit(solution)/shard_map/ppermute | solution.py:341
  97.7 2.0 %shard_map.76 = (f32[4,1,64,128]{3,2,1,0:T(8,128)S(1)}, f32[4,1,64,128]{3,2,1,0:T(8,128)S(1)}) custom-call(s32[3]{0:T(128)S(1)} %pad_add_fusion.place_ref, bf16[3072,128]{1,0:T(8,128)(2,1)} %shard_map.73.refs_0_, bf16[3072,128]{1,0:T(8,128)(2,1)} %collective-permute-done.3.refs_1_, bf16[3072,128]{1,0:T(8,128)(2,1)S(1)} %collective-permute-done.4.refs_2_, ...), custom_call_target="tpu_custom_call" | custom-call | flops 400000000 | bytes 6000000 | tf_op jit(solution)/shard_map/pallas_call | solution.py:305
  99.7 1.9 %collective-permute-start.10 = (f32[4,1,64,128]{3,2,1,0:T(8,128)S(1)}, f32[4,1,64,128]{3,2,1,0:T(8,128)S(1)}, u32[]{:S(2)}, u32[]{:S(2)}) collective-permute-start(f32[4,1,64,128]{3,2,1,0:T(8,128)S(1)} %get-tuple-element.16), channel_id=1, source_target_pairs={{0,16},{16,0},{1,17},{17,1},{2,18},{18,2},{3,19},{19,3},{4,20},{20... | collective-permute-start | bytes 393224 | tf_op jit(solution)/shard_map/ppermute | solution.py:439
  103.0 17.5 %all_to_all.21.parts_ref = f32[4,4,64,128]{3,2,1,0:T(8,128)S(1)} all-to-all(f32[4,4,64,128]{3,2,1,0:T(8,128)S(1)} %shard_map.77), channel_id=1, replica_groups=mesh['zh'=4,'zl'=4,'core'=2,'y'=4,'x'=4] {'zl'}, dimensions={0} | all-to-all | bytes 1048576 | tf_op jit(solution)/shard_map/all_to_all | solution.py:443
  121.0 17.4 %all_to_all.22.parts_ref = f32[4,64,128]{2,1,0:T(8,128)S(1)} all-to-all(f32[4,64,128]{2,1,0:T(8,128)S(1)} %shard_map.78), channel_id=1, replica_groups=mesh['zh'=4,'zl'=4,'core'=2,'y'=4,'x'=4] {'zh'}, dimensions={0} | all-to-all | bytes 262144 | tf_op jit(solution)/shard_map/all_to_all | solution.py:451
  138.4 6.1 %collective-permute-start.11 = (f32[64,128]{1,0:T(8,128)S(1)}, f32[64,128]{1,0:T(8,128)S(1)}, u32[]{:S(2)}, u32[]{:S(2)}) collective-permute-start(f32[64,128]{1,0:T(8,128)S(1)} %shard_map.79), channel_id=1, source_target_pairs={{0,0},{1,32},{2,64},{3,96},{32,1},{33,33},{34,65},{35,97},{64,2},{... | collective-permute-start | bytes 98312 | tf_op jit(solution)/shard_map/ppermute | solution.py:353
  144.6 3.6 %collective-permute-done.11 = f32[64,128]{1,0:T(8,128)S(1)} collective-permute-done((f32[64,128]{1,0:T(8,128)S(1)}, f32[64,128]{1,0:T(8,128)S(1)}, u32[]{:S(2)}, u32[]{:S(2)}) %collective-permute-start.11) | collective-permute-done | bytes 32800 | tf_op jit(solution)/shard_map/ppermute | solution.py:353
  (35 shorter events, 14.7 us)
Async XLA Ops:
  0.6 1.4 copy-start
  2.0 29.6 %copy-start.1 = (f32[3,8,16,8,128]{4,3,2,1,0:T(8,128)S(1)}, f32[3,8,16,8,128]{4,3,2,1,0:T(8,128)}, u32[]{:S(2)}) copy-start(f32[3,8,16,8,128]{4,3,2,1,0:T(8,128)} %x_ref.3) | copy-start | bytes 4718596
  2.0 34.0 %copy-start.4 = (f32[3,3,8,16,8]{3,4,2,1,0:T(8,128)S(1)}, f32[3,3,8,16,8]{3,4,2,1,0:T(8,128)}, u32[]{:S(2)}) copy-start(f32[3,3,8,16,8]{3,4,2,1,0:T(8,128)} %param.6) | copy-start | bytes 110596
  2.0 34.0 %copy-start.5 = (f32[3,8,16,8]{2,3,1,0:T(8,128)S(1)}, f32[3,8,16,8]{2,3,1,0:T(8,128)}, u32[]{:S(2)}) copy-start(f32[3,8,16,8]{2,3,1,0:T(8,128)} %param.5) | copy-start | bytes 36868
  2.0 34.0 %copy-start.6 = (f32[8,16,8]{1,2,0:T(8,128)S(1)}, f32[8,16,8]{1,2,0:T(8,128)}, u32[]{:S(2)}) copy-start(f32[8,16,8]{1,2,0:T(8,128)} %param.7) | copy-start | bytes 12292
  3.0 3.1 %collective-permute-start = (f32[72,128]{1,0:T(8,128)S(1)}, f32[72,128]{1,0:T(8,128)S(1)}, u32[]{:S(2)}, u32[]{:S(2)}) collective-permute-start(f32[72,128]{1,0:T(8,128)S(1)} %shard_map.67.a_ref), channel_id=1, source_target_pairs={{0,16},{16,0},{1,17},{17,1},{2,18},{18,2},{3,19},{19,3},{4,20},{20... | collective-permute-start | bytes 110600 | tf_op jit(solution)/shard_map/ppermute | solution.py:377
  19.3 28.0 %all-to-all-start.1 = ((f32[4,72,128]{2,1,0:T(8,128)}), f32[4,72,128]{2,1,0:T(8,128)}, u32[]{:S(2)}, u32[]{:S(2)}) async-start(f32[4,72,128]{2,1,0:T(8,128)} %shard_map.69), calls=%async_computation.1 | async-start | bytes 294912 | tf_op jit(solution)/shard_map/all_to_all | solution.py:381
  31.7 6.3 %collective-permute-start.2 = (f32[3,1,16,8,128]{4,3,2,1,0:T(8,128)S(1)}, f32[3,1,16,8,128]{4,3,2,1,0:T(8,128)S(1)}, u32[]{:S(2)}, u32[]{:S(2)}) collective-permute-start(f32[3,1,16,8,128]{4,3,2,1,0:T(8,128)S(1)} %get-tuple-element.19), channel_id=1, source_target_pairs={{16,0},{32,16},{48,32},{64,48},{80,64},{96,80},{112,96},{128,112},... | collective-permute-start | bytes 589832 | tf_op jit(solution)/shard_map/ppermute | solution.py:363
  33.0 5.0 %collective-permute-start.1 = (f32[3,1,16,8,128]{4,3,2,1,0:T(8,128)S(1)}, f32[3,1,16,8,128]{4,3,2,1,0:T(8,128)S(1)}, u32[]{:S(2)}, u32[]{:S(2)}) collective-permute-start(f32[3,1,16,8,128]{4,3,2,1,0:T(8,128)S(1)} %get-tuple-element.20), channel_id=1, source_target_pairs={{0,16},{16,32},{32,48},{48,64},{64,80},{80,96},{96,112},{112,128},... | collective-permute-start | bytes 589832 | tf_op jit(solution)/shard_map/ppermute | solution.py:362
  36.2 1.7 %copy-start.2 = (f32[15,8,128]{2,1,0:T(8,128)}, f32[15,8,128]{2,1,0:T(8,128)S(1)}, u32[]{:S(2)}) copy-start(f32[15,8,128]{2,1,0:T(8,128)S(1)} %shard_map.70.coefficient_ref) | copy-start | bytes 184324
  53.7 4.3 %copy-start.3 = (f32[15,8,128]{2,1,0:T(8,128)S(1)}, f32[15,8,128]{2,1,0:T(8,128)}, u32[]{:S(2)}) copy-start(f32[15,8,128]{2,1,0:T(8,128)} %copy-done.2) | copy-start | bytes 184324
  55.5 18.6 %collective-permute-start.3 = (bf16[3072,128]{1,0:T(8,128)(2,1)}, bf16[3072,128]{1,0:T(8,128)(2,1)}, u32[]{:S(2)}, u32[]{:S(2)}) collective-permute-start(bf16[3072,128]{1,0:T(8,128)(2,1)} %shard_map.73.refs_0_), channel_id=1, source_target_pairs={{0,1},{1,2},{2,3},{3,0},{16,19},{17,16},{18,17},{19,18},{4,5},{5,6... | collective-permute-start | bytes 2359304 | tf_op jit(solution)/shard_map/ppermute | solution.py:341
  60.7 20.9 %collective-permute-start.6 = (bf16[3072,128]{1,0:T(8,128)(2,1)}, bf16[3072,128]{1,0:T(8,128)(2,1)S(1)}, u32[]{:S(2)}, u32[]{:S(2)}) collective-permute-start(bf16[3072,128]{1,0:T(8,128)(2,1)} %get-tuple-element.12.refs_4_), channel_id=1, source_target_pairs={{0,4},{4,8},{8,12},{12,0},{16,28},{20,16},{24,20},{28,24},{1,5},{5... | collective-permute-start | bytes 2359304 | tf_op jit(solution)/shard_map/ppermute | solution.py:341
  64.2 22.4 %collective-permute-start.4 = (bf16[3072,128]{1,0:T(8,128)(2,1)}, bf16[3072,128]{1,0:T(8,128)(2,1)S(1)}, u32[]{:S(2)}, u32[]{:S(2)}) collective-permute-start(bf16[3072,128]{1,0:T(8,128)(2,1)} %shard_map.73.refs_0_), channel_id=1, source_target_pairs={{1,0},{2,1},{3,2},{0,3},{19,16},{16,17},{17,18},{18,19},{5,4},{6,5... | collective-permute-start | bytes 2359304 | tf_op jit(solution)/shard_map/ppermute | solution.py:341
  67.7 21.8 %collective-permute-start.7 = (bf16[3072,128]{1,0:T(8,128)(2,1)}, bf16[3072,128]{1,0:T(8,128)(2,1)}, u32[]{:S(2)}, u32[]{:S(2)}) collective-permute-start(bf16[3072,128]{1,0:T(8,128)(2,1)} %get-tuple-element.12.refs_4_), channel_id=1, source_target_pairs={{4,0},{8,4},{12,8},{0,12},{28,16},{16,20},{20,24},{24,28},{5,1},{9... | collective-permute-start | bytes 2359304 | tf_op jit(solution)/shard_map/ppermute | solution.py:341
  74.1 15.4 %collective-permute-start.5 = (bf16[3072,128]{1,0:T(8,128)(2,1)}, bf16[3072,128]{1,0:T(8,128)(2,1)S(1)}, u32[]{:S(2)}, u32[]{:S(2)}) collective-permute-start(bf16[3072,128]{1,0:T(8,128)(2,1)} %collective-permute-done.3.refs_1_), channel_id=1, source_target_pairs={{0,1},{1,2},{2,3},{3,0},{16,19},{17,16},{18,17},{19,18},{4,5},{5,6... | collective-permute-start | bytes 2359304 | tf_op jit(solution)/shard_map/ppermute | solution.py:341
  81.6 16.1 %collective-permute-start.9 = (bf16[3072,128]{1,0:T(8,128)(2,1)S(1)}, bf16[3072,128]{1,0:T(8,128)(2,1)S(1)}, u32[]{:S(2)}, u32[]{:S(2)}) collective-permute-start(bf16[3072,128]{1,0:T(8,128)(2,1)S(1)} %collective-permute-done.6.refs_5_), channel_id=1, source_target_pairs={{0,4},{4,8},{8,12},{12,0},{16,28},{20,16},{24,20},{28,24},{1,5},{5... | collective-permute-start | bytes 2359304 | tf_op jit(solution)/shard_map/ppermute | solution.py:341
  92.9 10.1 %collective-permute-start.8 = (f32[4,3,64,128]{3,2,1,0:T(8,128)S(1)}, f32[4,3,64,128]{3,2,1,0:T(8,128)S(1)}, u32[]{:S(2)}, u32[]{:S(2)}) collective-permute-start(f32[4,3,64,128]{3,2,1,0:T(8,128)S(1)} %get-tuple-element.14), channel_id=1, source_target_pairs={{0,16},{16,0},{1,17},{17,1},{2,18},{18,2},{3,19},{19,3},{4,20},{20... | collective-permute-start | bytes 1179656 | tf_op jit(solution)/shard_map/ppermute | solution.py:437
  99.7 3.2 %collective-permute-start.10 = (f32[4,1,64,128]{3,2,1,0:T(8,128)S(1)}, f32[4,1,64,128]{3,2,1,0:T(8,128)S(1)}, u32[]{:S(2)}, u32[]{:S(2)}) collective-permute-start(f32[4,1,64,128]{3,2,1,0:T(8,128)S(1)} %get-tuple-element.16), channel_id=1, source_target_pairs={{0,16},{16,0},{1,17},{17,1},{2,18},{18,2},{3,19},{19,3},{4,20},{20... | collective-permute-start | bytes 393224 | tf_op jit(solution)/shard_map/ppermute | solution.py:439
  138.4 9.7 %collective-permute-start.11 = (f32[64,128]{1,0:T(8,128)S(1)}, f32[64,128]{1,0:T(8,128)S(1)}, u32[]{:S(2)}, u32[]{:S(2)}) collective-permute-start(f32[64,128]{1,0:T(8,128)S(1)} %shard_map.79), channel_id=1, source_target_pairs={{0,0},{1,32},{2,64},{3,96},{32,1},{33,33},{34,65},{35,97},{64,2},{... | collective-permute-start | bytes 98312 | tf_op jit(solution)/shard_map/ppermute | solution.py:353

commit v4 on v3

--- a/solution.py
+++ b/solution.py
@@ -42,7 +42,9 @@
     return lax.dot_general(a, b, (((0,), (0,)), ((), ())), preferred_element_type=F32)
 
 
-def coefficient_kernel(flow_ref, gradient_ref, viscosity_ref, out_ref):
+def coefficient_kernel(place_ref, flow_ref, gradient_ref, viscosity_ref, out_ref):
+    del place_ref
+
     def wide(values):
         return jnp.concatenate([values[x] for x in range(values.shape[0])], axis=1)
 
@@ -106,7 +108,7 @@
         rounded_ref[at, :] = times(x_ref[at, :]).astype(BF16)
 
 
-def image_layer(x, x_ref, beside, coefficient_ref, out_ref):
+def image_layer(x, x_ref, beside, coefficient_ref, out_ref, skipped=0):
     cells_x, cells_y, cells_z = x_ref.shape[1:4]
     values = [coefficient_ref[n] for n in range(15)]
     for y in range(cells_y):
@@ -124,13 +126,14 @@
             image = image + lower_c * pltpu.roll(center[i], 1, 0)
             for j in range(3):
                 image = image - cell[6 + 3 * i + j] * center[j]
-            first = ((i * cells_x + x) * cells_y + y) * cells_z
+            layer = i * (cells_x - 2 * skipped) + x - skipped
+            first = (layer * cells_y + y) * cells_z
             out_ref[first : first + cells_z, :] = image
 
 
 def inner_kernel(x_ref, coefficient_ref, raw_ref):
     for x in range(1, x_ref.shape[1] - 1):
-        image_layer(x, x_ref, lambda i, x, y: x_ref[i, x, y], coefficient_ref, raw_ref)
+        image_layer(x, x_ref, lambda i, x, y: x_ref[i, x, y], coefficient_ref, raw_ref, 1)
 
 
 def image_kernel(
@@ -148,10 +151,11 @@
     times = times_inverse(inverse_ref[...])
     sent = []
 
-    def finish(source_ref, x, layers):
+    def finish(source_ref, x, layers, skipped=0):
         for i in range(3):
             at = pl.ds((i * cells_x + x) * layer, layers * layer)
-            advected = times(source_ref[at, :])
+            source = pl.ds((i * (cells_x - 2 * skipped) + x - skipped) * layer, layers * layer)
+            advected = times(source_ref[source, :])
             work_ref[at, :] = advected
             rounded_ref[at, :] = advected.astype(BF16)
             sent.append(
@@ -160,9 +164,9 @@
             sent[-1].start()
 
     half = cells_x // 2
-    finish(inner_ref, 1, half - 1)
+    finish(inner_ref, 1, half - 1, 1)
     image_layer(0, x_ref, beside, coefficient_ref, work_ref)
-    finish(inner_ref, half, half - 1)
+    finish(inner_ref, half, half - 1, 1)
     image_layer(cells_x - 1, x_ref, beside, coefficient_ref, work_ref)
     finish(work_ref, 0, 1)
     finish(work_ref, cells_x - 1, 1)
@@ -365,14 +369,20 @@
     packed = jax.ShapeDtypeStruct((72, 128), F32)
     packed4 = jax.ShapeDtypeStruct((4, 72, 128), F32)
     gram = kernel_call(gram_kernel, packed, flops=600_000_000, moved=1_600_000)(flat)
-    coefficients = kernel_call(
+    place = jnp.stack([lax.axis_index(axis) for axis in ("core", "x", "y")])
+    whole = pl.BlockSpec(memory_space=pltpu.VMEM)
+    scalars = pl.BlockSpec(memory_space=pltpu.SMEM)
+    coefficients = pl.pallas_call(
         coefficient_kernel,
-        jax.ShapeDtypeStruct((15, cells_z, cells_x * cells_y), F32),
-        flops=200_000,
-        moved=500_000,
-    )(mean_flow.swapaxes(2, 3), flow_gradient.swapaxes(3, 4), viscosity.swapaxes(1, 2))
+        out_shape=jax.ShapeDtypeStruct((15, cells_z, cells_x * cells_y), F32),
+        in_specs=[scalars, whole, whole, whole],
+        out_specs=whole,
+        compiler_params=pltpu.CompilerParams(vmem_limit_bytes=VMEM_BYTES),
+        cost_estimate=pl.CostEstimate(flops=200_000, bytes_accessed=500_000, transcendentals=0),
+    )(place, mean_flow.swapaxes(2, 3), flow_gradient.swapaxes(3, 4), viscosity.swapaxes(1, 2))
+    inner_rows = 3 * (cells_x - 2) * cells_y * cells_z
     inner = kernel_call(
-        inner_kernel, jax.ShapeDtypeStruct((rows, width), F32), flops=25_000_000, moved=3_000_000
+        inner_kernel, jax.ShapeDtypeStruct((inner_rows, width), F32), flops=25_000_000, moved=3_000_000
     )(basis, coefficients)
     received = lax.ppermute(gram, "core", SWAP)
     mine = kernel_call(pair_kernel, packed4, moved=200_000)(gram, received)
@@ -431,7 +441,6 @@
     modes.append(pass_on(modes[1], "x", AHEAD))
     last_image = pass_on(images[1], "y", AHEAD)
 
-    place = jnp.stack([lax.axis_index(axis) for axis in ("core", "x", "y")])
     turns = (0, 1, -1, 2)
     keep, send = product(place, modes, images, turns)
     received = lax.ppermute(send, "core", SWAP)

time: 152 us -> 149 us (0.980)
  Pallas kernels: 20.5 us -> 16.2 us
  blocking collectives: 47.4 us -> 49 us
    pallas_call x2, Pallas kernels: 5.32 us -> 3.17 us  [product(): pl.pallas_call(functools.partial(product_kernel, mode_turns), out_shape=(...]
    all_to_all x1, blocking collectives: 17.4 us -> 19 us  [body(): far = lax.all_to_all(near, 'zh', 0, 0, tiled=True)]
  transfers between devices with their start and end apart: 13 -> 13, of which waited for: 9 -> 10; matrix products, arithmetic and copies ran while one was open for 0% -> 1% of each run, Pallas kernels for 7% -> 5%
where the time goes in v4:
time: 149 us; the launch traced here: 147 us
  blocking collectives  49 us (33%)
  starting transfers between devices  47.4 us (32%)
  waiting for transfers between devices  30.3 us (20%)
  Pallas kernels  16.2 us (11%)
  local copies, waits for them, and re-layouts  2.73 us (2%)
    all_to_all x1, blocking collectives, body(): far = lax.all_to_all(near, 'zh', 0, 0, tiled=True)  19 us
    ppermute x6, starting transfers between devices, pass_on(): return lax.ppermute(block, ('core', axis), pairs)  18.8 us
    all_to_all x1, blocking collectives, body(): near = lax.all_to_all(partial, 'zl', 0, 0, tiled=True)  17.5 us
    ppermute x6, waiting for transfers between devices, pass_on(): return lax.ppermute(block, ('core', axis), pairs)  16.3 us
    all_to_all x1, blocking collectives, body(): near = lax.all_to_all(mine, 'zl', 0, 0, tiled=True)  12.5 us
    all_to_all x1, starting transfers between devices, body(): parts = lax.all_to_all(near, 'zh', 0, 0, tiled=True)  12.4 us
    all_to_all x1, waiting for transfers between devices, body(): parts = lax.all_to_all(near, 'zh', 0, 0, tiled=True)  7.89 us
    ppermute x1, starting transfers between devices, turn_over(): return lax.ppermute(block, ('zl', 'x'), pairs)  6.15 us
  transfers between devices with their start and end apart: 13, of which 10 were waited for; matrix products, arithmetic and copies ran while one was open for 1% of the time, Pallas kernels for 5%

profile of v4, /device:TPU:6, one launch (start us, length us, event | category | flops | bytes accessed | tf_op | source)
XLA Modules:
  0.0 146.6 jit_solution(17898791703229002979)
XLA Ops:
  3.0 1.9 %collective-permute-start = (f32[72,128]{1,0:T(8,128)S(1)}, f32[72,128]{1,0:T(8,128)S(1)}, u32[]{:S(2)}, u32[]{:S(2)}) collective-permute-start(f32[72,128]{1,0:T(8,128)S(1)} %shard_map.67.a_ref), channel_id=1, source_target_pairs={{0,16},{16,0},{1,17},{17,1},{2,18},{18,2},{3,19},{19,3},{4,20},{20... | collective-permute-start | bytes 110600 | tf_op jit(solution)/shard_map/ppermute | solution.py:387
  6.1 12.5 %all_to_all.20.parts_ref = f32[4,72,128]{2,1,0:T(8,128)S(1)} all-to-all(f32[4,72,128]{2,1,0:T(8,128)S(1)} %shard_map.68), channel_id=1, replica_groups=mesh['zh'=4,'zl'=4,'core'=2,'y'=4,'x'=4] {'zl'}, dimensions={0} | all-to-all | bytes 294912 | tf_op jit(solution)/shard_map/all_to_all | solution.py:389
  19.3 12.4 %all-to-all-start.1 = ((f32[4,72,128]{2,1,0:T(8,128)}), f32[4,72,128]{2,1,0:T(8,128)S(1)}, u32[]{:S(2)}, u32[]{:S(2)}) async-start(f32[4,72,128]{2,1,0:T(8,128)} %shard_map.69), calls=%async_computation.1 | async-start | bytes 294912 | tf_op jit(solution)/shard_map/all_to_all | solution.py:391
  33.6 3.0 %collective-permute-start.1 = (f32[3,1,16,8,128]{4,3,2,1,0:T(8,128)S(1)}, f32[3,1,16,8,128]{4,3,2,1,0:T(8,128)S(1)}, u32[]{:S(2)}, u32[]{:S(2)}) collective-permute-start(f32[3,1,16,8,128]{4,3,2,1,0:T(8,128)S(1)} %get-tuple-element.20), channel_id=1, source_target_pairs={{0,16},{16,32},{32,48},{48,64},{64,80},{80,96},{96,112},{112,128},... | collective-permute-start | bytes 589832 | tf_op jit(solution)/shard_map/ppermute | solution.py:366
  39.2 7.9 %all-to-all-done.1.parts_ref = f32[4,72,128]{2,1,0:T(8,128)S(1)} async-done(((f32[4,72,128]{2,1,0:T(8,128)}), f32[4,72,128]{2,1,0:T(8,128)S(1)}, u32[]{:S(2)}, u32[]{:S(2)}) %all-to-all-start.1) | async-done | bytes 147488 | tf_op jit(solution)/shard_map/all_to_all | solution.py:391
  47.1 5.5 %shard_map.72 = (f32[128,128]{1,0:T(8,128)}, bf16[128,384]{1,0:T(8,128)(2,1)S(1)}) custom-call(f32[4,72,128]{2,1,0:T(8,128)S(1)} %all-to-all-done.1.parts_ref, f32[3,1,16,8,128]{4,3,2,1,0:T(8,128)S(1)} %collective-permute-done.1.west_ref, f32[3,1,16,8,128]{4,3,2,1,0:T(8,128)S(1)} %collective-permute-done.2.east_ref, f32[2304,128]{1,0:T(8,128)S(1)} %shard_map.71.inner_ref), custom_call_target="tpu_custom_call" | custom-call | flops 10000000 | bytes 400000 | tf_op jit(solution)/shard_map/pallas_call | solution.py:394
  53.7 2.4 %collective-permute-start.3 = (bf16[3072,128]{1,0:T(8,128)(2,1)S(1)}, bf16[3072,128]{1,0:T(8,128)(2,1)S(1)}, u32[]{:S(2)}, u32[]{:S(2)}) collective-permute-start(bf16[3072,128]{1,0:T(8,128)(2,1)S(1)} %shard_map.73.refs_0_), channel_id=1, source_target_pairs={{0,1},{1,2},{2,3},{3,0},{16,19},{17,16},{18,17},{19,18},{4,5},{5,6... | collective-permute-start | bytes 2359304 | tf_op jit(solution)/shard_map/ppermute | solution.py:345
  56.0 1.9 %shard_map.74 = (f32[3072,128]{1,0:T(8,128)}, bf16[3072,128]{1,0:T(8,128)(2,1)S(1)}) custom-call(f32[3,8,16,8,128]{4,3,2,1,0:T(8,128)S(1)} %copy-done.1, f32[3,1,16,8,128]{4,3,2,1,0:T(8,128)S(1)} %collective-permute-done.1.west_ref, f32[3,1,16,8,128]{4,3,2,1,0:T(8,128)S(1)} %collective-permute-done.2.east_ref, f32[15,8,128]{2,1,0:T(8,128)S(1)} %shard_map.70.coefficient_ref, ...), custom_call_target="tpu_custom_call" | custom-call | flops 600000000 | bytes 5000000 | tf_op jit(solution)/shard_map/pallas_call | solution.py:416
  58.0 3.5 %collective-permute-start.6 = (bf16[3072,128]{1,0:T(8,128)(2,1)S(1)}, bf16[3072,128]{1,0:T(8,128)(2,1)S(1)}, u32[]{:S(2)}, u32[]{:S(2)}) collective-permute-start(bf16[3072,128]{1,0:T(8,128)(2,1)S(1)} %get-tuple-element.12.refs_4_), channel_id=1, source_target_pairs={{0,4},{4,8},{8,12},{12,0},{16,28},{20,16},{24,20},{28,24},{1,5},{5... | collective-permute-start | bytes 2359304 | tf_op jit(solution)/shard_map/ppermute | solution.py:345
  61.5 3.5 %collective-permute-start.4 = (bf16[3072,128]{1,0:T(8,128)(2,1)S(1)}, bf16[3072,128]{1,0:T(8,128)(2,1)S(1)}, u32[]{:S(2)}, u32[]{:S(2)}) collective-permute-start(bf16[3072,128]{1,0:T(8,128)(2,1)S(1)} %shard_map.73.refs_0_), channel_id=1, source_target_pairs={{1,0},{2,1},{3,2},{0,3},{19,16},{16,17},{17,18},{18,19},{5,4},{6,5... | collective-permute-start | bytes 2359304 | tf_op jit(solution)/shard_map/ppermute | solution.py:345
  64.9 3.6 %collective-permute-start.7 = (bf16[3072,128]{1,0:T(8,128)(2,1)S(1)}, bf16[3072,128]{1,0:T(8,128)(2,1)S(1)}, u32[]{:S(2)}, u32[]{:S(2)}) collective-permute-start(bf16[3072,128]{1,0:T(8,128)(2,1)S(1)} %get-tuple-element.12.refs_4_), channel_id=1, source_target_pairs={{4,0},{8,4},{12,8},{0,12},{28,16},{16,20},{20,24},{24,28},{5,1},{9... | collective-permute-start | bytes 2359304 | tf_op jit(solution)/shard_map/ppermute | solution.py:345
  68.5 4.3 %collective-permute-done.3.refs_1_ = bf16[3072,128]{1,0:T(8,128)(2,1)S(1)} collective-permute-done((bf16[3072,128]{1,0:T(8,128)(2,1)S(1)}, bf16[3072,128]{1,0:T(8,128)(2,1)S(1)}, u32[]{:S(2)}, u32[]{:S(2)}) %collective-permute-start.3) | collective-permute-done | bytes 786464 | tf_op jit(solution)/shard_map/ppermute | solution.py:345
  72.8 1.9 %collective-permute-start.5 = (bf16[3072,128]{1,0:T(8,128)(2,1)S(1)}, bf16[3072,128]{1,0:T(8,128)(2,1)S(1)}, u32[]{:S(2)}, u32[]{:S(2)}) collective-permute-start(bf16[3072,128]{1,0:T(8,128)(2,1)S(1)} %collective-permute-done.3.refs_1_), channel_id=1, source_target_pairs={{0,1},{1,2},{2,3},{3,0},{16,19},{17,16},{18,17},{19,18},{4,5},{5,6... | collective-permute-start | bytes 2359304 | tf_op jit(solution)/shard_map/ppermute | solution.py:345
  74.8 3.9 %collective-permute-done.6.refs_5_ = bf16[3072,128]{1,0:T(8,128)(2,1)S(1)} collective-permute-done((bf16[3072,128]{1,0:T(8,128)(2,1)S(1)}, bf16[3072,128]{1,0:T(8,128)(2,1)S(1)}, u32[]{:S(2)}, u32[]{:S(2)}) %collective-permute-start.6) | collective-permute-done | bytes 786464 | tf_op jit(solution)/shard_map/ppermute | solution.py:345
  78.6 4.0 %collective-permute-start.9 = (bf16[3072,128]{1,0:T(8,128)(2,1)S(1)}, bf16[3072,128]{1,0:T(8,128)(2,1)S(1)}, u32[]{:S(2)}, u32[]{:S(2)}) collective-permute-start(bf16[3072,128]{1,0:T(8,128)(2,1)S(1)} %collective-permute-done.6.refs_5_), channel_id=1, source_target_pairs={{0,4},{4,8},{8,12},{12,0},{16,28},{20,16},{24,20},{28,24},{1,5},{5... | collective-permute-start | bytes 2359304 | tf_op jit(solution)/shard_map/ppermute | solution.py:345
  83.7 2.9 %collective-permute-done.7.refs_6_ = bf16[3072,128]{1,0:T(8,128)(2,1)S(1)} collective-permute-done((bf16[3072,128]{1,0:T(8,128)(2,1)S(1)}, bf16[3072,128]{1,0:T(8,128)(2,1)S(1)}, u32[]{:S(2)}, u32[]{:S(2)}) %collective-permute-start.7) | collective-permute-done | bytes 786464 | tf_op jit(solution)/shard_map/ppermute | solution.py:345
  86.7 2.0 %shard_map.75 = (f32[4,3,64,128]{3,2,1,0:T(8,128)S(1)}, f32[4,3,64,128]{3,2,1,0:T(8,128)S(1)}) custom-call(s32[3]{0:T(128)S(1)} %pad_add_fusion.place_ref, bf16[3072,128]{1,0:T(8,128)(2,1)S(1)} %shard_map.73.refs_0_, bf16[3072,128]{1,0:T(8,128)(2,1)S(1)} %collective-permute-done.3.refs_1_, bf16[3072,128]{1,0:T(8,128)(2,1)S(1)} %collective-permute-done.4.refs_2_, ...), custom_call_target="tpu_custom_call" | custom-call | flops 1200000000 | bytes 6000000 | tf_op jit(solution)/shard_map/pallas_call | solution.py:309
  88.7 1.9 %collective-permute-start.8 = (f32[4,3,64,128]{3,2,1,0:T(8,128)S(1)}, f32[4,3,64,128]{3,2,1,0:T(8,128)S(1)}, u32[]{:S(2)}, u32[]{:S(2)}) collective-permute-start(f32[4,3,64,128]{3,2,1,0:T(8,128)S(1)} %get-tuple-element.14), channel_id=1, source_target_pairs={{0,16},{16,0},{1,17},{17,1},{2,18},{18,2},{3,19},{19,3},{4,20},{20... | collective-permute-start | bytes 1179656 | tf_op jit(solution)/shard_map/ppermute | solution.py:446
  90.6 4.0 %collective-permute-done.9.refs_4_ = bf16[3072,128]{1,0:T(8,128)(2,1)S(1)} collective-permute-done((bf16[3072,128]{1,0:T(8,128)(2,1)S(1)}, bf16[3072,128]{1,0:T(8,128)(2,1)S(1)}, u32[]{:S(2)}, u32[]{:S(2)}) %collective-permute-start.9) | collective-permute-done | bytes 786464 | tf_op jit(solution)/shard_map/ppermute | solution.py:345
  95.9 1.9 %collective-permute-start.10 = (f32[4,1,64,128]{3,2,1,0:T(8,128)S(1)}, f32[4,1,64,128]{3,2,1,0:T(8,128)S(1)}, u32[]{:S(2)}, u32[]{:S(2)}) collective-permute-start(f32[4,1,64,128]{3,2,1,0:T(8,128)S(1)} %get-tuple-element.16), channel_id=1, source_target_pairs={{0,16},{16,0},{1,17},{17,1},{2,18},{18,2},{3,19},{19,3},{4,20},{20... | collective-permute-start | bytes 393224 | tf_op jit(solution)/shard_map/ppermute | solution.py:448
  99.2 17.5 %all_to_all.21.parts_ref = f32[4,4,64,128]{3,2,1,0:T(8,128)S(1)} all-to-all(f32[4,4,64,128]{3,2,1,0:T(8,128)S(1)} %shard_map.77), channel_id=1, replica_groups=mesh['zh'=4,'zl'=4,'core'=2,'y'=4,'x'=4] {'zl'}, dimensions={0} | all-to-all | bytes 1048576 | tf_op jit(solution)/shard_map/all_to_all | solution.py:452
  117.2 19.0 %all_to_all.22.parts_ref = f32[4,64,128]{2,1,0:T(8,128)S(1)} all-to-all(f32[4,64,128]{2,1,0:T(8,128)S(1)} %shard_map.78), channel_id=1, replica_groups=mesh['zh'=4,'zl'=4,'core'=2,'y'=4,'x'=4] {'zh'}, dimensions={0} | all-to-all | bytes 262144 | tf_op jit(solution)/shard_map/all_to_all | solution.py:460
  136.2 6.1 %collective-permute-start.11 = (f32[64,128]{1,0:T(8,128)S(1)}, f32[64,128]{1,0:T(8,128)S(1)}, u32[]{:S(2)}, u32[]{:S(2)}) collective-permute-start(f32[64,128]{1,0:T(8,128)S(1)} %shard_map.79), channel_id=1, source_target_pairs={{0,0},{1,32},{2,64},{3,96},{32,1},{33,33},{34,65},{35,97},{64,2},{... | collective-permute-start | bytes 98312 | tf_op jit(solution)/shard_map/ppermute | solution.py:357
  142.4 3.6 %collective-permute-done.11 = f32[64,128]{1,0:T(8,128)S(1)} collective-permute-done((f32[64,128]{1,0:T(8,128)S(1)}, f32[64,128]{1,0:T(8,128)S(1)}, u32[]{:S(2)}, u32[]{:S(2)}) %collective-permute-start.11) | collective-permute-done | bytes 32800 | tf_op jit(solution)/shard_map/ppermute | solution.py:357
  (31 shorter events, 14.6 us)
Async XLA Ops:
  0.6 1.4 copy-start
  2.0 29.6 %copy-start.1 = (f32[3,8,16,8,128]{4,3,2,1,0:T(8,128)S(1)}, f32[3,8,16,8,128]{4,3,2,1,0:T(8,128)}, u32[]{:S(2)}) copy-start(f32[3,8,16,8,128]{4,3,2,1,0:T(8,128)} %x_ref.3) | copy-start | bytes 4718596
  2.0 34.7 %copy-start.2 = (f32[3,3,8,16,8]{3,4,2,1,0:T(8,128)S(1)}, f32[3,3,8,16,8]{3,4,2,1,0:T(8,128)}, u32[]{:S(2)}) copy-start(f32[3,3,8,16,8]{3,4,2,1,0:T(8,128)} %param.6) | copy-start | bytes 110596
  2.0 34.7 %copy-start.3 = (f32[3,8,16,8]{2,3,1,0:T(8,128)S(1)}, f32[3,8,16,8]{2,3,1,0:T(8,128)}, u32[]{:S(2)}) copy-start(f32[3,8,16,8]{2,3,1,0:T(8,128)} %param.5) | copy-start | bytes 36868
  2.0 34.7 %copy-start.4 = (f32[8,16,8]{1,2,0:T(8,128)S(1)}, f32[8,16,8]{1,2,0:T(8,128)}, u32[]{:S(2)}) copy-start(f32[8,16,8]{1,2,0:T(8,128)} %param.7) | copy-start | bytes 12292
  3.0 3.1 %collective-permute-start = (f32[72,128]{1,0:T(8,128)S(1)}, f32[72,128]{1,0:T(8,128)S(1)}, u32[]{:S(2)}, u32[]{:S(2)}) collective-permute-start(f32[72,128]{1,0:T(8,128)S(1)} %shard_map.67.a_ref), channel_id=1, source_target_pairs={{0,16},{16,0},{1,17},{17,1},{2,18},{18,2},{3,19},{19,3},{4,20},{20... | collective-permute-start | bytes 110600 | tf_op jit(solution)/shard_map/ppermute | solution.py:387
  19.3 27.9 %all-to-all-start.1 = ((f32[4,72,128]{2,1,0:T(8,128)}), f32[4,72,128]{2,1,0:T(8,128)S(1)}, u32[]{:S(2)}, u32[]{:S(2)}) async-start(f32[4,72,128]{2,1,0:T(8,128)} %shard_map.69), calls=%async_computation.1 | async-start | bytes 294912 | tf_op jit(solution)/shard_map/all_to_all | solution.py:391
  32.4 6.9 %collective-permute-start.2 = (f32[3,1,16,8,128]{4,3,2,1,0:T(8,128)}, f32[3,1,16,8,128]{4,3,2,1,0:T(8,128)S(1)}, u32[]{:S(2)}, u32[]{:S(2)}) collective-permute-start(f32[3,1,16,8,128]{4,3,2,1,0:T(8,128)} %get-tuple-element.19), channel_id=1, source_target_pairs={{16,0},{32,16},{48,32},{64,48},{80,64},{96,80},{112,96},{128,112},... | collective-permute-start | bytes 589832 | tf_op jit(solution)/shard_map/ppermute | solution.py:367
  33.6 5.6 %collective-permute-start.1 = (f32[3,1,16,8,128]{4,3,2,1,0:T(8,128)S(1)}, f32[3,1,16,8,128]{4,3,2,1,0:T(8,128)S(1)}, u32[]{:S(2)}, u32[]{:S(2)}) collective-permute-start(f32[3,1,16,8,128]{4,3,2,1,0:T(8,128)S(1)} %get-tuple-element.20), channel_id=1, source_target_pairs={{0,16},{16,32},{32,48},{48,64},{64,80},{80,96},{96,112},{112,128},... | collective-permute-start | bytes 589832 | tf_op jit(solution)/shard_map/ppermute | solution.py:366
  53.7 19.2 %collective-permute-start.3 = (bf16[3072,128]{1,0:T(8,128)(2,1)S(1)}, bf16[3072,128]{1,0:T(8,128)(2,1)S(1)}, u32[]{:S(2)}, u32[]{:S(2)}) collective-permute-start(bf16[3072,128]{1,0:T(8,128)(2,1)S(1)} %shard_map.73.refs_0_), channel_id=1, source_target_pairs={{0,1},{1,2},{2,3},{3,0},{16,19},{17,16},{18,17},{19,18},{4,5},{5,6... | collective-permute-start | bytes 2359304 | tf_op jit(solution)/shard_map/ppermute | solution.py:345
  58.0 20.7 %collective-permute-start.6 = (bf16[3072,128]{1,0:T(8,128)(2,1)S(1)}, bf16[3072,128]{1,0:T(8,128)(2,1)S(1)}, u32[]{:S(2)}, u32[]{:S(2)}) collective-permute-start(bf16[3072,128]{1,0:T(8,128)(2,1)S(1)} %get-tuple-element.12.refs_4_), channel_id=1, source_target_pairs={{0,4},{4,8},{8,12},{12,0},{16,28},{20,16},{24,20},{28,24},{1,5},{5... | collective-permute-start | bytes 2359304 | tf_op jit(solution)/shard_map/ppermute | solution.py:345
  61.5 22.2 %collective-permute-start.4 = (bf16[3072,128]{1,0:T(8,128)(2,1)S(1)}, bf16[3072,128]{1,0:T(8,128)(2,1)S(1)}, u32[]{:S(2)}, u32[]{:S(2)}) collective-permute-start(bf16[3072,128]{1,0:T(8,128)(2,1)S(1)} %shard_map.73.refs_0_), channel_id=1, source_target_pairs={{1,0},{2,1},{3,2},{0,3},{19,16},{16,17},{17,18},{18,19},{5,4},{6,5... | collective-permute-start | bytes 2359304 | tf_op jit(solution)/shard_map/ppermute | solution.py:345
  64.9 21.7 %collective-permute-start.7 = (bf16[3072,128]{1,0:T(8,128)(2,1)S(1)}, bf16[3072,128]{1,0:T(8,128)(2,1)S(1)}, u32[]{:S(2)}, u32[]{:S(2)}) collective-permute-start(bf16[3072,128]{1,0:T(8,128)(2,1)S(1)} %get-tuple-element.12.refs_4_), channel_id=1, source_target_pairs={{4,0},{8,4},{12,8},{0,12},{28,16},{16,20},{20,24},{24,28},{5,1},{9... | collective-permute-start | bytes 2359304 | tf_op jit(solution)/shard_map/ppermute | solution.py:345
  72.8 13.9 %collective-permute-start.5 = (bf16[3072,128]{1,0:T(8,128)(2,1)S(1)}, bf16[3072,128]{1,0:T(8,128)(2,1)S(1)}, u32[]{:S(2)}, u32[]{:S(2)}) collective-permute-start(bf16[3072,128]{1,0:T(8,128)(2,1)S(1)} %collective-permute-done.3.refs_1_), channel_id=1, source_target_pairs={{0,1},{1,2},{2,3},{3,0},{16,19},{17,16},{18,17},{19,18},{4,5},{5,6... | collective-permute-start | bytes 2359304 | tf_op jit(solution)/shard_map/ppermute | solution.py:345
  78.6 16.1 %collective-permute-start.9 = (bf16[3072,128]{1,0:T(8,128)(2,1)S(1)}, bf16[3072,128]{1,0:T(8,128)(2,1)S(1)}, u32[]{:S(2)}, u32[]{:S(2)}) collective-permute-start(bf16[3072,128]{1,0:T(8,128)(2,1)S(1)} %collective-permute-done.6.refs_5_), channel_id=1, source_target_pairs={{0,4},{4,8},{8,12},{12,0},{16,28},{20,16},{24,20},{28,24},{1,5},{5... | collective-permute-start | bytes 2359304 | tf_op jit(solution)/shard_map/ppermute | solution.py:345
  88.7 10.4 %collective-permute-start.8 = (f32[4,3,64,128]{3,2,1,0:T(8,128)S(1)}, f32[4,3,64,128]{3,2,1,0:T(8,128)S(1)}, u32[]{:S(2)}, u32[]{:S(2)}) collective-permute-start(f32[4,3,64,128]{3,2,1,0:T(8,128)S(1)} %get-tuple-element.14), channel_id=1, source_target_pairs={{0,16},{16,0},{1,17},{17,1},{2,18},{18,2},{3,19},{19,3},{4,20},{20... | collective-permute-start | bytes 1179656 | tf_op jit(solution)/shard_map/ppermute | solution.py:446
  95.9 3.2 %collective-permute-start.10 = (f32[4,1,64,128]{3,2,1,0:T(8,128)S(1)}, f32[4,1,64,128]{3,2,1,0:T(8,128)S(1)}, u32[]{:S(2)}, u32[]{:S(2)}) collective-permute-start(f32[4,1,64,128]{3,2,1,0:T(8,128)S(1)} %get-tuple-element.16), channel_id=1, source_target_pairs={{0,16},{16,0},{1,17},{17,1},{2,18},{18,2},{3,19},{19,3},{4,20},{20... | collective-permute-start | bytes 393224 | tf_op jit(solution)/shard_map/ppermute | solution.py:448
  136.2 9.7 %collective-permute-start.11 = (f32[64,128]{1,0:T(8,128)S(1)}, f32[64,128]{1,0:T(8,128)S(1)}, u32[]{:S(2)}, u32[]{:S(2)}) collective-permute-start(f32[64,128]{1,0:T(8,128)S(1)} %shard_map.79), channel_id=1, source_target_pairs={{0,0},{1,32},{2,64},{3,96},{32,1},{33,33},{34,65},{35,97},{64,2},{... | collective-permute-start | bytes 98312 | tf_op jit(solution)/shard_map/ppermute | solution.py:357

commit v5 on v4

--- a/solution.py
+++ b/solution.py
@@ -290,17 +290,18 @@
             total_ref[...] = product
         else:
             total_ref[...] += product
-    core, x = place_ref[0], place_ref[1]
+    core, x, zl = place_ref[0], place_ref[1], place_ref[3]
     ahead = 2 * core - 1
     for a, mode_turn in enumerate(mode_turns):
         panel_x = lax.rem(x + 4 + ahead * mode_turn, 4)
+        distance = lax.rem(panel_x + 4 - zl, 4)
         lanes = slice(128 * a, 128 * a + 128)
         for b in range(len(image_refs)):
             slot = b if b == 0 else b + core * (3 - 2 * b)
             mine = pl.ds(pl.multiple_of(128 * b + 64 * core, 64), 64)
             other = pl.ds(pl.multiple_of(128 * b + 64 * (1 - core), 64), 64)
-            keep_ref[panel_x, slot] = total_ref[mine, lanes]
-            send_ref[panel_x, slot] = total_ref[other, lanes]
+            keep_ref[distance, slot] = total_ref[mine, lanes]
+            send_ref[distance, slot] = total_ref[other, lanes]
 
 
 def product(place, modes, images, mode_turns):
@@ -319,17 +320,17 @@
     )(place, *modes, *images)
 
 
-def join_kernel(keep_ref, received_ref, keep_last_ref, received_last_ref, out_ref):
-    for n in range(4):
-        out_ref[n, :3] = keep_ref[n] + received_ref[n]
-        out_ref[n, 3] = keep_last_ref[n, 0] + received_last_ref[n, 0]
-
-
-def near_kernel(place_ref, parts_ref, out_ref):
+def join_kernel(keep_ref, received_ref, keep_last_ref, received_last_ref, *out_refs):
+    for n, out_ref in enumerate(out_refs):
+        out_ref[:3] = keep_ref[n] + received_ref[n]
+        out_ref[3] = keep_last_ref[n, 0] + received_last_ref[n, 0]
+
+
+def near_kernel(place_ref, a_ref, b_ref, c_ref, d_ref, out_ref):
     y = place_ref[2]
     for slot, turn in enumerate((0, -1, 1, 2)):
-        out_ref[lax.rem(y + 4 + turn, 4)] = (parts_ref[0, slot] + parts_ref[1, slot]) + (
-            parts_ref[2, slot] + parts_ref[3, slot]
+        out_ref[lax.rem(y + 4 + turn, 4)] = (a_ref[slot] + b_ref[slot]) + (
+            c_ref[slot] + d_ref[slot]
         )
 
 
@@ -369,7 +370,7 @@
     packed = jax.ShapeDtypeStruct((72, 128), F32)
     packed4 = jax.ShapeDtypeStruct((4, 72, 128), F32)
     gram = kernel_call(gram_kernel, packed, flops=600_000_000, moved=1_600_000)(flat)
-    place = jnp.stack([lax.axis_index(axis) for axis in ("core", "x", "y")])
+    place = jnp.stack([lax.axis_index(axis) for axis in ("core", "x", "y", "zl")])
     whole = pl.BlockSpec(memory_space=pltpu.VMEM)
     scalars = pl.BlockSpec(memory_space=pltpu.SMEM)
     coefficients = pl.pallas_call(
@@ -446,17 +447,20 @@
     received = lax.ppermute(send, "core", SWAP)
     keep_last, send_last = product(place, modes, [last_image], turns)
     received_last = lax.ppermute(send_last, "core", SWAP)
-    partial = kernel_call(
-        join_kernel, jax.ShapeDtypeStruct((4, 4, 64, 128), F32), moved=1_500_000
+    own, *others = kernel_call(
+        join_kernel, [jax.ShapeDtypeStruct((4, 64, 128), F32)] * 4, moved=1_500_000
     )(keep, received, keep_last, received_last)
-    near = lax.all_to_all(partial, "zl", 0, 0, tiled=True)
+    arrived = [
+        lax.ppermute(block, "zl", [(i, (i + n + 1) % 4) for i in range(4)])
+        for n, block in enumerate(others)
+    ]
     near = pl.pallas_call(
         near_kernel,
         out_shape=jax.ShapeDtypeStruct((4, 64, 128), F32),
-        in_specs=[pl.BlockSpec(memory_space=pltpu.SMEM), whole],
+        in_specs=[scalars] + [whole] * 4,
         out_specs=whole,
         compiler_params=pltpu.CompilerParams(vmem_limit_bytes=VMEM_BYTES),
-    )(place, near)
+    )(place, own, *arrived)
     far = lax.all_to_all(near, "zh", 0, 0, tiled=True)
     piece = kernel_call(
         functools.partial(far_kernel, weight), jax.ShapeDtypeStruct((64, 128), F32), moved=200_000

time: 149 us -> 148 us (level)
  blocking collectives: 49 us -> 31.6 us
  starting transfers between devices: 47.4 us -> 58.7 us
  waiting for transfers between devices: 30.3 us -> 35.1 us
    all_to_all x1 -> x0, blocking collectives: 17.5 us -> none  [body(): near = lax.all_to_all(partial, 'zl', 0, 0, tiled=True)]
    ppermute x0 -> x3, starting transfers between devices: none -> 9.56 us  [body(): lax.ppermute(block, 'zl', [(i, (i + n + 1) % 4) for i in range(4)])]
    ppermute x0 -> x3, waiting for transfers between devices: none -> 6.49 us  [body(): lax.ppermute(block, 'zl', [(i, (i + n + 1) % 4) for i in range(4)])]
    ppermute x1, starting transfers between devices: 6.15 us -> 7.86 us  [turn_over(): return lax.ppermute(block, ('zl', 'x'), pairs)]
    ppermute x1, waiting for transfers between devices: 3.56 us -> 1.88 us  [turn_over(): return lax.ppermute(block, ('zl', 'x'), pairs)]
  transfers between devices with their start and end apart: 13 -> 16, of which waited for: 10 -> 13; matrix products, arithmetic and copies ran while one was open for 1% -> 1% of each run, Pallas kernels for 5% -> 5%
where the time goes in v5:
time: 148 us; the launch traced here: 145 us
  starting transfers between devices  58.7 us (40%)
  waiting for transfers between devices  35.1 us (24%)
  blocking collectives  31.6 us (21%)
  Pallas kernels  16.3 us (11%)
  local copies, waits for them, and re-layouts  2.73 us (2%)
    all_to_all x1, blocking collectives, body(): far = lax.all_to_all(near, 'zh', 0, 0, tiled=True)  19.1 us
    ppermute x6, starting transfers between devices, pass_on(): return lax.ppermute(block, ('core', axis), pairs)  18.8 us
    ppermute x6, waiting for transfers between devices, pass_on(): return lax.ppermute(block, ('core', axis), pairs)  16.3 us
    all_to_all x1, blocking collectives, body(): near = lax.all_to_all(mine, 'zl', 0, 0, tiled=True)  12.5 us
    all_to_all x1, starting transfers between devices, body(): parts = lax.all_to_all(near, 'zh', 0, 0, tiled=True)  12.4 us
    ppermute x3, starting transfers between devices, body(): lax.ppermute(block, 'zl', [(i, (i + n + 1) % 4) for i in range(4)])  9.56 us
    all_to_all x1, waiting for transfers between devices, body(): parts = lax.all_to_all(near, 'zh', 0, 0, tiled=True)  7.89 us
    ppermute x1, starting transfers between devices, turn_over(): return lax.ppermute(block, ('zl', 'x'), pairs)  7.86 us
  transfers between devices with their start and end apart: 16, of which 13 were waited for; matrix products, arithmetic and copies ran while one was open for 1% of the time, Pallas kernels for 5%

profile of v5, /device:TPU:6, one launch (start us, length us, event | category | flops | bytes accessed | tf_op | source)
XLA Modules:
  0.0 145.3 jit_solution(16246205868328717680)
XLA Ops:
  3.0 1.9 %collective-permute-start = (f32[72,128]{1,0:T(8,128)S(1)}, f32[72,128]{1,0:T(8,128)S(1)}, u32[]{:S(2)}, u32[]{:S(2)}) collective-permute-start(f32[72,128]{1,0:T(8,128)S(1)} %shard_map.67.a_ref), channel_id=1, source_target_pairs={{0,16},{16,0},{1,17},{17,1},{2,18},{18,2},{3,19},{19,3},{4,20},{20... | collective-permute-start | bytes 110600 | tf_op jit(solution)/shard_map/ppermute | solution.py:388
  6.1 12.5 %all_to_all.15.parts_ref = f32[4,72,128]{2,1,0:T(8,128)S(1)} all-to-all(f32[4,72,128]{2,1,0:T(8,128)S(1)} %shard_map.68), channel_id=1, replica_groups=mesh['zh'=4,'zl'=4,'core'=2,'y'=4,'x'=4] {'zl'}, dimensions={0} | all-to-all | bytes 294912 | tf_op jit(solution)/shard_map/all_to_all | solution.py:390
  19.3 12.4 %all-to-all-start.1 = ((f32[4,72,128]{2,1,0:T(8,128)}), f32[4,72,128]{2,1,0:T(8,128)S(1)}, u32[]{:S(2)}, u32[]{:S(2)}) async-start(f32[4,72,128]{2,1,0:T(8,128)} %shard_map.69), calls=%async_computation.1 | async-start | bytes 294912 | tf_op jit(solution)/shard_map/all_to_all | solution.py:392
  33.7 3.0 %collective-permute-start.1 = (f32[3,1,16,8,128]{4,3,2,1,0:T(8,128)S(1)}, f32[3,1,16,8,128]{4,3,2,1,0:T(8,128)S(1)}, u32[]{:S(2)}, u32[]{:S(2)}) collective-permute-start(f32[3,1,16,8,128]{4,3,2,1,0:T(8,128)S(1)} %get-tuple-element.28), channel_id=1, source_target_pairs={{0,16},{16,32},{32,48},{48,64},{64,80},{80,96},{96,112},{112,128},... | collective-permute-start | bytes 589832 | tf_op jit(solution)/shard_map/ppermute | solution.py:367
  39.3 7.9 %all-to-all-done.1.parts_ref = f32[4,72,128]{2,1,0:T(8,128)S(1)} async-done(((f32[4,72,128]{2,1,0:T(8,128)}), f32[4,72,128]{2,1,0:T(8,128)S(1)}, u32[]{:S(2)}, u32[]{:S(2)}) %all-to-all-start.1) | async-done | bytes 147488 | tf_op jit(solution)/shard_map/all_to_all | solution.py:392
  47.2 5.5 %shard_map.72 = (f32[128,128]{1,0:T(8,128)}, bf16[128,384]{1,0:T(8,128)(2,1)S(1)}) custom-call(f32[4,72,128]{2,1,0:T(8,128)S(1)} %all-to-all-done.1.parts_ref, f32[3,1,16,8,128]{4,3,2,1,0:T(8,128)S(1)} %collective-permute-done.1.west_ref, f32[3,1,16,8,128]{4,3,2,1,0:T(8,128)S(1)} %collective-permute-done.2.east_ref, f32[2304,128]{1,0:T(8,128)S(1)} %shard_map.71.inner_ref), custom_call_target="tpu_custom_call" | custom-call | flops 10000000 | bytes 400000 | tf_op jit(solution)/shard_map/pallas_call | solution.py:395
  53.7 2.4 %collective-permute-start.3 = (bf16[3072,128]{1,0:T(8,128)(2,1)S(1)}, bf16[3072,128]{1,0:T(8,128)(2,1)S(1)}, u32[]{:S(2)}, u32[]{:S(2)}) collective-permute-start(bf16[3072,128]{1,0:T(8,128)(2,1)S(1)} %shard_map.73.refs_0_), channel_id=1, source_target_pairs={{0,1},{1,2},{2,3},{3,0},{16,19},{17,16},{18,17},{19,18},{4,5},{5,6... | collective-permute-start | bytes 2359304 | tf_op jit(solution)/shard_map/ppermute | solution.py:346
  58.0 3.5 %collective-permute-start.6 = (bf16[3072,128]{1,0:T(8,128)(2,1)S(1)}, bf16[3072,128]{1,0:T(8,128)(2,1)S(1)}, u32[]{:S(2)}, u32[]{:S(2)}) collective-permute-start(bf16[3072,128]{1,0:T(8,128)(2,1)S(1)} %get-tuple-element.16.refs_4_), channel_id=1, source_target_pairs={{0,4},{4,8},{8,12},{12,0},{16,28},{20,16},{24,20},{28,24},{1,5},{5... | collective-permute-start | bytes 2359304 | tf_op jit(solution)/shard_map/ppermute | solution.py:346
  61.5 3.5 %collective-permute-start.4 = (bf16[3072,128]{1,0:T(8,128)(2,1)S(1)}, bf16[3072,128]{1,0:T(8,128)(2,1)S(1)}, u32[]{:S(2)}, u32[]{:S(2)}) collective-permute-start(bf16[3072,128]{1,0:T(8,128)(2,1)S(1)} %shard_map.73.refs_0_), channel_id=1, source_target_pairs={{1,0},{2,1},{3,2},{0,3},{19,16},{16,17},{17,18},{18,19},{5,4},{6,5... | collective-permute-start | bytes 2359304 | tf_op jit(solution)/shard_map/ppermute | solution.py:346
  64.9 3.6 %collective-permute-start.7 = (bf16[3072,128]{1,0:T(8,128)(2,1)S(1)}, bf16[3072,128]{1,0:T(8,128)(2,1)S(1)}, u32[]{:S(2)}, u32[]{:S(2)}) collective-permute-start(bf16[3072,128]{1,0:T(8,128)(2,1)S(1)} %get-tuple-element.16.refs_4_), channel_id=1, source_target_pairs={{4,0},{8,4},{12,8},{0,12},{28,16},{16,20},{20,24},{24,28},{5,1},{9... | collective-permute-start | bytes 2359304 | tf_op jit(solution)/shard_map/ppermute | solution.py:346
  68.5 4.3 %collective-permute-done.3.refs_1_ = bf16[3072,128]{1,0:T(8,128)(2,1)S(1)} collective-permute-done((bf16[3072,128]{1,0:T(8,128)(2,1)S(1)}, bf16[3072,128]{1,0:T(8,128)(2,1)S(1)}, u32[]{:S(2)}, u32[]{:S(2)}) %collective-permute-start.3) | collective-permute-done | bytes 786464 | tf_op jit(solution)/shard_map/ppermute | solution.py:346
  74.8 3.9 %collective-permute-done.6.refs_5_ = bf16[3072,128]{1,0:T(8,128)(2,1)S(1)} collective-permute-done((bf16[3072,128]{1,0:T(8,128)(2,1)S(1)}, bf16[3072,128]{1,0:T(8,128)(2,1)S(1)}, u32[]{:S(2)}, u32[]{:S(2)}) %collective-permute-start.6) | collective-permute-done | bytes 786464 | tf_op jit(solution)/shard_map/ppermute | solution.py:346
  78.6 4.0 %collective-permute-start.9 = (bf16[3072,128]{1,0:T(8,128)(2,1)S(1)}, bf16[3072,128]{1,0:T(8,128)(2,1)S(1)}, u32[]{:S(2)}, u32[]{:S(2)}) collective-permute-start(bf16[3072,128]{1,0:T(8,128)(2,1)S(1)} %collective-permute-done.6.refs_5_), channel_id=1, source_target_pairs={{0,4},{4,8},{8,12},{12,0},{16,28},{20,16},{24,20},{28,24},{1,5},{5... | collective-permute-start | bytes 2359304 | tf_op jit(solution)/shard_map/ppermute | solution.py:346
  83.7 2.9 %collective-permute-done.7.refs_6_ = bf16[3072,128]{1,0:T(8,128)(2,1)S(1)} collective-permute-done((bf16[3072,128]{1,0:T(8,128)(2,1)S(1)}, bf16[3072,128]{1,0:T(8,128)(2,1)S(1)}, u32[]{:S(2)}, u32[]{:S(2)}) %collective-permute-start.7) | collective-permute-done | bytes 786464 | tf_op jit(solution)/shard_map/ppermute | solution.py:346
  86.7 2.0 %shard_map.75 = (f32[4,3,64,128]{3,2,1,0:T(8,128)S(1)}, f32[4,3,64,128]{3,2,1,0:T(8,128)S(1)}) custom-call(s32[4]{0:T(128)S(1)} %pad_add_fusion.place_ref, bf16[3072,128]{1,0:T(8,128)(2,1)S(1)} %shard_map.73.refs_0_, bf16[3072,128]{1,0:T(8,128)(2,1)S(1)} %collective-permute-done.3.refs_1_, bf16[3072,128]{1,0:T(8,128)(2,1)S(1)} %collective-permute-done.4.refs_2_, ...), custom_call_target="tpu_custom_call" | custom-call | flops 1200000000 | bytes 6000000 | tf_op jit(solution)/shard_map/pallas_call | solution.py:310
  88.7 1.9 %collective-permute-start.8 = (f32[4,3,64,128]{3,2,1,0:T(8,128)S(1)}, f32[4,3,64,128]{3,2,1,0:T(8,128)S(1)}, u32[]{:S(2)}, u32[]{:S(2)}) collective-permute-start(f32[4,3,64,128]{3,2,1,0:T(8,128)S(1)} %get-tuple-element.18), channel_id=1, source_target_pairs={{0,16},{16,0},{1,17},{17,1},{2,18},{18,2},{3,19},{19,3},{4,20},{20... | collective-permute-start | bytes 1179656 | tf_op jit(solution)/shard_map/ppermute | solution.py:447
  90.7 4.1 %collective-permute-done.9.refs_4_ = bf16[3072,128]{1,0:T(8,128)(2,1)S(1)} collective-permute-done((bf16[3072,128]{1,0:T(8,128)(2,1)S(1)}, bf16[3072,128]{1,0:T(8,128)(2,1)S(1)}, u32[]{:S(2)}, u32[]{:S(2)}) %collective-permute-start.9) | collective-permute-done | bytes 786464 | tf_op jit(solution)/shard_map/ppermute | solution.py:346
  95.9 1.9 %collective-permute-start.10 = (f32[4,1,64,128]{3,2,1,0:T(8,128)S(1)}, f32[4,1,64,128]{3,2,1,0:T(8,128)S(1)}, u32[]{:S(2)}, u32[]{:S(2)}) collective-permute-start(f32[4,1,64,128]{3,2,1,0:T(8,128)S(1)} %get-tuple-element.20), channel_id=1, source_target_pairs={{0,16},{16,0},{1,17},{17,1},{2,18},{18,2},{3,19},{19,3},{4,20},{20... | collective-permute-start | bytes 393224 | tf_op jit(solution)/shard_map/ppermute | solution.py:449
  99.2 1.9 %collective-permute-start.11 = (f32[4,64,128]{2,1,0:T(8,128)S(1)}, f32[4,64,128]{2,1,0:T(8,128)S(1)}, u32[]{:S(2)}, u32[]{:S(2)}) collective-permute-start(f32[4,64,128]{2,1,0:T(8,128)S(1)} %get-tuple-element.22), channel_id=1, source_target_pairs={{0,32},{32,64},{64,96},{96,0},{1,33},{33,65},{65,97},{97,1},{2,34}... | collective-permute-start | bytes 393224 | tf_op jit(solution)/shard_map/ppermute | solution.py:454
  101.1 2.0 %collective-permute-start.12 = (f32[4,64,128]{2,1,0:T(8,128)S(1)}, f32[4,64,128]{2,1,0:T(8,128)S(1)}, u32[]{:S(2)}, u32[]{:S(2)}) collective-permute-start(f32[4,64,128]{2,1,0:T(8,128)S(1)} %get-tuple-element.23), channel_id=1, source_target_pairs={{0,64},{32,96},{64,0},{96,32},{1,65},{33,97},{65,1},{97,33},{2,66}... | collective-permute-start | bytes 393224 | tf_op jit(solution)/shard_map/ppermute | solution.py:454
  103.2 5.6 %collective-permute-start.13 = (f32[4,64,128]{2,1,0:T(8,128)S(1)}, f32[4,64,128]{2,1,0:T(8,128)S(1)}, u32[]{:S(2)}, u32[]{:S(2)}) collective-permute-start(f32[4,64,128]{2,1,0:T(8,128)S(1)} %get-tuple-element.24), channel_id=1, source_target_pairs={{0,96},{32,0},{64,32},{96,64},{1,97},{33,1},{65,33},{97,65},{2,98}... | collective-permute-start | bytes 393224 | tf_op jit(solution)/shard_map/ppermute | solution.py:454
  109.3 4.8 %collective-permute-done.12.c_ref = f32[4,64,128]{2,1,0:T(8,128)S(1)} collective-permute-done((f32[4,64,128]{2,1,0:T(8,128)S(1)}, f32[4,64,128]{2,1,0:T(8,128)S(1)}, u32[]{:S(2)}, u32[]{:S(2)}) %collective-permute-start.12) | collective-permute-done | bytes 131104 | tf_op jit(solution)/shard_map/ppermute | solution.py:454
  115.9 19.1 %all_to_all.16.parts_ref = f32[4,64,128]{2,1,0:T(8,128)S(1)} all-to-all(f32[4,64,128]{2,1,0:T(8,128)S(1)} %shard_map.78), channel_id=1, replica_groups=mesh['zh'=4,'zl'=4,'core'=2,'y'=4,'x'=4] {'zh'}, dimensions={0} | all-to-all | bytes 262144 | tf_op jit(solution)/shard_map/all_to_all | solution.py:464
  134.9 7.9 %collective-permute-start.14 = (f32[64,128]{1,0:T(8,128)S(1)}, f32[64,128]{1,0:T(8,128)S(1)}, u32[]{:S(2)}, u32[]{:S(2)}) collective-permute-start(f32[64,128]{1,0:T(8,128)S(1)} %shard_map.79), channel_id=1, source_target_pairs={{0,0},{1,32},{2,64},{3,96},{32,1},{33,33},{34,65},{35,97},{64,2},{... | collective-permute-start | bytes 98312 | tf_op jit(solution)/shard_map/ppermute | solution.py:358
  (36 shorter events, 22.0 us)
Async XLA Ops:
  0.6 1.4 copy-start
  2.0 29.6 %copy-start.1 = (f32[3,8,16,8,128]{4,3,2,1,0:T(8,128)S(1)}, f32[3,8,16,8,128]{4,3,2,1,0:T(8,128)}, u32[]{:S(2)}) copy-start(f32[3,8,16,8,128]{4,3,2,1,0:T(8,128)} %x_ref.3) | copy-start | bytes 4718596
  2.0 34.8 %copy-start.2 = (f32[3,3,8,16,8]{3,4,2,1,0:T(8,128)S(1)}, f32[3,3,8,16,8]{3,4,2,1,0:T(8,128)}, u32[]{:S(2)}) copy-start(f32[3,3,8,16,8]{3,4,2,1,0:T(8,128)} %param.6) | copy-start | bytes 110596
  2.0 34.8 %copy-start.3 = (f32[3,8,16,8]{2,3,1,0:T(8,128)S(1)}, f32[3,8,16,8]{2,3,1,0:T(8,128)}, u32[]{:S(2)}) copy-start(f32[3,8,16,8]{2,3,1,0:T(8,128)} %param.5) | copy-start | bytes 36868
  2.0 34.8 %copy-start.4 = (f32[8,16,8]{1,2,0:T(8,128)S(1)}, f32[8,16,8]{1,2,0:T(8,128)}, u32[]{:S(2)}) copy-start(f32[8,16,8]{1,2,0:T(8,128)} %param.7) | copy-start | bytes 12292
  3.0 3.1 %collective-permute-start = (f32[72,128]{1,0:T(8,128)S(1)}, f32[72,128]{1,0:T(8,128)S(1)}, u32[]{:S(2)}, u32[]{:S(2)}) collective-permute-start(f32[72,128]{1,0:T(8,128)S(1)} %shard_map.67.a_ref), channel_id=1, source_target_pairs={{0,16},{16,0},{1,17},{17,1},{2,18},{18,2},{3,19},{19,3},{4,20},{20... | collective-permute-start | bytes 110600 | tf_op jit(solution)/shard_map/ppermute | solution.py:388
  19.3 27.9 %all-to-all-start.1 = ((f32[4,72,128]{2,1,0:T(8,128)}), f32[4,72,128]{2,1,0:T(8,128)S(1)}, u32[]{:S(2)}, u32[]{:S(2)}) async-start(f32[4,72,128]{2,1,0:T(8,128)} %shard_map.69), calls=%async_computation.1 | async-start | bytes 294912 | tf_op jit(solution)/shard_map/all_to_all | solution.py:392
  32.4 6.9 %collective-permute-start.2 = (f32[3,1,16,8,128]{4,3,2,1,0:T(8,128)}, f32[3,1,16,8,128]{4,3,2,1,0:T(8,128)S(1)}, u32[]{:S(2)}, u32[]{:S(2)}) collective-permute-start(f32[3,1,16,8,128]{4,3,2,1,0:T(8,128)} %get-tuple-element.27), channel_id=1, source_target_pairs={{16,0},{32,16},{48,32},{64,48},{80,64},{96,80},{112,96},{128,112},... | collective-permute-start | bytes 589832 | tf_op jit(solution)/shard_map/ppermute | solution.py:368
  33.7 5.6 %collective-permute-start.1 = (f32[3,1,16,8,128]{4,3,2,1,0:T(8,128)S(1)}, f32[3,1,16,8,128]{4,3,2,1,0:T(8,128)S(1)}, u32[]{:S(2)}, u32[]{:S(2)}) collective-permute-start(f32[3,1,16,8,128]{4,3,2,1,0:T(8,128)S(1)} %get-tuple-element.28), channel_id=1, source_target_pairs={{0,16},{16,32},{32,48},{48,64},{64,80},{80,96},{96,112},{112,128},... | collective-permute-start | bytes 589832 | tf_op jit(solution)/shard_map/ppermute | solution.py:367
  53.7 19.2 %collective-permute-start.3 = (bf16[3072,128]{1,0:T(8,128)(2,1)S(1)}, bf16[3072,128]{1,0:T(8,128)(2,1)S(1)}, u32[]{:S(2)}, u32[]{:S(2)}) collective-permute-start(bf16[3072,128]{1,0:T(8,128)(2,1)S(1)} %shard_map.73.refs_0_), channel_id=1, source_target_pairs={{0,1},{1,2},{2,3},{3,0},{16,19},{17,16},{18,17},{19,18},{4,5},{5,6... | collective-permute-start | bytes 2359304 | tf_op jit(solution)/shard_map/ppermute | solution.py:346
  58.0 20.7 %collective-permute-start.6 = (bf16[3072,128]{1,0:T(8,128)(2,1)S(1)}, bf16[3072,128]{1,0:T(8,128)(2,1)S(1)}, u32[]{:S(2)}, u32[]{:S(2)}) collective-permute-start(bf16[3072,128]{1,0:T(8,128)(2,1)S(1)} %get-tuple-element.16.refs_4_), channel_id=1, source_target_pairs={{0,4},{4,8},{8,12},{12,0},{16,28},{20,16},{24,20},{28,24},{1,5},{5... | collective-permute-start | bytes 2359304 | tf_op jit(solution)/shard_map/ppermute | solution.py:346
  61.5 22.3 %collective-permute-start.4 = (bf16[3072,128]{1,0:T(8,128)(2,1)S(1)}, bf16[3072,128]{1,0:T(8,128)(2,1)S(1)}, u32[]{:S(2)}, u32[]{:S(2)}) collective-permute-start(bf16[3072,128]{1,0:T(8,128)(2,1)S(1)} %shard_map.73.refs_0_), channel_id=1, source_target_pairs={{1,0},{2,1},{3,2},{0,3},{19,16},{16,17},{17,18},{18,19},{5,4},{6,5... | collective-permute-start | bytes 2359304 | tf_op jit(solution)/shard_map/ppermute | solution.py:346
  64.9 21.7 %collective-permute-start.7 = (bf16[3072,128]{1,0:T(8,128)(2,1)S(1)}, bf16[3072,128]{1,0:T(8,128)(2,1)S(1)}, u32[]{:S(2)}, u32[]{:S(2)}) collective-permute-start(bf16[3072,128]{1,0:T(8,128)(2,1)S(1)} %get-tuple-element.16.refs_4_), channel_id=1, source_target_pairs={{4,0},{8,4},{12,8},{0,12},{28,16},{16,20},{20,24},{24,28},{5,1},{9... | collective-permute-start | bytes 2359304 | tf_op jit(solution)/shard_map/ppermute | solution.py:346
  72.8 13.9 %collective-permute-start.5 = (bf16[3072,128]{1,0:T(8,128)(2,1)S(1)}, bf16[3072,128]{1,0:T(8,128)(2,1)S(1)}, u32[]{:S(2)}, u32[]{:S(2)}) collective-permute-start(bf16[3072,128]{1,0:T(8,128)(2,1)S(1)} %collective-permute-done.3.refs_1_), channel_id=1, source_target_pairs={{0,1},{1,2},{2,3},{3,0},{16,19},{17,16},{18,17},{19,18},{4,5},{5,6... | collective-permute-start | bytes 2359304 | tf_op jit(solution)/shard_map/ppermute | solution.py:346
  78.6 16.1 %collective-permute-start.9 = (bf16[3072,128]{1,0:T(8,128)(2,1)S(1)}, bf16[3072,128]{1,0:T(8,128)(2,1)S(1)}, u32[]{:S(2)}, u32[]{:S(2)}) collective-permute-start(bf16[3072,128]{1,0:T(8,128)(2,1)S(1)} %collective-permute-done.6.refs_5_), channel_id=1, source_target_pairs={{0,4},{4,8},{8,12},{12,0},{16,28},{20,16},{24,20},{28,24},{1,5},{5... | collective-permute-start | bytes 2359304 | tf_op jit(solution)/shard_map/ppermute | solution.py:346
  88.7 10.4 %collective-permute-start.8 = (f32[4,3,64,128]{3,2,1,0:T(8,128)S(1)}, f32[4,3,64,128]{3,2,1,0:T(8,128)S(1)}, u32[]{:S(2)}, u32[]{:S(2)}) collective-permute-start(f32[4,3,64,128]{3,2,1,0:T(8,128)S(1)} %get-tuple-element.18), channel_id=1, source_target_pairs={{0,16},{16,0},{1,17},{17,1},{2,18},{18,2},{3,19},{19,3},{4,20},{20... | collective-permute-start | bytes 1179656 | tf_op jit(solution)/shard_map/ppermute | solution.py:447
  95.9 3.2 %collective-permute-start.10 = (f32[4,1,64,128]{3,2,1,0:T(8,128)S(1)}, f32[4,1,64,128]{3,2,1,0:T(8,128)S(1)}, u32[]{:S(2)}, u32[]{:S(2)}) collective-permute-start(f32[4,1,64,128]{3,2,1,0:T(8,128)S(1)} %get-tuple-element.20), channel_id=1, source_target_pairs={{0,16},{16,0},{1,17},{17,1},{2,18},{18,2},{3,19},{19,3},{4,20},{20... | collective-permute-start | bytes 393224 | tf_op jit(solution)/shard_map/ppermute | solution.py:449
  99.2 10.1 %collective-permute-start.11 = (f32[4,64,128]{2,1,0:T(8,128)S(1)}, f32[4,64,128]{2,1,0:T(8,128)S(1)}, u32[]{:S(2)}, u32[]{:S(2)}) collective-permute-start(f32[4,64,128]{2,1,0:T(8,128)S(1)} %get-tuple-element.22), channel_id=1, source_target_pairs={{0,32},{32,64},{64,96},{96,0},{1,33},{33,65},{65,97},{97,1},{2,34}... | collective-permute-start | bytes 393224 | tf_op jit(solution)/shard_map/ppermute | solution.py:454
  101.1 13.0 %collective-permute-start.12 = (f32[4,64,128]{2,1,0:T(8,128)S(1)}, f32[4,64,128]{2,1,0:T(8,128)S(1)}, u32[]{:S(2)}, u32[]{:S(2)}) collective-permute-start(f32[4,64,128]{2,1,0:T(8,128)S(1)} %get-tuple-element.23), channel_id=1, source_target_pairs={{0,64},{32,96},{64,0},{96,32},{1,65},{33,97},{65,1},{97,33},{2,66}... | collective-permute-start | bytes 393224 | tf_op jit(solution)/shard_map/ppermute | solution.py:454
  103.2 12.1 %collective-permute-start.13 = (f32[4,64,128]{2,1,0:T(8,128)S(1)}, f32[4,64,128]{2,1,0:T(8,128)S(1)}, u32[]{:S(2)}, u32[]{:S(2)}) collective-permute-start(f32[4,64,128]{2,1,0:T(8,128)S(1)} %get-tuple-element.24), channel_id=1, source_target_pairs={{0,96},{32,0},{64,32},{96,64},{1,97},{33,1},{65,33},{97,65},{2,98}... | collective-permute-start | bytes 393224 | tf_op jit(solution)/shard_map/ppermute | solution.py:454
  134.9 9.8 %collective-permute-start.14 = (f32[64,128]{1,0:T(8,128)S(1)}, f32[64,128]{1,0:T(8,128)S(1)}, u32[]{:S(2)}, u32[]{:S(2)}) collective-permute-start(f32[64,128]{1,0:T(8,128)S(1)} %shard_map.79), channel_id=1, source_target_pairs={{0,0},{1,32},{2,64},{3,96},{32,1},{33,33},{34,65},{35,97},{64,2},{... | collective-permute-start | bytes 98312 | tf_op jit(solution)/shard_map/ppermute | solution.py:358

commit v6 on v5

--- a/solution.py
+++ b/solution.py
@@ -320,18 +320,39 @@
     )(place, *modes, *images)
 
 
-def join_kernel(keep_ref, received_ref, keep_last_ref, received_last_ref, *out_refs):
-    for n, out_ref in enumerate(out_refs):
+def ahead_kernel(keep_ref, received_ref, last_ref, out_ref):
+    del last_ref
+    out_ref[...] = keep_ref[2] + received_ref[2]
+
+
+def next_kernel(keep_ref, received_ref, keep_last_ref, received_last_ref, ahead_ref, next_ref):
+    del ahead_ref
+    next_ref[:3] = keep_ref[1] + received_ref[1]
+    next_ref[3] = keep_last_ref[1, 0] + received_last_ref[1, 0]
+
+
+def rest_kernel(
+    keep_ref, received_ref, keep_last_ref, received_last_ref, arrived_ref,
+    own_ref, back_ref, two_ref,
+):
+    del arrived_ref
+    for n, out_ref in ((0, own_ref), (3, back_ref)):
         out_ref[:3] = keep_ref[n] + received_ref[n]
         out_ref[3] = keep_last_ref[n, 0] + received_last_ref[n, 0]
-
-
-def near_kernel(place_ref, a_ref, b_ref, c_ref, d_ref, out_ref):
+    two_ref[...] = keep_last_ref[2] + received_last_ref[2]
+
+
+def near_kernel(place_ref, own_ref, next_ref, back_ref, first_ref, last_ref, out_ref):
     y = place_ref[2]
     for slot, turn in enumerate((0, -1, 1, 2)):
-        out_ref[lax.rem(y + 4 + turn, 4)] = (a_ref[slot] + b_ref[slot]) + (
-            c_ref[slot] + d_ref[slot]
+        two = first_ref[slot] if slot < 3 else last_ref[0]
+        out_ref[lax.rem(y + 4 + turn, 4)] = (own_ref[slot] + next_ref[slot]) + (
+            back_ref[slot] + two
         )
+
+
+def near_move(block, distance):
+    return lax.ppermute(block, "zl", [(i, (i + distance) % 4) for i in range(4)])
 
 
 def far_kernel(weight, parts_ref, out_ref):
@@ -447,20 +468,39 @@
     received = lax.ppermute(send, "core", SWAP)
     keep_last, send_last = product(place, modes, [last_image], turns)
     received_last = lax.ppermute(send_last, "core", SWAP)
-    own, *others = kernel_call(
-        join_kernel, [jax.ShapeDtypeStruct((4, 64, 128), F32)] * 4, moved=1_500_000
-    )(keep, received, keep_last, received_last)
-    arrived = [
-        lax.ppermute(block, "zl", [(i, (i + n + 1) % 4) for i in range(4)])
-        for n, block in enumerate(others)
-    ]
+    two_first = pl.pallas_call(
+        ahead_kernel,
+        out_shape=jax.ShapeDtypeStruct((3, 64, 128), F32),
+        in_specs=[whole, whole, anywhere],
+        out_specs=whole,
+        compiler_params=pltpu.CompilerParams(vmem_limit_bytes=VMEM_BYTES),
+        cost_estimate=pl.CostEstimate(flops=30_000, bytes_accessed=300_000, transcendentals=0),
+    )(keep, received, send_last)
+    sums = (keep, received, keep_last, received_last)
+    full = jax.ShapeDtypeStruct((4, 64, 128), F32)
+    one = pl.pallas_call(
+        next_kernel,
+        out_shape=full,
+        in_specs=[whole] * 4 + [anywhere],
+        out_specs=whole,
+        compiler_params=pltpu.CompilerParams(vmem_limit_bytes=VMEM_BYTES),
+    )(*sums, two_first)
+    one = near_move(one, 1)
+    two_first = near_move(two_first, 2)
+    own, back, two_last = pl.pallas_call(
+        rest_kernel,
+        out_shape=[full, full, jax.ShapeDtypeStruct((1, 64, 128), F32)],
+        in_specs=[whole] * 4 + [anywhere],
+        out_specs=[whole] * 3,
+        compiler_params=pltpu.CompilerParams(vmem_limit_bytes=VMEM_BYTES),
+    )(*sums, two_first)
     near = pl.pallas_call(
         near_kernel,
         out_shape=jax.ShapeDtypeStruct((4, 64, 128), F32),
-        in_specs=[scalars] + [whole] * 4,
+        in_specs=[scalars] + [whole] * 5,
         out_specs=whole,
         compiler_params=pltpu.CompilerParams(vmem_limit_bytes=VMEM_BYTES),
-    )(place, own, *arrived)
+    )(place, own, one, near_move(back, 3), two_first, near_move(two_last, 2))
     far = lax.all_to_all(near, "zh", 0, 0, tiled=True)
     piece = kernel_call(
         functools.partial(far_kernel, weight), jax.ShapeDtypeStruct((64, 128), F32), moved=200_000

time: 148 us -> 148 us (level)
  waiting for transfers between devices: 35.1 us -> 37.5 us
  blocking collectives: 31.6 us -> 30 us
  starting transfers between devices: 58.7 us -> 57.2 us
    ppermute x3 -> x4, waiting for transfers between devices: 6.49 us -> 8.77 us  [near_move(): lax.ppermute(block, 'zl', [(i, (i + distance) % 4) for i in range(4)])]
    all_to_all x1, blocking collectives: 19.1 us -> 17.5 us  [body(): far = lax.all_to_all(near, 'zh', 0, 0, tiled=True)]
    ppermute x3 -> x4, starting transfers between devices: 9.56 us -> 9.6 us  [near_move(): lax.ppermute(block, 'zl', [(i, (i + distance) % 4) for i in range(4)])]
  transfers between devices with their start and end apart: 16 -> 17, of which waited for: 13 -> 11; matrix products, arithmetic and copies ran while one was open for 1% -> 1% of each run, Pallas kernels for 5% -> 5%
where the time goes in v6:
time: 148 us; the launch traced here: 145 us
  starting transfers between devices  57.2 us (39%)
  waiting for transfers between devices  37.5 us (25%)
  blocking collectives  30 us (20%)
  Pallas kernels  16.3 us (11%)
  local copies, waits for them, and re-layouts  2.73 us (2%)
    ppermute x6, starting transfers between devices, pass_on(): return lax.ppermute(block, ('core', axis), pairs)  18.8 us
    all_to_all x1, blocking collectives, body(): far = lax.all_to_all(near, 'zh', 0, 0, tiled=True)  17.5 us
    ppermute x6, waiting for transfers between devices, pass_on(): return lax.ppermute(block, ('core', axis), pairs)  16.4 us
    all_to_all x1, blocking collectives, body(): near = lax.all_to_all(mine, 'zl', 0, 0, tiled=True)  12.5 us
    all_to_all x1, starting transfers between devices, body(): parts = lax.all_to_all(near, 'zh', 0, 0, tiled=True)  12.4 us
    ppermute x4, starting transfers between devices, near_move(): lax.ppermute(block, 'zl', [(i, (i + distance) % 4) for i in range(4)])  9.6 us
    ppermute x4, waiting for transfers between devices, near_move(): lax.ppermute(block, 'zl', [(i, (i + distance) % 4) for i in range(4)])  8.77 us
    all_to_all x1, waiting for transfers between devices, body(): parts = lax.all_to_all(near, 'zh', 0, 0, tiled=True)  7.89 us
  transfers between devices with their start and end apart: 17, of which 11 were waited for; matrix products, arithmetic and copies ran while one was open for 1% of the time, Pallas kernels for 5%

profile of v6, /device:TPU:6, one launch (start us, length us, event | category | flops | bytes accessed | tf_op | source)
XLA Modules:
  0.0 144.8 jit_solution(13192431677654307452)
XLA Ops:
  3.0 1.9 %collective-permute-start = (f32[72,128]{1,0:T(8,128)S(1)}, f32[72,128]{1,0:T(8,128)S(1)}, u32[]{:S(2)}, u32[]{:S(2)}) collective-permute-start(f32[72,128]{1,0:T(8,128)S(1)} %shard_map.67.a_ref), channel_id=1, source_target_pairs={{0,16},{16,0},{1,17},{17,1},{2,18},{18,2},{3,19},{19,3},{4,20},{20... | collective-permute-start | bytes 110600 | tf_op jit(solution)/shard_map/ppermute | solution.py:409
  6.1 12.5 %all_to_all.15.parts_ref = f32[4,72,128]{2,1,0:T(8,128)S(1)} all-to-all(f32[4,72,128]{2,1,0:T(8,128)S(1)} %shard_map.68), channel_id=1, replica_groups=mesh['zh'=4,'zl'=4,'core'=2,'y'=4,'x'=4] {'zl'}, dimensions={0} | all-to-all | bytes 294912 | tf_op jit(solution)/shard_map/all_to_all | solution.py:411
  19.3 12.4 %all-to-all-start.1 = ((f32[4,72,128]{2,1,0:T(8,128)}), f32[4,72,128]{2,1,0:T(8,128)S(1)}, u32[]{:S(2)}, u32[]{:S(2)}) async-start(f32[4,72,128]{2,1,0:T(8,128)} %shard_map.69), calls=%async_computation.1 | async-start | bytes 294912 | tf_op jit(solution)/shard_map/all_to_all | solution.py:413
  33.7 3.0 %collective-permute-start.1 = (f32[3,1,16,8,128]{4,3,2,1,0:T(8,128)S(1)}, f32[3,1,16,8,128]{4,3,2,1,0:T(8,128)S(1)}, u32[]{:S(2)}, u32[]{:S(2)}) collective-permute-start(f32[3,1,16,8,128]{4,3,2,1,0:T(8,128)S(1)} %get-tuple-element.26), channel_id=1, source_target_pairs={{0,16},{16,32},{32,48},{48,64},{64,80},{80,96},{96,112},{112,128},... | collective-permute-start | bytes 589832 | tf_op jit(solution)/shard_map/ppermute | solution.py:388
  39.3 7.9 %all-to-all-done.1.parts_ref = f32[4,72,128]{2,1,0:T(8,128)S(1)} async-done(((f32[4,72,128]{2,1,0:T(8,128)}), f32[4,72,128]{2,1,0:T(8,128)S(1)}, u32[]{:S(2)}, u32[]{:S(2)}) %all-to-all-start.1) | async-done | bytes 147488 | tf_op jit(solution)/shard_map/all_to_all | solution.py:413
  47.2 5.5 %shard_map.72 = (f32[128,128]{1,0:T(8,128)}, bf16[128,384]{1,0:T(8,128)(2,1)S(1)}) custom-call(f32[4,72,128]{2,1,0:T(8,128)S(1)} %all-to-all-done.1.parts_ref, f32[3,1,16,8,128]{4,3,2,1,0:T(8,128)S(1)} %collective-permute-done.1.west_ref, f32[3,1,16,8,128]{4,3,2,1,0:T(8,128)S(1)} %collective-permute-done.2.east_ref, f32[2304,128]{1,0:T(8,128)S(1)} %shard_map.71.inner_ref), custom_call_target="tpu_custom_call" | custom-call | flops 10000000 | bytes 400000 | tf_op jit(solution)/shard_map/pallas_call | solution.py:416
  53.7 2.4 %collective-permute-start.3 = (bf16[3072,128]{1,0:T(8,128)(2,1)S(1)}, bf16[3072,128]{1,0:T(8,128)(2,1)S(1)}, u32[]{:S(2)}, u32[]{:S(2)}) collective-permute-start(bf16[3072,128]{1,0:T(8,128)(2,1)S(1)} %shard_map.73.refs_0_), channel_id=1, source_target_pairs={{0,1},{1,2},{2,3},{3,0},{16,19},{17,16},{18,17},{19,18},{4,5},{5,6... | collective-permute-start | bytes 2359304 | tf_op jit(solution)/shard_map/ppermute | solution.py:367
  58.0 3.5 %collective-permute-start.6 = (bf16[3072,128]{1,0:T(8,128)(2,1)S(1)}, bf16[3072,128]{1,0:T(8,128)(2,1)S(1)}, u32[]{:S(2)}, u32[]{:S(2)}) collective-permute-start(bf16[3072,128]{1,0:T(8,128)(2,1)S(1)} %get-tuple-element.15.refs_4_), channel_id=1, source_target_pairs={{0,4},{4,8},{8,12},{12,0},{16,28},{20,16},{24,20},{28,24},{1,5},{5... | collective-permute-start | bytes 2359304 | tf_op jit(solution)/shard_map/ppermute | solution.py:367
  61.5 3.5 %collective-permute-start.4 = (bf16[3072,128]{1,0:T(8,128)(2,1)S(1)}, bf16[3072,128]{1,0:T(8,128)(2,1)S(1)}, u32[]{:S(2)}, u32[]{:S(2)}) collective-permute-start(bf16[3072,128]{1,0:T(8,128)(2,1)S(1)} %shard_map.73.refs_0_), channel_id=1, source_target_pairs={{1,0},{2,1},{3,2},{0,3},{19,16},{16,17},{17,18},{18,19},{5,4},{6,5... | collective-permute-start | bytes 2359304 | tf_op jit(solution)/shard_map/ppermute | solution.py:367
  64.9 3.6 %collective-permute-start.7 = (bf16[3072,128]{1,0:T(8,128)(2,1)S(1)}, bf16[3072,128]{1,0:T(8,128)(2,1)S(1)}, u32[]{:S(2)}, u32[]{:S(2)}) collective-permute-start(bf16[3072,128]{1,0:T(8,128)(2,1)S(1)} %get-tuple-element.15.refs_4_), channel_id=1, source_target_pairs={{4,0},{8,4},{12,8},{0,12},{28,16},{16,20},{20,24},{24,28},{5,1},{9... | collective-permute-start | bytes 2359304 | tf_op jit(solution)/shard_map/ppermute | solution.py:367
  68.5 4.3 %collective-permute-done.3.refs_1_ = bf16[3072,128]{1,0:T(8,128)(2,1)S(1)} collective-permute-done((bf16[3072,128]{1,0:T(8,128)(2,1)S(1)}, bf16[3072,128]{1,0:T(8,128)(2,1)S(1)}, u32[]{:S(2)}, u32[]{:S(2)}) %collective-permute-start.3) | collective-permute-done | bytes 786464 | tf_op jit(solution)/shard_map/ppermute | solution.py:367
  74.8 3.9 %collective-permute-done.6.refs_5_ = bf16[3072,128]{1,0:T(8,128)(2,1)S(1)} collective-permute-done((bf16[3072,128]{1,0:T(8,128)(2,1)S(1)}, bf16[3072,128]{1,0:T(8,128)(2,1)S(1)}, u32[]{:S(2)}, u32[]{:S(2)}) %collective-permute-start.6) | collective-permute-done | bytes 786464 | tf_op jit(solution)/shard_map/ppermute | solution.py:367
  78.7 4.0 %collective-permute-start.9 = (bf16[3072,128]{1,0:T(8,128)(2,1)S(1)}, bf16[3072,128]{1,0:T(8,128)(2,1)S(1)}, u32[]{:S(2)}, u32[]{:S(2)}) collective-permute-start(bf16[3072,128]{1,0:T(8,128)(2,1)S(1)} %collective-permute-done.6.refs_5_), channel_id=1, source_target_pairs={{0,4},{4,8},{8,12},{12,0},{16,28},{20,16},{24,20},{28,24},{1,5},{5... | collective-permute-start | bytes 2359304 | tf_op jit(solution)/shard_map/ppermute | solution.py:367
  83.7 2.9 %collective-permute-done.7.refs_6_ = bf16[3072,128]{1,0:T(8,128)(2,1)S(1)} collective-permute-done((bf16[3072,128]{1,0:T(8,128)(2,1)S(1)}, bf16[3072,128]{1,0:T(8,128)(2,1)S(1)}, u32[]{:S(2)}, u32[]{:S(2)}) %collective-permute-start.7) | collective-permute-done | bytes 786464 | tf_op jit(solution)/shard_map/ppermute | solution.py:367
  86.7 2.0 %shard_map.75 = (f32[4,3,64,128]{3,2,1,0:T(8,128)S(1)}, f32[4,3,64,128]{3,2,1,0:T(8,128)S(1)}) custom-call(s32[4]{0:T(128)S(1)} %pad_add_fusion.place_ref, bf16[3072,128]{1,0:T(8,128)(2,1)S(1)} %shard_map.73.refs_0_, bf16[3072,128]{1,0:T(8,128)(2,1)S(1)} %collective-permute-done.3.refs_1_, bf16[3072,128]{1,0:T(8,128)(2,1)S(1)} %collective-permute-done.4.refs_2_, ...), custom_call_target="tpu_custom_call" | custom-call | flops 1200000000 | bytes 6000000 | tf_op jit(solution)/shard_map/pallas_call | solution.py:310
  88.7 1.9 %collective-permute-start.8 = (f32[4,3,64,128]{3,2,1,0:T(8,128)S(1)}, f32[4,3,64,128]{3,2,1,0:T(8,128)S(1)}, u32[]{:S(2)}, u32[]{:S(2)}) collective-permute-start(f32[4,3,64,128]{3,2,1,0:T(8,128)S(1)} %get-tuple-element.17), channel_id=1, source_target_pairs={{0,16},{16,0},{1,17},{17,1},{2,18},{18,2},{3,19},{19,3},{4,20},{20... | collective-permute-start | bytes 1179656 | tf_op jit(solution)/shard_map/ppermute | solution.py:468
  90.7 4.0 %collective-permute-done.9.refs_4_ = bf16[3072,128]{1,0:T(8,128)(2,1)S(1)} collective-permute-done((bf16[3072,128]{1,0:T(8,128)(2,1)S(1)}, bf16[3072,128]{1,0:T(8,128)(2,1)S(1)}, u32[]{:S(2)}, u32[]{:S(2)}) %collective-permute-start.9) | collective-permute-done | bytes 786464 | tf_op jit(solution)/shard_map/ppermute | solution.py:367
  99.8 2.0 %collective-permute-start.12 = (f32[4,64,128]{2,1,0:T(8,128)S(1)}, f32[4,64,128]{2,1,0:T(8,128)S(1)}, u32[]{:S(2)}, u32[]{:S(2)}) collective-permute-start(f32[4,64,128]{2,1,0:T(8,128)S(1)} %shard_map.79), channel_id=1, source_target_pairs={{0,32},{32,64},{64,96},{96,0},{1,33},{33,65},{65,97},{97,1},{2,34}... | collective-permute-start | bytes 393224 | tf_op jit(solution)/shard_map/ppermute | solution.py:355
  101.9 4.0 %collective-permute-done.11.arrived_ref.first_ref = f32[3,64,128]{2,1,0:T(8,128)S(1)} collective-permute-done((f32[3,64,128]{2,1,0:T(8,128)S(1)}, f32[3,64,128]{2,1,0:T(8,128)S(1)}, u32[]{:S(2)}, u32[]{:S(2)}) %collective-permute-start.11) | collective-permute-done | bytes 98336 | tf_op jit(solution)/shard_map/ppermute | solution.py:355
  105.9 3.7 %collective-permute-start.13 = (f32[4,64,128]{2,1,0:T(8,128)S(1)}, f32[4,64,128]{2,1,0:T(8,128)S(1)}, u32[]{:S(2)}, u32[]{:S(2)}) collective-permute-start(f32[4,64,128]{2,1,0:T(8,128)S(1)} %get-tuple-element.21), channel_id=1, source_target_pairs={{0,96},{32,0},{64,32},{96,64},{1,97},{33,1},{65,33},{97,65},{2,98}... | collective-permute-start | bytes 393224 | tf_op jit(solution)/shard_map/ppermute | solution.py:355
  111.5 4.8 %collective-permute-done.14.last_ref = f32[1,64,128]{2,1,0:T(8,128)S(1)} collective-permute-done((f32[1,64,128]{2,1,0:T(8,128)S(1)}, f32[1,64,128]{2,1,0:T(8,128)S(1)}, u32[]{:S(2)}, u32[]{:S(2)}) %collective-permute-start.14) | collective-permute-done | bytes 32800 | tf_op jit(solution)/shard_map/ppermute | solution.py:355
  116.9 17.5 %all_to_all.16.parts_ref = f32[4,64,128]{2,1,0:T(8,128)S(1)} all-to-all(f32[4,64,128]{2,1,0:T(8,128)S(1)} %shard_map.80), channel_id=1, replica_groups=mesh['zh'=4,'zl'=4,'core'=2,'y'=4,'x'=4] {'zh'}, dimensions={0} | all-to-all | bytes 262144 | tf_op jit(solution)/shard_map/all_to_all | solution.py:504
  134.4 6.4 %collective-permute-start.15 = (f32[64,128]{1,0:T(8,128)S(1)}, f32[64,128]{1,0:T(8,128)S(1)}, u32[]{:S(2)}, u32[]{:S(2)}) collective-permute-start(f32[64,128]{1,0:T(8,128)S(1)} %shard_map.81), channel_id=1, source_target_pairs={{0,0},{1,32},{2,64},{3,96},{32,1},{33,33},{34,65},{35,97},{64,2},{... | collective-permute-start | bytes 98312 | tf_op jit(solution)/shard_map/ppermute | solution.py:379
  140.9 3.3 %collective-permute-done.15 = f32[64,128]{1,0:T(8,128)S(1)} collective-permute-done((f32[64,128]{1,0:T(8,128)S(1)}, f32[64,128]{1,0:T(8,128)S(1)}, u32[]{:S(2)}, u32[]{:S(2)}) %collective-permute-start.15) | collective-permute-done | bytes 32800 | tf_op jit(solution)/shard_map/ppermute | solution.py:379
  (40 shorter events, 22.9 us)
Async XLA Ops:
  0.6 1.4 copy-start
  2.0 29.6 %copy-start.1 = (f32[3,8,16,8,128]{4,3,2,1,0:T(8,128)S(1)}, f32[3,8,16,8,128]{4,3,2,1,0:T(8,128)}, u32[]{:S(2)}) copy-start(f32[3,8,16,8,128]{4,3,2,1,0:T(8,128)} %x_ref.3) | copy-start | bytes 4718596
  2.0 34.8 %copy-start.2 = (f32[3,3,8,16,8]{3,4,2,1,0:T(8,128)S(1)}, f32[3,3,8,16,8]{3,4,2,1,0:T(8,128)}, u32[]{:S(2)}) copy-start(f32[3,3,8,16,8]{3,4,2,1,0:T(8,128)} %param.6) | copy-start | bytes 110596
  2.0 34.8 %copy-start.3 = (f32[3,8,16,8]{2,3,1,0:T(8,128)S(1)}, f32[3,8,16,8]{2,3,1,0:T(8,128)}, u32[]{:S(2)}) copy-start(f32[3,8,16,8]{2,3,1,0:T(8,128)} %param.5) | copy-start | bytes 36868
  2.0 34.8 %copy-start.4 = (f32[8,16,8]{1,2,0:T(8,128)S(1)}, f32[8,16,8]{1,2,0:T(8,128)}, u32[]{:S(2)}) copy-start(f32[8,16,8]{1,2,0:T(8,128)} %param.7) | copy-start | bytes 12292
  3.0 3.1 %collective-permute-start = (f32[72,128]{1,0:T(8,128)S(1)}, f32[72,128]{1,0:T(8,128)S(1)}, u32[]{:S(2)}, u32[]{:S(2)}) collective-permute-start(f32[72,128]{1,0:T(8,128)S(1)} %shard_map.67.a_ref), channel_id=1, source_target_pairs={{0,16},{16,0},{1,17},{17,1},{2,18},{18,2},{3,19},{19,3},{4,20},{20... | collective-permute-start | bytes 110600 | tf_op jit(solution)/shard_map/ppermute | solution.py:409
  19.3 27.9 %all-to-all-start.1 = ((f32[4,72,128]{2,1,0:T(8,128)}), f32[4,72,128]{2,1,0:T(8,128)S(1)}, u32[]{:S(2)}, u32[]{:S(2)}) async-start(f32[4,72,128]{2,1,0:T(8,128)} %shard_map.69), calls=%async_computation.1 | async-start | bytes 294912 | tf_op jit(solution)/shard_map/all_to_all | solution.py:413
  32.4 6.9 %collective-permute-start.2 = (f32[3,1,16,8,128]{4,3,2,1,0:T(8,128)}, f32[3,1,16,8,128]{4,3,2,1,0:T(8,128)S(1)}, u32[]{:S(2)}, u32[]{:S(2)}) collective-permute-start(f32[3,1,16,8,128]{4,3,2,1,0:T(8,128)} %get-tuple-element.25), channel_id=1, source_target_pairs={{16,0},{32,16},{48,32},{64,48},{80,64},{96,80},{112,96},{128,112},... | collective-permute-start | bytes 589832 | tf_op jit(solution)/shard_map/ppermute | solution.py:389
  33.7 5.6 %collective-permute-start.1 = (f32[3,1,16,8,128]{4,3,2,1,0:T(8,128)S(1)}, f32[3,1,16,8,128]{4,3,2,1,0:T(8,128)S(1)}, u32[]{:S(2)}, u32[]{:S(2)}) collective-permute-start(f32[3,1,16,8,128]{4,3,2,1,0:T(8,128)S(1)} %get-tuple-element.26), channel_id=1, source_target_pairs={{0,16},{16,32},{32,48},{48,64},{64,80},{80,96},{96,112},{112,128},... | collective-permute-start | bytes 589832 | tf_op jit(solution)/shard_map/ppermute | solution.py:388
  53.7 19.2 %collective-permute-start.3 = (bf16[3072,128]{1,0:T(8,128)(2,1)S(1)}, bf16[3072,128]{1,0:T(8,128)(2,1)S(1)}, u32[]{:S(2)}, u32[]{:S(2)}) collective-permute-start(bf16[3072,128]{1,0:T(8,128)(2,1)S(1)} %shard_map.73.refs_0_), channel_id=1, source_target_pairs={{0,1},{1,2},{2,3},{3,0},{16,19},{17,16},{18,17},{19,18},{4,5},{5,6... | collective-permute-start | bytes 2359304 | tf_op jit(solution)/shard_map/ppermute | solution.py:367
  58.0 20.7 %collective-permute-start.6 = (bf16[3072,128]{1,0:T(8,128)(2,1)S(1)}, bf16[3072,128]{1,0:T(8,128)(2,1)S(1)}, u32[]{:S(2)}, u32[]{:S(2)}) collective-permute-start(bf16[3072,128]{1,0:T(8,128)(2,1)S(1)} %get-tuple-element.15.refs_4_), channel_id=1, source_target_pairs={{0,4},{4,8},{8,12},{12,0},{16,28},{20,16},{24,20},{28,24},{1,5},{5... | collective-permute-start | bytes 2359304 | tf_op jit(solution)/shard_map/ppermute | solution.py:367
  61.5 22.2 %collective-permute-start.4 = (bf16[3072,128]{1,0:T(8,128)(2,1)S(1)}, bf16[3072,128]{1,0:T(8,128)(2,1)S(1)}, u32[]{:S(2)}, u32[]{:S(2)}) collective-permute-start(bf16[3072,128]{1,0:T(8,128)(2,1)S(1)} %shard_map.73.refs_0_), channel_id=1, source_target_pairs={{1,0},{2,1},{3,2},{0,3},{19,16},{16,17},{17,18},{18,19},{5,4},{6,5... | collective-permute-start | bytes 2359304 | tf_op jit(solution)/shard_map/ppermute | solution.py:367
  64.9 21.7 %collective-permute-start.7 = (bf16[3072,128]{1,0:T(8,128)(2,1)S(1)}, bf16[3072,128]{1,0:T(8,128)(2,1)S(1)}, u32[]{:S(2)}, u32[]{:S(2)}) collective-permute-start(bf16[3072,128]{1,0:T(8,128)(2,1)S(1)} %get-tuple-element.15.refs_4_), channel_id=1, source_target_pairs={{4,0},{8,4},{12,8},{0,12},{28,16},{16,20},{20,24},{24,28},{5,1},{9... | collective-permute-start | bytes 2359304 | tf_op jit(solution)/shard_map/ppermute | solution.py:367
  72.8 13.9 %collective-permute-start.5 = (bf16[3072,128]{1,0:T(8,128)(2,1)S(1)}, bf16[3072,128]{1,0:T(8,128)(2,1)S(1)}, u32[]{:S(2)}, u32[]{:S(2)}) collective-permute-start(bf16[3072,128]{1,0:T(8,128)(2,1)S(1)} %collective-permute-done.3.refs_1_), channel_id=1, source_target_pairs={{0,1},{1,2},{2,3},{3,0},{16,19},{17,16},{18,17},{19,18},{4,5},{5,6... | collective-permute-start | bytes 2359304 | tf_op jit(solution)/shard_map/ppermute | solution.py:367
  78.7 16.0 %collective-permute-start.9 = (bf16[3072,128]{1,0:T(8,128)(2,1)S(1)}, bf16[3072,128]{1,0:T(8,128)(2,1)S(1)}, u32[]{:S(2)}, u32[]{:S(2)}) collective-permute-start(bf16[3072,128]{1,0:T(8,128)(2,1)S(1)} %collective-permute-done.6.refs_5_), channel_id=1, source_target_pairs={{0,4},{4,8},{8,12},{12,0},{16,28},{20,16},{24,20},{28,24},{1,5},{5... | collective-permute-start | bytes 2359304 | tf_op jit(solution)/shard_map/ppermute | solution.py:367
  88.7 9.1 %collective-permute-start.8 = (f32[4,3,64,128]{3,2,1,0:T(8,128)S(1)}, f32[4,3,64,128]{3,2,1,0:T(8,128)S(1)}, u32[]{:S(2)}, u32[]{:S(2)}) collective-permute-start(f32[4,3,64,128]{3,2,1,0:T(8,128)S(1)} %get-tuple-element.17), channel_id=1, source_target_pairs={{0,16},{16,0},{1,17},{17,1},{2,18},{18,2},{3,19},{19,3},{4,20},{20... | collective-permute-start | bytes 1179656 | tf_op jit(solution)/shard_map/ppermute | solution.py:468
  95.9 3.9 %collective-permute-start.10 = (f32[4,1,64,128]{3,2,1,0:T(8,128)S(1)}, f32[4,1,64,128]{3,2,1,0:T(8,128)S(1)}, u32[]{:S(2)}, u32[]{:S(2)}) collective-permute-start(f32[4,1,64,128]{3,2,1,0:T(8,128)S(1)} %get-tuple-element.19.last_ref), channel_id=1, source_target_pairs={{0,16},{16,0},{1,17},{17,1},{2,18},{18,2},{3,19},{19,3},{4,20},{20... | collective-permute-start | bytes 393224 | tf_op jit(solution)/shard_map/ppermute | solution.py:470
  97.8 8.0 %collective-permute-start.11 = (f32[3,64,128]{2,1,0:T(8,128)S(1)}, f32[3,64,128]{2,1,0:T(8,128)S(1)}, u32[]{:S(2)}, u32[]{:S(2)}) collective-permute-start(f32[3,64,128]{2,1,0:T(8,128)S(1)} %shard_map.77.ahead_ref), channel_id=1, source_target_pairs={{0,64},{32,96},{64,0},{96,32},{1,65},{33,97},{65,1},{97,33},{2,66}... | collective-permute-start | bytes 294920 | tf_op jit(solution)/shard_map/ppermute | solution.py:355
  99.8 16.5 %collective-permute-start.12 = (f32[4,64,128]{2,1,0:T(8,128)S(1)}, f32[4,64,128]{2,1,0:T(8,128)S(1)}, u32[]{:S(2)}, u32[]{:S(2)}) collective-permute-start(f32[4,64,128]{2,1,0:T(8,128)S(1)} %shard_map.79), channel_id=1, source_target_pairs={{0,32},{32,64},{64,96},{96,0},{1,33},{33,65},{65,97},{97,1},{2,34}... | collective-permute-start | bytes 393224 | tf_op jit(solution)/shard_map/ppermute | solution.py:355
  105.9 10.4 %collective-permute-start.13 = (f32[4,64,128]{2,1,0:T(8,128)S(1)}, f32[4,64,128]{2,1,0:T(8,128)S(1)}, u32[]{:S(2)}, u32[]{:S(2)}) collective-permute-start(f32[4,64,128]{2,1,0:T(8,128)S(1)} %get-tuple-element.21), channel_id=1, source_target_pairs={{0,96},{32,0},{64,32},{96,64},{1,97},{33,1},{65,33},{97,65},{2,98}... | collective-permute-start | bytes 393224 | tf_op jit(solution)/shard_map/ppermute | solution.py:355
  109.6 6.7 %collective-permute-start.14 = (f32[1,64,128]{2,1,0:T(8,128)S(1)}, f32[1,64,128]{2,1,0:T(8,128)S(1)}, u32[]{:S(2)}, u32[]{:S(2)}) collective-permute-start(f32[1,64,128]{2,1,0:T(8,128)S(1)} %get-tuple-element.22), channel_id=1, source_target_pairs={{0,64},{32,96},{64,0},{96,32},{1,65},{33,97},{65,1},{97,33},{2,66}... | collective-permute-start | bytes 98312 | tf_op jit(solution)/shard_map/ppermute | solution.py:355
  134.4 9.7 %collective-permute-start.15 = (f32[64,128]{1,0:T(8,128)S(1)}, f32[64,128]{1,0:T(8,128)S(1)}, u32[]{:S(2)}, u32[]{:S(2)}) collective-permute-start(f32[64,128]{1,0:T(8,128)S(1)} %shard_map.81), channel_id=1, source_target_pairs={{0,0},{1,32},{2,64},{3,96},{32,1},{33,33},{34,65},{35,97},{64,2},{... | collective-permute-start | bytes 98312 | tf_op jit(solution)/shard_map/ppermute | solution.py:379
